TPU v7x, 32 devices: a whole 2x2x4 slice. The times are simulated.
32 devices in a mesh: dp: 2 (over core), row: 4 (over y, x), col: 4 (over z).
Axes of the slice: x: 2, y: 2, z: 4, core: 2. Of those that a mesh axis runs over, the one named last changes fastest.
Arguments:
- block_input: bfloat16 [16384, 768], P(('dp', 'col', 'row')), may hold values from -6 to 6
- out_grad: bfloat16 [16384, 768], P(('dp', 'col', 'row')), may hold values from -6 to 6
- lengths: int32 [8, 2], P(('dp', 'col')), may hold values from 256 to 1024, as said below
- w_qkv: float32 [3, 768, 768], P(None, 'col', 'row'), may hold values from -0.21875 to 0.21875
- w_out: float32 [768, 768], P('row', 'col'), may hold values from -3.5 to 3.5
- w_gate_up: float32 [2, 768, 2048], P(None, 'col', 'row'), may hold values from -0.21875 to 0.21875
- w_down: float32 [2048, 768], P('row', 'col'), may hold values from -0.125 to 0.125
- gains: float32 [2, 768], replicated, may hold values from 0.5 to 1.5
- mom_qkv: float32 [3, 768, 768], P(None, 'col', 'row'), may hold values from -0.0015033532 to 0.0015033532
- mom_out: float32 [768, 768], P('row', 'col'), may hold values from -0.0015033532 to 0.0015033532
- mom_gate_up: float32 [2, 768, 2048], P(None, 'col', 'row'), may hold values from -0.0015033532 to 0.0015033532
- mom_down: float32 [2048, 768], P('row', 'col'), may hold values from -0.0015033532 to 0.0015033532
- mom_gains: float32 [2, 768], replicated, may hold values from -0.006013413 to 0.006013413
- ema_qkv: float32 [3, 768, 768], P(None, 'col', 'row'), may hold values from -0.21875 to 0.21875
- ema_out: float32 [768, 768], P('row', 'col'), may hold values from -3.5 to 3.5
- ema_gate_up: float32 [2, 768, 2048], P(None, 'col', 'row'), may hold values from -0.21875 to 0.21875
- ema_down: float32 [2048, 768], P('row', 'col'), may hold values from -0.125 to 0.125
- ema_gains: float32 [2, 768], replicated, may hold values from 0.5 to 1.5
Outputs:
- output: float32 [16384, 768], P(('dp', 'col', 'row'))
- input_grad: float32 [16384, 768], P(('dp', 'col', 'row'))
- grad_norm: float32 [], replicated
- new_mom_qkv: float32 [3, 768, 768], P(None, 'col', 'row')
- new_mom_out: float32 [768, 768], P('row', 'col')
- new_mom_gate_up: float32 [2, 768, 2048], P(None, 'col', 'row')
- new_mom_down: float32 [2048, 768], P('row', 'col')
- new_mom_gains: float32 [2, 768], replicated
- new_w_qkv: float32 [3, 768, 768], P(None, 'col', 'row')
- new_w_out: float32 [768, 768], P('row', 'col')
- new_w_gate_up: float32 [2, 768, 2048], P(None, 'col', 'row')
- new_w_down: float32 [2048, 768], P('row', 'col')
- new_gains: float32 [2, 768], replicated
- new_ema_qkv: float32 [3, 768, 768], P(None, 'col', 'row')
- new_ema_out: float32 [768, 768], P('row', 'col')
- new_ema_gate_up: float32 [2, 768, 2048], P(None, 'col', 'row')
- new_ema_down: float32 [2048, 768], P('row', 'col')
- new_ema_gains: float32 [2, 768], replicated
Inputs may be any that keep to these rules, and one draw needn't show every extreme that they name: `lengths`: each sequence's real tokens fill its first slots; the rest are padding. Some sequence is full.
All inputs are finite; a program needn't handle non-finite values.
Results may differ from a plain program's by a relative error of at most 0.02.
Values may be sent and summed in bfloat16 or wider, within the bound.
No kernel may reach another device: no remote copies, remote signals or barrier semaphores. Data moves between devices by JAX's collectives and lax.ppermute only.
A program may use at most 192 MiB of HBM per device.

v0:
```python
import jax
import jax.numpy as jnp
from jax import lax
from jax.sharding import PartitionSpec as P

D = 768
HD = 64
LEN = 1024


EPSILON = 1e-06
THETA = 10000.0
MOMENTUM = 0.9
RATE = 300.0
DECAY = 0.6
CLIP = 1.0
NEGATIVE = -1e30


def rope_tables():
    half_dim = HD // 2
    freqs = THETA ** (-(jnp.arange(half_dim, dtype=jnp.float32) * 2.0) / HD)
    angles = jnp.arange(LEN, dtype=jnp.float32)[:, None] * freqs[None, :]
    return (jnp.cos(angles), jnp.sin(angles))


def rotate(tensor, cosine, sine_table):
    half_dim = HD // 2
    first_half = tensor[..., :half_dim]
    second = tensor[..., half_dim:]
    cos_b = cosine[None, :, None, :]
    sin_b = sine_table[None, :, None, :]
    return jnp.concatenate(
        [first_half * cos_b - second * sin_b, first_half * sin_b + second * cos_b], -1
    )


def unrotate(tensor, cosine, sine_table):
    half_dim = HD // 2
    first_half = tensor[..., :half_dim]
    second = tensor[..., half_dim:]
    cos_b = cosine[None, :, None, :]
    sin_b = sine_table[None, :, None, :]
    return jnp.concatenate(
        [first_half * cos_b + second * sin_b, second * cos_b - first_half * sin_b], -1
    )


def gather_weights(w_qkv, w_out, w_gate_up, w_down):
    return (
        lax.all_gather(w_qkv.astype(jnp.bfloat16), "col", axis=1, tiled=True),
        lax.all_gather(w_out.astype(jnp.bfloat16), "col", axis=1, tiled=True),
        lax.all_gather(w_gate_up.astype(jnp.bfloat16), "col", axis=1, tiled=True),
        lax.all_gather(w_down.astype(jnp.bfloat16), "col", axis=1, tiled=True),
    )


def gather_rows(operand):
    return lax.all_gather(operand, "row", axis=0, tiled=True)


def sum_rows(partial_value):
    return lax.psum_scatter(
        partial_value.astype(jnp.bfloat16), "row", scatter_dimension=0, tiled=True
    ).astype(jnp.float32)


def gather_grads(operand):
    return lax.all_gather(operand, "row", axis=0, tiled=True)


def sum_grads(partial_value):
    return lax.psum_scatter(
        partial_value.astype(jnp.bfloat16), "row", scatter_dimension=0, tiled=True
    ).astype(jnp.float32)


def block_mask(row_start, block_rows, length_now):
    key_pos = jnp.arange(LEN, dtype=jnp.int32)
    query_pos = row_start + jnp.arange(block_rows, dtype=jnp.int32)
    return (key_pos[None, :] <= query_pos[:, None]) & (key_pos[None, :] < length_now)


def attend_forward(queries, keys_rot, values, seq_lengths):
    seq_count = queries.shape[0]
    heads_here = queries.shape[2]
    block_rows = min(512, LEN)
    blocks = LEN // block_rows
    score_scale = HD ** (-0.5)

    def one_block(flat_id):
        seq_id = flat_id // blocks
        row_start = flat_id % blocks * block_rows
        query_seq = lax.dynamic_index_in_dim(queries, seq_id, 0, keepdims=False)
        query_blk = lax.dynamic_slice_in_dim(query_seq, row_start, block_rows, 0)
        key_seq = lax.dynamic_index_in_dim(keys_rot, seq_id, 0, keepdims=False)
        value_seq = lax.dynamic_index_in_dim(values, seq_id, 0, keepdims=False)
        length_now = lax.dynamic_index_in_dim(seq_lengths, seq_id, 0, keepdims=False)
        live_mask = block_mask(row_start, block_rows, length_now)
        scores = (
            jnp.einsum("qhd,khd->hqk", query_blk, key_seq, preferred_element_type=jnp.float32)
            * score_scale
        )
        scores = jnp.where(live_mask[None], scores, NEGATIVE)
        row_max = jnp.max(scores, -1, keepdims=True)
        exp_scores = jnp.exp(scores - row_max)
        exp_total = jnp.sum(exp_scores, -1, keepdims=True)
        softmax_w = (exp_scores / exp_total).astype(jnp.bfloat16)
        attended = jnp.einsum(
            "hqk,khd->qhd", softmax_w, value_seq, preferred_element_type=jnp.float32
        )
        return (attended, (row_max + jnp.log(exp_total))[..., 0])

    attended, log_totals = lax.map(one_block, jnp.arange(seq_count * blocks, dtype=jnp.int32))
    attended = attended.reshape(seq_count, LEN, heads_here, HD)
    log_totals = (
        log_totals.reshape(seq_count, blocks, heads_here, block_rows)
        .transpose(0, 2, 1, 3)
        .reshape(seq_count, heads_here, LEN)
    )
    return (attended, log_totals)


def attend_backward(queries, keys_rot, values, grad_att, log_totals, seq_lengths):
    seq_count = queries.shape[0]
    heads_here = queries.shape[2]
    block_rows = min(512, LEN)
    blocks = LEN // block_rows
    score_scale = HD ** (-0.5)

    def one_seq(seq_id):
        query_seq = lax.dynamic_index_in_dim(queries, seq_id, 0, keepdims=False)
        key_seq = lax.dynamic_index_in_dim(keys_rot, seq_id, 0, keepdims=False)
        value_seq = lax.dynamic_index_in_dim(values, seq_id, 0, keepdims=False)
        grad_seq = lax.dynamic_index_in_dim(grad_att, seq_id, 0, keepdims=False)
        lse_seq = lax.dynamic_index_in_dim(log_totals, seq_id, 0, keepdims=False)
        length_now = lax.dynamic_index_in_dim(seq_lengths, seq_id, 0, keepdims=False)
        grad_keys = jnp.zeros((LEN, heads_here, HD), jnp.float32)
        grad_values = jnp.zeros((LEN, heads_here, HD), jnp.float32)
        query_parts = []
        for block_id in range(blocks):
            row_start = block_id * block_rows
            query_blk = query_seq[row_start : row_start + block_rows]
            grad_blk = grad_seq[row_start : row_start + block_rows]
            lse_blk = lse_seq[:, row_start : row_start + block_rows]
            live_mask = block_mask(row_start, block_rows, length_now)
            scores = (
                jnp.einsum("qhd,khd->hqk", query_blk, key_seq, preferred_element_type=jnp.float32)
                * score_scale
            )
            scores = jnp.where(live_mask[None], scores, NEGATIVE)
            softmax_w = jnp.exp(scores - lse_blk[:, :, None])
            grad_values = grad_values + jnp.einsum(
                "hqk,qhd->khd",
                softmax_w.astype(jnp.bfloat16),
                grad_blk,
                preferred_element_type=jnp.float32,
            )
            grad_probs = jnp.einsum(
                "qhd,khd->hqk", grad_blk, value_seq, preferred_element_type=jnp.float32
            )
            row_inner = jnp.sum(softmax_w * grad_probs, -1, keepdims=True)
            grad_scores = (score_scale * (softmax_w * (grad_probs - row_inner))).astype(
                jnp.bfloat16
            )
            query_parts.append(
                jnp.einsum("hqk,khd->qhd", grad_scores, key_seq, preferred_element_type=jnp.float32)
            )
            grad_keys = grad_keys + jnp.einsum(
                "hqk,qhd->khd", grad_scores, query_blk, preferred_element_type=jnp.float32
            )
        return (jnp.concatenate(query_parts, 0), grad_keys, grad_values)

    return lax.map(one_seq, jnp.arange(seq_count, dtype=jnp.int32))


def update(grad_full, moment, weight, average, factor):
    clipped = grad_full * factor
    new_moment = MOMENTUM * moment + clipped
    new_weight = weight - RATE * (clipped + MOMENTUM * new_moment)
    new_average = DECAY * average + (1.0 - DECAY) * new_weight
    return (new_moment, new_weight, new_average)


def body(
    block_input,
    out_grad,
    lengths,
    w_qkv,
    w_out,
    w_gate_up,
    w_down,
    gains,
    mom_qkv,
    mom_out,
    mom_gate_up,
    mom_down,
    mom_gains,
    ema_qkv,
    ema_out,
    ema_gate_up,
    ema_down,
    ema_gains,
):
    local_rows = block_input.shape[0]
    seq_lengths = lengths[0]
    seq_total = seq_lengths.shape[0]
    cosine, sine_table = rope_tables()
    full_qkv, full_out, full_gate_up, full_down = gather_weights(w_qkv, w_out, w_gate_up, w_down)
    inputs = block_input.astype(jnp.float32)
    gathered_x = gather_rows(block_input)
    group_rows = gathered_x.shape[0]
    seq_count = group_rows // LEN
    width_here = full_qkv.shape[2]
    heads_here = width_here // HD
    qkv = jnp.einsum("td,kde->kte", gathered_x, full_qkv, preferred_element_type=jnp.float32)
    queries = rotate(qkv[0].reshape(seq_count, LEN, heads_here, HD), cosine, sine_table).astype(
        jnp.bfloat16
    )
    keys_rot = rotate(qkv[1].reshape(seq_count, LEN, heads_here, HD), cosine, sine_table).astype(
        jnp.bfloat16
    )
    values = qkv[2].reshape(seq_count, LEN, heads_here, HD).astype(jnp.bfloat16)
    attended, log_totals = attend_forward(queries, keys_rot, values, seq_lengths)
    attended_b = attended.reshape(group_rows, width_here).astype(jnp.bfloat16)
    branch = sum_rows(jnp.dot(attended_b, full_out, preferred_element_type=jnp.float32))
    residual = inputs + branch
    scale_one = lax.rsqrt(jnp.mean(residual * residual, -1, keepdims=True) + EPSILON)
    normed = residual * scale_one * gains[0]
    gathered_y = gather_rows(normed.astype(jnp.bfloat16))
    gate_up = jnp.einsum(
        "td,kde->kte", gathered_y, full_gate_up, preferred_element_type=jnp.float32
    )
    gate_act = gate_up[0]
    up_act = gate_up[1]
    sigmoid_g = jax.nn.sigmoid(gate_act)
    silu_g = gate_act * sigmoid_g
    hidden_b = (silu_g * up_act).astype(jnp.bfloat16)
    ffn_out = sum_rows(jnp.dot(hidden_b, full_down, preferred_element_type=jnp.float32))
    summed = normed + ffn_out
    scale_two = lax.rsqrt(jnp.mean(summed * summed, -1, keepdims=True) + EPSILON)
    output = summed * scale_two * gains[1]
    full_qkv, full_out, full_gate_up, full_down = gather_weights(w_qkv, w_out, w_gate_up, w_down)
    slot_ids = lax.axis_index("row") * local_rows + jnp.arange(local_rows, dtype=jnp.int32)
    seq_of = slot_ids // LEN
    pos_of = slot_ids % LEN
    seq_match = seq_of[:, None] == jnp.arange(seq_total, dtype=jnp.int32)[None, :]
    length_of = jnp.sum(jnp.where(seq_match, seq_lengths[None, :], 0), 1)
    row_live = (pos_of < length_of).astype(jnp.float32)[:, None]
    cot_live = out_grad.astype(jnp.float32) * row_live
    grad_gain_two = jnp.sum(cot_live * summed * scale_two, 0)
    hat_two = cot_live * gains[1]
    inner_two = jnp.sum(hat_two * summed, -1, keepdims=True)
    d_summed = scale_two * (hat_two - summed * scale_two * scale_two * inner_two / D)
    grad_ffn_full = gather_grads(d_summed.astype(jnp.bfloat16))
    d_down = jnp.einsum("tf,td->fd", hidden_b, grad_ffn_full, preferred_element_type=jnp.float32)
    d_hidden = jnp.einsum("td,fd->tf", grad_ffn_full, full_down, preferred_element_type=jnp.float32)
    d_gate = d_hidden * up_act * (sigmoid_g * (1.0 + gate_act * (1.0 - sigmoid_g)))
    d_up = d_hidden * silu_g
    grad_gu_b = jnp.stack([d_gate, d_up]).astype(jnp.bfloat16)
    d_gate_up = jnp.einsum("td,ktf->kdf", gathered_y, grad_gu_b, preferred_element_type=jnp.float32)
    d_normed = d_summed + sum_grads(
        jnp.einsum("ktf,kdf->td", grad_gu_b, full_gate_up, preferred_element_type=jnp.float32)
    )
    grad_gain_one = jnp.sum(d_normed * residual * scale_one, 0)
    hat_one = d_normed * gains[0]
    inner_one = jnp.sum(hat_one * residual, -1, keepdims=True)
    d_residual = scale_one * (hat_one - residual * scale_one * scale_one * inner_one / D)
    grad_attn_full = gather_grads(d_residual.astype(jnp.bfloat16))
    d_out_w = jnp.einsum(
        "te,td->ed", attended_b, grad_attn_full, preferred_element_type=jnp.float32
    )
    grad_att = jnp.einsum(
        "td,ed->te", grad_attn_full, full_out, preferred_element_type=jnp.float32
    ).astype(jnp.bfloat16)
    grad_att = grad_att.reshape(seq_count, LEN, heads_here, HD)
    grad_q, grad_k, grad_v = attend_backward(
        queries, keys_rot, values, grad_att, log_totals, seq_lengths
    )
    grad_q = unrotate(grad_q, cosine, sine_table).reshape(group_rows, width_here)
    grad_k = unrotate(grad_k, cosine, sine_table).reshape(group_rows, width_here)
    grad_qkv_b = jnp.stack([grad_q, grad_k, grad_v.reshape(group_rows, width_here)]).astype(
        jnp.bfloat16
    )
    d_qkv = jnp.einsum("td,kte->kde", gathered_x, grad_qkv_b, preferred_element_type=jnp.float32)
    input_grad = d_residual + sum_grads(
        jnp.einsum("kte,kde->td", grad_qkv_b, full_qkv, preferred_element_type=jnp.float32)
    )
    shard_grads = (
        lax.psum_scatter(d_qkv.astype(jnp.bfloat16), "col", scatter_dimension=1, tiled=True).astype(
            jnp.float32
        ),
        lax.psum_scatter(
            d_out_w.astype(jnp.bfloat16), "col", scatter_dimension=1, tiled=True
        ).astype(jnp.float32),
        lax.psum_scatter(
            d_gate_up.astype(jnp.bfloat16), "col", scatter_dimension=1, tiled=True
        ).astype(jnp.float32),
        lax.psum_scatter(
            d_down.astype(jnp.bfloat16), "col", scatter_dimension=1, tiled=True
        ).astype(jnp.float32),
    )
    reduced = (
        lax.psum(shard_grads[0].astype(jnp.bfloat16), "dp").astype(jnp.float32),
        lax.psum(shard_grads[1].astype(jnp.bfloat16), "dp").astype(jnp.float32),
        lax.psum(shard_grads[2].astype(jnp.bfloat16), "dp").astype(jnp.float32),
        lax.psum(shard_grads[3].astype(jnp.bfloat16), "dp").astype(jnp.float32),
    )
    gain_total = lax.psum(jnp.stack([grad_gain_one, grad_gain_two]), ("dp", "row", "col"))
    local_squares = sum((jnp.sum(g_arr * g_arr) for g_arr in reduced))
    first_device = (lax.axis_index("col") == 0) & (lax.axis_index("row") == 0)
    local_squares = local_squares + jnp.where(first_device, jnp.sum(gain_total * gain_total), 0.0)
    grad_norm = jnp.sqrt(lax.psum(local_squares, ("row", "col")))
    factor = jnp.minimum(1.0, CLIP / (grad_norm + 1e-06))
    grads_all = (reduced[0], reduced[1], reduced[2], reduced[3], gain_total)
    params = (w_qkv, w_out, w_gate_up, w_down, gains)
    moments = (mom_qkv, mom_out, mom_gate_up, mom_down, mom_gains)
    averages = (ema_qkv, ema_out, ema_gate_up, ema_down, ema_gains)
    results = [
        update(g_arr, m_arr, w_arr, e_arr, factor)
        for g_arr, m_arr, w_arr, e_arr in zip(grads_all, moments, params, averages)
    ]
    return (
        output,
        input_grad,
        grad_norm,
        results[0][0],
        results[1][0],
        results[2][0],
        results[3][0],
        results[4][0],
        results[0][1],
        results[1][1],
        results[2][1],
        results[3][1],
        results[4][1],
        results[0][2],
        results[1][2],
        results[2][2],
        results[3][2],
        results[4][2],
    )


def solution(mesh):
    in_specs = (
        P(("dp", "col", "row"), None),
        P(("dp", "col", "row"), None),
        P(("dp", "col"), None),
        P(None, "col", "row"),
        P("row", "col"),
        P(None, "col", "row"),
        P("row", "col"),
        P(),
        P(None, "col", "row"),
        P("row", "col"),
        P(None, "col", "row"),
        P("row", "col"),
        P(),
        P(None, "col", "row"),
        P("row", "col"),
        P(None, "col", "row"),
        P("row", "col"),
        P(),
    )
    out_specs = (
        P(("dp", "col", "row"), None),
        P(("dp", "col", "row"), None),
        P(),
        P(None, "col", "row"),
        P("row", "col"),
        P(None, "col", "row"),
        P("row", "col"),
        P(),
        P(None, "col", "row"),
        P("row", "col"),
        P(None, "col", "row"),
        P("row", "col"),
        P(),
        P(None, "col", "row"),
        P("row", "col"),
        P(None, "col", "row"),
        P("row", "col"),
        P(),
    )
    return jax.shard_map(body, mesh=mesh, in_specs=in_specs, out_specs=out_specs, check_vma=False)
```

profile of v0, /device:TPU:0, one launch (start us, length us, event | category | flops | bytes accessed | tf_op | source)
XLA Modules:
  0.0 813.9 jit_solution(5509820822577120183)
XLA Ops:
  11.2 16.3 %all_gather.30 = bf16[192,768]{0,1:T(8,128)(2,1)S(1)} all-gather(bf16[192,192]{0,1:T(8,128)(2,1)S(1)} %copy.160), channel_id=1, replica_groups=mesh['dp'=2,'row'=4,'col'=4] {'col'}, dimensions={1}, use_global_device_ids=true | all-gather | bytes 368640 | tf_op jit(solution)/shard_map/all_gather | solution.py:52
  28.8 28.5 %all_gather.28 = bf16[3,768,192]{2,0,1:T(4,128)(2,1)S(1)} all-gather(bf16[3,192,192]{2,0,1:T(4,128)(2,1)S(1)} %copy.152), channel_id=1, replica_groups=mesh['dp'=2,'row'=4,'col'=4] {'col'}, dimensions={1}, use_global_device_ids=true | all-gather | bytes 1105920 | tf_op jit(solution)/shard_map/all_gather | solution.py:51
  57.4 5.1 convolution_bitcast_fusion.1
  66.2 2.9 convert_element_type.141
  70.9 2.6 reshape_squeeze.7
  75.9 44.7 %while.29 = (s32[]{:T(128)}, bf16[4,512,3,64]{1,3,2,0:T(8,128)(2,1)}, f32[4,3,512]{2,1,0:T(4,128)}, s32[4]{0:T(128)S(1)}, bf16[2,1024,3,64]{1,3,2,0:T(8,128)(2,1...) while((s32[]{:T(128)}, ...), condition=%wide.region_3.4_spmd, body=%wide.region_0.3_spmd.sunk | while | flops 422576160 | bytes 28701224 | solution.py:114
  84.1 2.1 fusion.271
  95.3 2.1 fusion.271
  106.5 2.1 fusion.271
  117.7 2.1 fusion.271
  120.7 2.0 copy.159
  123.7 2.7 convolution_convert_fusion.1
  128.7 41.6 %reduce-scatter.12.cloned.1.call-done = bf16[512,768]{1,0:T(8,128)(2,1)} async-done(((bf16[2048,768]{1,0:T(8,128)(2,1)}), bf16[512,768]{1,0:T(8,128)(2,1)}) %reduce-scatter.12.cloned.1.call-update) | async-done | bytes 786448 | tf_op jit(solution)/shard_map/reduce_scatter | solution.py:63
  171.8 2.3 multiply_convert_fusion.5
  174.2 19.6 %all_gather.33 = bf16[512,768]{0,1:T(8,128)(2,1)S(1)} all-gather(bf16[512,192]{0,1:T(8,128)(2,1)S(1)} %convert_element_type.150), channel_id=1, replica_groups=mesh['dp'=2,'row'=4,'col'=4] {'col'}, dimensions={1}, use_global_device_ids=true | all-gather | bytes 983040 | tf_op jit(solution)/shard_map/all_gather | solution.py:54
  193.8 24.2 %all-gather.8.cloned.1.call-done = bf16[2048,768]{1,0:T(8,128)(2,1)} async-done(((bf16[512,768]{1,0:T(8,128)(2,1)}), bf16[2048,768]{1,0:T(8,128)(2,1)}) %all-gather.8.cloned.1.call-update) | async-done | bytes 3145744 | tf_op jit(solution)/shard_map/all_gather | solution.py:59
  218.0 5.9 convolution_bitcast_fusion
  228.6 3.6 convolution_convert_fusion
  232.3 43.8 %reduce-scatter.14.cloned.1.call-done = bf16[512,768]{1,0:T(8,128)(2,1)} async-done(((bf16[2048,768]{1,0:T(8,128)(2,1)}), bf16[512,768]{1,0:T(8,128)(2,1)}) %reduce-scatter.14.cloned.1.call-update) | async-done | bytes 786448 | tf_op jit(solution)/shard_map/reduce_scatter | solution.py:63
  279.2 2.5 fusion.216
  282.0 43.9 %all-gather.12.cloned.1.call-done = bf16[2048,768]{1,0:T(8,128)(2,1)} async-done(((bf16[512,768]{1,0:T(8,128)(2,1)}), bf16[2048,768]{1,0:T(8,128)(2,1)}) %all-gather.12.cloned.1.call-update) | async-done | bytes 3145744 | tf_op jit(solution)/shard_map/all_gather | solution.py:69
  325.9 8.1 fusion.162
  335.9 4.8 bitcast_convert_fusion.1
  340.8 43.9 %reduce-scatter.16.cloned.1.call-done = bf16[512,768]{1,0:T(8,128)(2,1)} async-done(((bf16[2048,768]{1,0:T(8,128)(2,1)}), bf16[512,768]{1,0:T(8,128)(2,1)}) %reduce-scatter.16.cloned.1.call-update) | async-done | bytes 786448 | tf_op jit(solution)/shard_map/reduce_scatter | solution.py:73
  384.7 3.0 multiply_reduce_fusion.3
  387.7 2.1 fusion.215
  391.3 6.7 fusion.167
  398.0 3.0 copy.170
  401.1 32.8 %all-gather.14.cloned.1.call-done = bf16[2048,768]{1,0:T(8,128)(2,1)} async-done(((bf16[512,768]{1,0:T(8,128)(2,1)}), bf16[2048,768]{1,0:T(8,128)(2,1)}) %all-gather.14.cloned.1.call-update) | async-done | bytes 3145744 | tf_op jit(solution)/shard_map/all_gather | solution.py:69
  433.9 4.0 convolution_convert_fusion.2
  437.9 2.6 reshape.309
  441.5 161.9 %while.30 = (s32[]{:T(128)}, f32[2,1024,3,64]{1,3,2,0:T(8,128)}, f32[2,1024,3,64]{1,3,2,0:T(8,128)}, bf16[2,1024,3,64]{1,3,2,0:T(8,128)(2,1)}, s32[2]{0:T(128)S(...) while((s32[]{:T(128)}, f32[2,1024,3,64]{1,3,2,0:T(8,128)}, ...), condition=%wide.region_15.16_spmd, body=%wide.region_12.15_spmd.sunk | while | flops 2097753600 | bytes 217222576 | solution.py:174
  449.1 3.1 copy-done
  456.9 3.6 fusion.289
  460.6 13.4 %fusion.291 = f32[512,3,64]{0,2,1:T(8,128)} fusion(f32[3,512,1024]{2,1,0:T(8,128)} %fusion.289, f32[3,512,1024]{2,1,0:T(8,128)} %copy-done.1, f32[3,512]{1,0:T(4,128)S(1)} %get-tuple-element.629, pred[512,1024]{1,0:T(8,128)(4,1)S(1)} %get-tuple-element.630, bf16[2,1024,3,64]{1,3,2,0:T(8,128)(2,1)S(1)} %get-tuple-element.708, s32[]{:T(128)S(6)} %select_n.226), kind=kOutput, calls=%fused_computation.71.clone.1 | convolution fusion | flops 218630656 | bytes 27017220 | tf_op jit(solution)/shard_map/while/body/eval_jaxpr/hqk,khd->qhd/dot_general | solution.py:167
  474.0 14.3 %fusion.293 = f32[3,64,1024]{2,1,0:T(8,128)} fusion(f32[3,512,1024]{2,1,0:T(8,128)} %fusion.289, f32[3,512,1024]{2,1,0:T(8,128)} %copy-done.1, f32[3,512]{1,0:T(4,128)S(1)} %get-tuple-element.629, pred[512,1024]{1,0:T(8,128)(4,1)S(1)} %get-tuple-element.630, bf16[2,1024,3,64]{1,3,2,0:T(8,128)(2,1)S(1)} %get-tuple-element.710, s32[]{:T(128)S(6)} %select_n.226), kind=kOutput, calls=%fused_computation.35.clone.1 | convolution fusion | flops 218630656 | bytes 27213828 | tf_op jit(solution)/shard_map/while/body/eval_jaxpr/hqk,qhd->khd/dot_general | solution.py:169
  488.2 4.6 fusion.284
  492.8 13.4 %fusion.288 = f32[512,3,64]{0,2,1:T(8,128)} fusion(f32[3,512,1024]{2,1,0:T(8,128)} %fusion.284, f32[3,512,1024]{2,1,0:T(8,128)} %copy-done, f32[3,512]{1,0:T(4,128)S(1)} %get-tuple-element.627, pred[512,1024]{1,0:T(8,128)(4,1)S(1)} %get-tuple-element.628, bf16[2,1024,3,64]{1,3,2,0:T(8,128)(2,1)S(1)} %get-tuple-element.708, s32[]{:T(128)S(6)} %select_n.226), kind=kOutput, calls=%fused_computation.70.clone.1 | convolution fusion | flops 218630656 | bytes 27017220 | tf_op jit(solution)/shard_map/while/body/eval_jaxpr/hqk,khd->qhd/dot_general | solution.py:167
  506.1 14.6 %fusion.294 = f32[2,1024,3,64]{1,3,2,0:T(8,128)} fusion(f32[2,1024,3,64]{1,3,2,0:T(8,128)} %get-tuple-element.690, s32[]{:T(128)S(6)} %copy.225, f32[3,64,1024]{2,1,0:T(8,128)} %fusion.293, f32[3,512,1024]{2,1,0:T(8,128)} %fusion.284, f32[3,512,1024]{2,1,0:T(8,128)} %copy-done, f32[3,512]{1,0:T(4,128)S(1)} %get-tuple-element.627, ...), kind=kOutput, calls=%fused_computation.66.clone.1 | convolution fusion | flops 218827264 | bytes 28000268 | tf_op jit(solution)/shard_map/while/body/eval_jaxpr/hqk,qhd->khd/dot_general | solution.py:169
  520.7 2.0 fusion.292
  529.9 3.1 copy-done
  534.9 1.9 fusion.296
  537.7 3.6 fusion.289
  541.3 13.4 %fusion.291 = f32[512,3,64]{0,2,1:T(8,128)} fusion(f32[3,512,1024]{2,1,0:T(8,128)} %fusion.289, f32[3,512,1024]{2,1,0:T(8,128)} %copy-done.1, f32[3,512]{1,0:T(4,128)S(1)} %get-tuple-element.629, pred[512,1024]{1,0:T(8,128)(4,1)S(1)} %get-tuple-element.630, bf16[2,1024,3,64]{1,3,2,0:T(8,128)(2,1)S(1)} %get-tuple-element.708, s32[]{:T(128)S(6)} %select_n.226), kind=kOutput, calls=%fused_computation.71.clone.1 | convolution fusion | flops 218630656 | bytes 27017220 | tf_op jit(solution)/shard_map/while/body/eval_jaxpr/hqk,khd->qhd/dot_general | solution.py:167
  554.7 14.3 %fusion.293 = f32[3,64,1024]{2,1,0:T(8,128)} fusion(f32[3,512,1024]{2,1,0:T(8,128)} %fusion.289, f32[3,512,1024]{2,1,0:T(8,128)} %copy-done.1, f32[3,512]{1,0:T(4,128)S(1)} %get-tuple-element.629, pred[512,1024]{1,0:T(8,128)(4,1)S(1)} %get-tuple-element.630, bf16[2,1024,3,64]{1,3,2,0:T(8,128)(2,1)S(1)} %get-tuple-element.710, s32[]{:T(128)S(6)} %select_n.226), kind=kOutput, calls=%fused_computation.35.clone.1 | convolution fusion | flops 218630656 | bytes 27213828 | tf_op jit(solution)/shard_map/while/body/eval_jaxpr/hqk,qhd->khd/dot_general | solution.py:169
  568.9 4.6 fusion.284
  573.5 13.4 %fusion.288 = f32[512,3,64]{0,2,1:T(8,128)} fusion(f32[3,512,1024]{2,1,0:T(8,128)} %fusion.284, f32[3,512,1024]{2,1,0:T(8,128)} %copy-done, f32[3,512]{1,0:T(4,128)S(1)} %get-tuple-element.627, pred[512,1024]{1,0:T(8,128)(4,1)S(1)} %get-tuple-element.628, bf16[2,1024,3,64]{1,3,2,0:T(8,128)(2,1)S(1)} %get-tuple-element.708, s32[]{:T(128)S(6)} %select_n.226), kind=kOutput, calls=%fused_computation.70.clone.1 | convolution fusion | flops 218630656 | bytes 27017220 | tf_op jit(solution)/shard_map/while/body/eval_jaxpr/hqk,khd->qhd/dot_general | solution.py:167
  586.9 14.5 %fusion.294 = f32[2,1024,3,64]{1,3,2,0:T(8,128)} fusion(f32[2,1024,3,64]{1,3,2,0:T(8,128)} %get-tuple-element.690, s32[]{:T(128)S(6)} %copy.225, f32[3,64,1024]{2,1,0:T(8,128)} %fusion.293, f32[3,512,1024]{2,1,0:T(8,128)} %fusion.284, f32[3,512,1024]{2,1,0:T(8,128)} %copy-done, f32[3,512]{1,0:T(4,128)S(1)} %get-tuple-element.627, ...), kind=kOutput, calls=%fused_computation.66.clone.1 | convolution fusion | flops 218827264 | bytes 28000268 | tf_op jit(solution)/shard_map/while/body/eval_jaxpr/hqk,qhd->khd/dot_general | solution.py:169
  601.4 1.9 fusion.292
  603.5 3.0 copy.167
  606.5 3.2 stack_reshape.14
  612.5 2.4 add_convert_fusion
  620.8 4.6 fusion.173
  626.4 2.2 reshape.314
  628.8 5.3 convolution_convert_fusion.3
  637.7 1.9 reduce-scatter.24.cloned.1.call-done
  641.2 25.0 %reduce-scatter.22.cloned.1.call-done = bf16[192,576]{1,0:T(8,128)(2,1)} async-done(((bf16[768,576]{1,0:T(8,128)(2,1)}), bf16[192,576]{1,0:T(8,128)(2,1)}) %reduce-scatter.22.cloned.1.call-update) | async-done | bytes 221200
  668.3 22.3 %reduce-scatter.20.cloned.1.call-done = bf16[512,192]{0,1:T(8,128)(2,1)} async-done(((bf16[512,768]{0,1:T(8,128)(2,1)}), bf16[512,192]{0,1:T(8,128)(2,1)}) %reduce-scatter.20.cloned.1.call-update) | async-done | bytes 196624 | tf_op jit(solution)/shard_map/reduce_scatter | solution.py:299
  690.7 6.0 bitcast_convert_fusion
  698.3 39.0 %psum.46 = f32[2,768]{1,0:T(2,128)S(1)} all-reduce(f32[2,768]{1,0:T(2,128)S(1)} %pad_maximum_fusion.11), channel_id=1, replica_groups=mesh['dp'=2,'row'=4,'col'=4] {'dp','row','col'}, use_global_device_ids=true, to_apply=%region_31.32 | all-reduce | flops 1536 | bytes 12288 | tf_op jit(solution)/shard_map/psum | solution.py:309
  748.2 41.4 %psum.47 = f32[]{:T(128)} all-reduce(f32[]{:T(128)S(6)} %add.293), channel_id=1, replica_groups=mesh['dp'=2,'row'=4,'col'=4] {'row','col'}, use_global_device_ids=true, to_apply=%region_33.34 | all-reduce | flops 1 | bytes 8 | tf_op jit(solution)/shard_map/psum | solution.py:313
  797.3 2.1 multiply_add_fusion.2
  799.4 3.3 multiply_add_fusion
  802.7 2.4 convert_add_fusion
  (281 shorter events, 105.9 us)
Async XLA Ops:
  8.0 49.4 %all-gather.6.cloned.1.call-start = ((), (), s32[]{:S(2)}) async-start(), calls=%async_computation.7 | async-start | bytes 3932160 | tf_op jit(solution)/shard_map/all_gather | solution.py:59
  8.8 161.5 %reduce-scatter.12.cloned.1.call-start = ((), (), s32[]{:S(2)}) async-start(), calls=%async_computation.8 | async-start | bytes 3932160 | tf_op jit(solution)/shard_map/reduce_scatter | solution.py:63
  57.3 5.2 copy-start.21
  82.4 1.8 copy-start.28
  93.5 1.8 copy-start.28
  104.7 1.8 copy-start.28
  115.9 1.8 copy-start.28
  120.7 2.2 copy-start.4
  123.7 2.8 copy-start.16
  126.4 43.8 %copy-start.2 = (bf16[512,768]{1,0:T(8,128)(2,1)S(1)}, bf16[512,768]{1,0:T(8,128)(2,1)}, u32[]{:S(2)}) copy-start(bf16[512,768]{1,0:T(8,128)(2,1)} %param.22) | copy-start | bytes 2359300
  126.5 67.3 %all-gather.10.cloned.1.call-start = ((), (), s32[]{:S(2)}) async-start(), calls=%async_computation.10 | async-start | bytes 1966080 | tf_op jit(solution)/shard_map/all_gather | solution.py:53
  127.3 46.8 %copy-start.23 = (f32[512,192]{0,1:T(8,128)S(1)}, f32[512,192]{0,1:T(8,128)}, u32[]{:S(2)}) copy-start(f32[512,192]{0,1:T(8,128)} %param.28) | copy-start | bytes 1179652
  127.4 90.6 %all-gather.8.cloned.1.call-start = ((), (), s32[]{:S(2)}) async-start(), calls=%async_computation.9 | async-start | bytes 3932160 | tf_op jit(solution)/shard_map/all_gather | solution.py:59
  174.1 102.0 %reduce-scatter.14.cloned.1.call-start = ((), (), s32[]{:S(2)}) async-start(), calls=%async_computation.11 | async-start | bytes 3932160 | tf_op jit(solution)/shard_map/reduce_scatter | solution.py:63
  193.8 31.6 %copy-start.32 = (bf16[512,768]{0,1:T(8,128)(2,1)}, bf16[512,768]{0,1:T(8,128)(2,1)S(1)}, u32[]{:S(2)}) copy-start(bf16[512,768]{0,1:T(8,128)(2,1)S(1)} %all_gather.33) | copy-start | bytes 2359300
  223.9 3.3 copy-start.10
  227.1 1.4 copy-start.20
  232.1 44.0 %copy-start.3 = (bf16[512,768]{1,0:T(8,128)(2,1)S(1)}, bf16[512,768]{1,0:T(8,128)(2,1)}, u32[]{:S(2)}) copy-start(bf16[512,768]{1,0:T(8,128)(2,1)} %reduce-scatter.12.cloned.1.call-done) | copy-start | bytes 2359300
  232.2 93.7 %all-gather.12.cloned.1.call-start = ((), (), s32[]{:S(2)}) async-start(), calls=%async_computation.12 | async-start | bytes 3932160 | tf_op jit(solution)/shard_map/all_gather | solution.py:69
  276.1 1.8 copy-start.18
  281.7 103.0 %reduce-scatter.16.cloned.1.call-start = ((), (), s32[]{:S(2)}) async-start(), calls=%async_computation.13 | async-start | bytes 3932160 | tf_op jit(solution)/shard_map/reduce_scatter | solution.py:73
  325.9 10.1 %copy-start.46 = (bf16[2,768,512]{2,1,0:T(8,128)(2,1)S(1)}, bf16[2,768,512]{2,1,0:T(8,128)(2,1)}, u32[]{:S(2)}) copy-start(bf16[2,768,512]{2,1,0:T(8,128)(2,1)} %all-gather.10.cloned.1.call-done) | copy-start | bytes 4718596
  334.0 1.3 copy-start.48
  334.0 1.9 copy-start.49
  340.8 93.2 %all-gather.14.cloned.1.call-start = ((), (), s32[]{:S(2)}) async-start(), calls=%async_computation.14 | async-start | bytes 3932160 | tf_op jit(solution)/shard_map/all_gather | solution.py:69
  384.7 3.0 copy-start.6
  384.7 3.0 copy-start.14
  389.8 245.8 %all-reduce.5.cloned.1.call-start = ((), (), s32[]{:S(2)}) async-start(), calls=%async_computation.19 | async-start | bytes 3145728
  401.0 40.5 %copy-start.5 = (bf16[2,1024,3,64]{1,3,2,0:T(8,128)(2,1)S(1)}, bf16[2,1024,3,64]{1,3,2,0:T(8,128)(2,1)}, u32[]{:S(2)}) copy-start(bf16[2,1024,3,64]{1,3,2,0:T(8,128)(2,1)} %copy-done.4) | copy-start | bytes 2359300
  401.0 40.5 %copy-start.45 = (s32[1,2]{1,0:T(1,128)S(1)}, s32[1,2]{1,0:T(1,128)}, u32[]{:S(2)}) copy-start(s32[1,2]{1,0:T(1,128)} %param.24) | copy-start | bytes 28
  401.0 238.6 %reduce-scatter.24.cloned.1.call-start = ((), (), s32[]{:S(2)}) async-start(), calls=%async_computation.18 | async-start | bytes 491520
  448.1 6.1 copy-start.1
  448.1 4.2 copy-start.9
  449.1 3.1 copy-start
  452.3 1.9 copy-start.30
  506.1 14.6 %copy-start.8 = (f32[512,3,64]{0,2,1:T(8,128)S(1)}, f32[512,3,64]{0,2,1:T(8,128)}, u32[]{:S(2)}) copy-start(f32[512,3,64]{0,2,1:T(8,128)} %fusion.291) | copy-start | bytes 1179652 | tf_op jit(solution)/shard_map/while
  528.8 6.1 copy-start.1
  528.8 4.2 copy-start.9
  529.9 3.1 copy-start
  533.0 1.9 copy-start.30
  586.9 14.5 %copy-start.8 = (f32[512,3,64]{0,2,1:T(8,128)S(1)}, f32[512,3,64]{0,2,1:T(8,128)}, u32[]{:S(2)}) copy-start(f32[512,3,64]{0,2,1:T(8,128)} %fusion.291) | copy-start | bytes 1179652 | tf_op jit(solution)/shard_map/while
  603.5 6.2 copy-start.7
  616.5 3.4 copy-start.13
  618.9 47.3 %reduce-scatter.22.cloned.1.call-start = ((), (), s32[]{:S(2)}) async-start(), calls=%async_computation.17 | async-start | bytes 1228800
  628.7 5.6 copy-start.47
  628.7 61.9 %reduce-scatter.20.cloned.1.call-start = ((), (), s32[]{:S(2)}) async-start(), calls=%async_computation.16 | async-start | bytes 983040 | tf_op jit(solution)/shard_map/reduce_scatter | solution.py:299
  634.0 56.6 %copy-start.22 = (bf16[3,768,192]{2,0,1:T(4,128)(2,1)S(1)}, bf16[3,768,192]{2,0,1:T(4,128)(2,1)}, u32[]{:S(2)}) copy-start(bf16[3,768,192]{2,0,1:T(4,128)(2,1)} %copy-done.21) | copy-start | bytes 2654212
  634.1 104.6 %all-reduce.7.cloned.1.call-start = ((), (), s32[]{:S(2)}) async-start(), calls=%async_computation.20 | async-start | bytes 1966080 | tf_op jit(solution)/shard_map/psum | solution.py:304
  690.6 112.1 %reduce-scatter.18.cloned.1.call-start = ((), (), s32[]{:S(2)}) async-start(), calls=%async_computation.15 | async-start | bytes 3932160 | tf_op jit(solution)/shard_map/reduce_scatter | solution.py:73
  696.7 1.3 copy-start.34
  696.7 1.6 copy-start.40
  696.7 1.6 copy-start.41
  696.7 51.3 %copy-start.35 = (f32[3,192,192]{2,1,0:T(8,128)S(1)}, f32[3,192,192]{2,1,0:T(8,128)}, u32[]{:S(2)}) copy-start(f32[3,192,192]{2,1,0:T(8,128)} %param.35) | copy-start | bytes 1327108
  790.3 4.5 copy-start.39
  791.5 3.3 copy-start.42
  791.5 3.3 copy-start.43
  791.5 3.9 copy-start.27
  791.6 3.9 copy-start.36
  791.6 3.9 copy-start.38
  791.6 5.7 copy-start.24
  791.6 5.7 copy-start.33
  791.6 5.6 copy-start.37
  792.7 6.7 copy-start.17
  799.4 3.3 copy-start.12
  (12 other events, 11.9 us)
Sparse Core Ops, SparseCore 0:
  10.7 46.6 all-gather.5
  126.6 43.6 reduce-scatter.11
  281.8 43.9 all-gather.11
  389.9 43.9 all-gather.13
  690.7 19.0 all-reduce.6
  713.0 45.9 reduce-scatter.17
Sparse Core Ops, SparseCore 1:
  129.1 36.6 all-gather.9
  174.2 43.8 all-gather.7
  232.2 43.8 reduce-scatter.13
  340.8 43.8 reduce-scatter.15
  401.1 68.8 all-reduce.4
  619.0 20.6 reduce-scatter.23
  641.9 24.2 reduce-scatter.21
  669.0 21.6 reduce-scatter.19
where the time goes:
time: 820 us; the launch traced here: 814 us
  waiting for transfers between devices  280 us (34%)
  matrix products  212 us (26%)
  blocking collectives  145 us (18%)
  local copies, waits for them, and re-layouts  75.3 us (9%)
  other arithmetic  62 us (8%)
  between operations  22.4 us (3%)
  loops' own time  15.4 us (2%)
    reduce_scatter x2, waiting for transfers between devices, sum_rows(): lax.psum_scatter(partial_value.astype(jnp.bfloat16), 'row', scatter_dimen...  85.3 us
    all_gather x2, waiting for transfers between devices, gather_grads(): return lax.all_gather(operand, 'row', axis=0, tiled=True)  76.7 us
    dot_general x4, matrix products, one_seq(): jnp.einsum('hqk,qhd->khd', grad_scores, query_blk, preferred_element_type...  57.6 us
    dot_general x4, matrix products, one_seq(): jnp.einsum('hqk,khd->qhd', grad_scores, key_seq, preferred_element_type=j...  53.5 us
    reduce_scatter x2, waiting for transfers between devices, sum_grads(): lax.psum_scatter(partial_value.astype(jnp.bfloat16), 'row', scatter_dimen...  43.9 us
    psum x1, blocking collectives, body(): grad_norm = jnp.sqrt(lax.psum(local_squares, ('row', 'col')))  41.4 us
    psum x1, blocking collectives, body(): lax.psum(jnp.stack([grad_gain_one, grad_gain_two]), ('dp', 'row', 'col'))  39 us
    all_gather x1, blocking collectives, gather_weights(): lax.all_gather(w_qkv.astype(jnp.bfloat16), 'col', axis=1, tiled=True)  28.5 us
  transfers between devices with their start and end apart: 14, of which 10 were waited for; matrix products, arithmetic and copies ran while one was open for 29% of the time, Pallas kernels for 0%

commit v1 on v0

v1 whole, which is shorter than its diff:
```python
import functools

import jax
import jax.numpy as jnp
import numpy as np
from jax import lax
from jax.experimental import pallas as pl
from jax.experimental.pallas import tpu as pltpu
from jax.sharding import PartitionSpec as P

HD = 64
LEN = 1024

EPSILON = 1e-06
THETA = 10000.0
MOMENTUM = 0.9
RATE = 300.0
DECAY = 0.6
CLIP = 1.0
NEGATIVE = -1e30

F32 = jnp.float32
BF16 = jnp.bfloat16
NT = (((1,), (1,)), ((), ()))
NN = (((1,), (0,)), ((), ()))
TN = (((0,), (0,)), ((), ()))
BQ = 256


def rope_tables():
    half = HD // 2
    freqs = np.float32(THETA) ** (-(np.arange(half, dtype=np.float32) * np.float32(2.0)) / np.float32(HD))
    angles = np.arange(LEN, dtype=np.float32)[:, None] * freqs[None, :].astype(np.float32)
    return np.cos(angles), np.sin(angles)


def padded_tables():
    cosine, sine = rope_tables()
    zero = np.zeros((LEN, HD), np.float32)
    return (
        jnp.asarray(np.concatenate([cosine, cosine, zero], 1)),
        jnp.asarray(np.concatenate([sine, -sine, zero], 1)),
    )


def mxu(lhs, rhs, dims):
    return lax.dot_general(lhs, rhs, dims, preferred_element_type=F32)


def causal(scores_t, block):
    keys = scores_t.shape[0]
    row = lax.broadcasted_iota(jnp.int32, (block, block), 0)
    column = lax.broadcasted_iota(jnp.int32, (block, block), 1)
    tail = jnp.where(row <= column, scores_t[keys - block :], NEGATIVE)
    return tail if keys == block else jnp.concatenate([scores_t[: keys - block], tail], 0)


def attend_forward_kernel(q_ref, k_ref, v_ref, o_ref, ot_ref, lse_ref):
    length = q_ref.shape[1]
    for block in range(length // BQ):
        keys = (block + 1) * BQ
        span = slice(block * BQ, keys)
        parts = []
        for head in range(3):
            scores = causal(mxu(k_ref[head, :keys, :], q_ref[head, span, :], NT), BQ)
            top = jnp.max(scores, 0, keepdims=True)
            probs = jnp.exp(scores - top).astype(BF16)
            out = mxu(v_ref[head, :keys, :], probs, TN)
            total = out[HD : HD + 1]
            parts.append(out[:HD] / total)
            lse_ref[0, head : head + 1, span] = top + jnp.log(total)
        out = jnp.concatenate(parts, 0)
        ot_ref[0, :, span] = out.astype(BF16)
        o_ref[0, span, :] = out.T.astype(BF16)


def attend_forward(q, k, v):
    heads, length, _ = q.shape
    groups = heads // 3
    blk = pl.BlockSpec((3, length, 128), lambda j: (j, 0, 0))
    return pl.pallas_call(
        attend_forward_kernel,
        grid=(groups,),
        in_specs=[blk] * 3,
        out_specs=[
            pl.BlockSpec((1, length, 192), lambda j: (j, 0, 0)),
            pl.BlockSpec((1, 192, length), lambda j: (j, 0, 0)),
            pl.BlockSpec((1, 8, length), lambda j: (j, 0, 0)),
        ],
        out_shape=[
            jax.ShapeDtypeStruct((groups, length, 192), BF16),
            jax.ShapeDtypeStruct((groups, 192, length), BF16),
            jax.ShapeDtypeStruct((groups, 8, length), F32),
        ],
        compiler_params=pltpu.CompilerParams(vmem_limit_bytes=48 << 20),
        cost_estimate=pl.CostEstimate(flops=4 << 30, bytes_accessed=6 << 20, transcendentals=4 << 20),
    )(q, k, v)


def attend_backward_kernel(
    q_ref, k_ref, v_ref, do_ref, ot_ref, lse_ref, cos_ref, sin_ref, dqk_ref, dv_ref, dk_acc, dv_acc
):
    length = q_ref.shape[1]
    products = do_ref[0].astype(F32).T * ot_ref[0].astype(F32)
    lane = lax.broadcasted_iota(jnp.int32, (1, 128), 1)

    def unrotate(t):
        swapped = jnp.where(lane < 32, pltpu.roll(t, 96, 1), pltpu.roll(t, 32, 1))
        return t * cos_ref[...] + swapped * sin_ref[...]

    for head in range(3):
        lanes = slice(head * HD, (head + 1) * HD)
        delta = jnp.sum(products[lanes], 0, keepdims=True)
        dq_parts = []
        for block in range(length // BQ):
            keys = (block + 1) * BQ
            span = slice(block * BQ, keys)
            before = keys - BQ
            q = q_ref[head, span, :]
            scores = causal(mxu(k_ref[head, :keys, :], q, NT), BQ)
            probs = jnp.exp(scores - lse_ref[0, head : head + 1, span])
            d_out = do_ref[0, span, lanes]
            d_probs = mxu(v_ref[head, :keys, :HD], d_out, NT)
            d_scores = (probs * (d_probs - delta[:, span])).astype(BF16)
            dv_part = mxu(probs.astype(BF16), d_out, NN)
            dk_part = mxu(d_scores, q, NN)
            if block:
                dv_acc[:before, :] += dv_part[:before]
                dk_acc[:before, :] += dk_part[:before]
            dv_acc[before:keys, :] = dv_part[before:]
            dk_acc[before:keys, :] = dk_part[before:]
            dq_parts.append(mxu(d_scores, k_ref[head, :keys, :], TN))
        dq = jnp.concatenate(dq_parts, 0) * (HD ** -0.5)
        dqk_ref[0, :, head * HD : (head + 1) * HD] = unrotate(dq)[:, :HD].astype(BF16)
        dqk_ref[0, :, 192 + head * HD : 192 + (head + 1) * HD] = unrotate(dk_acc[...])[:, :HD].astype(BF16)
        dv_ref[0, :, lanes] = dv_acc[...].astype(BF16)


def attend_backward(q, k, v, d_out, out_t, lse, cos, sin):
    heads, length, _ = q.shape
    groups = heads // 3
    blk = pl.BlockSpec((3, length, 128), lambda j: (j, 0, 0))
    table = pl.BlockSpec((length, 128), lambda j: (0, 0))
    wide = pl.BlockSpec((1, length, 192), lambda j: (j, 0, 0))
    return pl.pallas_call(
        attend_backward_kernel,
        grid=(groups,),
        in_specs=[blk] * 3
        + [
            wide,
            pl.BlockSpec((1, 192, length), lambda j: (j, 0, 0)),
            pl.BlockSpec((1, 8, length), lambda j: (j, 0, 0)),
            table,
            table,
        ],
        out_specs=[pl.BlockSpec((1, length, 384), lambda j: (j, 0, 0)), wide],
        out_shape=[
            jax.ShapeDtypeStruct((groups, length, 384), BF16),
            jax.ShapeDtypeStruct((groups, length, 192), BF16),
        ],
        scratch_shapes=[pltpu.VMEM((length, 128), F32), pltpu.VMEM((length, HD), F32)],
        compiler_params=pltpu.CompilerParams(vmem_limit_bytes=56 << 20),
        cost_estimate=pl.CostEstimate(flops=10 << 30, bytes_accessed=8 << 20, transcendentals=4 << 20),
    )(q, k, v, d_out, out_t, lse, cos, sin)


def update(grad_full, moment, weight, average, factor):
    clipped = grad_full * factor
    new_moment = MOMENTUM * moment + clipped
    new_weight = weight - RATE * (clipped + MOMENTUM * new_moment)
    new_average = DECAY * average + (1.0 - DECAY) * new_weight
    return (new_moment, new_weight, new_average)


def body(
    rows,
    cols,
    block_input,
    out_grad,
    lengths,
    w_qkv,
    w_out,
    w_gate_up,
    w_down,
    gains,
    mom_qkv,
    mom_out,
    mom_gate_up,
    mom_down,
    mom_gains,
    ema_qkv,
    ema_out,
    ema_gate_up,
    ema_down,
    ema_gains,
):
    d = lax.axis_index("dp")
    r = lax.axis_index("row")
    c = lax.axis_index("col")
    core0 = d == 0
    tokens, width = block_input.shape
    ring = cols <= 4
    part = width // cols

    pairs = [(i, j) for i in range(2) for j in range(rows)]
    swap_pairs = [(i * rows + j, (j % 2) * rows + (j // 2) * 2 + i) for i, j in pairs]
    first_pairs = [(i * rows + j, i * rows + (j ^ (1 if i == 0 else 2))) for i, j in pairs]
    second_pairs = [(i * rows + j, i * rows + (j ^ (2 if i == 0 else 1))) for i, j in pairs]

    def swap_tokens(t):
        return lax.ppermute(t, ("dp", "row"), swap_pairs)

    def first(t):
        return lax.ppermute(t, ("dp", "row"), first_pairs)

    def second(t):
        return lax.ppermute(t, ("dp", "row"), second_pairs)

    def core(t):
        return lax.ppermute(t, "dp", [(0, 1), (1, 0)])

    def along(t, k):
        return lax.ppermute(t, "col", [(i, (i + k) % cols) for i in range(cols)])

    def sum_all(t):
        for axis, size in (("dp", 2), ("row", rows), ("col", cols)):
            bit = 1
            while bit < size:
                t = t + lax.ppermute(t, axis, [(i, i ^ bit) for i in range(size)])
                bit *= 2
        return t

    def relative(t):
        if not ring:
            return t
        return lax.dynamic_slice_in_dim(jnp.concatenate([t, t], -1), c * part, width, t.ndim - 1)

    def absolute(t):
        if not ring:
            return t
        back = (cols - c) % cols
        return lax.dynamic_slice_in_dim(jnp.concatenate([t, t], -1), back * part, width, t.ndim - 1)

    def gather_cols(t, axis):
        if not ring:
            return lax.all_gather(t, "col", axis=axis, tiled=True)
        got = [t] + [along(t, k) for k in range(1, cols)]
        return jnp.concatenate([got[-k % cols] for k in range(cols)], axis)

    def gather_rows(t):
        one, two = first(t), second(t)
        return [t, one, two, second(one)]

    def scatter_rows(slots):
        slot_one = (slots[1].astype(F32) + second(slots[3]).astype(F32)).astype(BF16)
        return slots[0].astype(F32) + first(slot_one).astype(F32) + second(slots[2]).astype(F32)

    def scatter_cols(t, axis):
        if not ring:
            return lax.psum_scatter(t, "col", scatter_dimension=axis, tiled=True).astype(F32)
        blocks = [lax.slice_in_dim(t, k * part, (k + 1) * part, axis=axis) for k in range(cols)]
        total = blocks[0].astype(F32)
        for k in range(1, cols):
            total = total + along(blocks[k], k).astype(F32)
        return total

    x_own = relative(swap_tokens(block_input))
    own_length = swap_tokens(lengths)[0, :]
    seq_ids = jnp.arange(own_length.shape[0], dtype=jnp.int32)
    own_length = jnp.sum(jnp.where(seq_ids == r // 2, own_length, 0))
    gains_rel = relative(gains)

    half = w_gate_up.shape[2] // 2
    wq = w_qkv.astype(BF16)
    head_cols = wq.shape[2]
    piece_qk = jnp.concatenate([wq[0], wq[1]], 1)
    piece_vo = jnp.concatenate([wq[2], w_out.T.astype(BF16)], 1)
    piece_a = jnp.where(core0, piece_qk, piece_vo)
    wgu = lax.dynamic_slice_in_dim(w_gate_up, d * half, half, 2).astype(BF16)
    piece_g = jnp.concatenate([wgu[0], wgu[1]], 1)
    piece_d = lax.dynamic_slice_in_dim(w_down, d * half, half, 0).T.astype(BF16)

    slots_d = jnp.stack(gather_rows(piece_d))
    full_a = gather_cols(piece_a, 0)
    slots_a = gather_rows(full_a)
    full_g = gather_cols(piece_g, 0)
    w_gu = jnp.stack(gather_rows(full_g))
    w_dn = gather_cols(slots_d, 1)

    keep = jnp.where(core0, jnp.stack([slots_a[0], slots_a[1]]), jnp.stack([slots_a[1], slots_a[3]]))
    send = jnp.where(core0, jnp.stack([slots_a[2], slots_a[3]]), jnp.stack([slots_a[0], slots_a[2]]))
    got = core(send)
    w_qk = jnp.where(core0, keep, got)
    w_vo = jnp.where(core0, got, keep)

    x_other = core(x_own)
    x_full = jnp.where(
        core0, jnp.concatenate([x_own, x_other], 0), jnp.concatenate([x_other, x_own], 0)
    )
    cosine, sine = rope_tables()
    cosine = jnp.asarray(cosine)[None, :, None, :]
    sine = jnp.asarray(sine)[None, :, None, :]
    heads = head_cols // HD

    def rotate(t):
        t = t.reshape(2, LEN, heads, HD)
        u, w = t[..., : HD // 2], t[..., HD // 2 :]
        return jnp.concatenate([u * cosine - w * sine, u * sine + w * cosine], -1)

    def by_head(t, tail):
        t = t.reshape(2, LEN, heads, HD).transpose(0, 2, 1, 3).reshape(2 * heads, LEN, HD).astype(BF16)
        extra = jnp.broadcast_to(tail[None, :, None], (2 * heads, LEN, 1))
        return jnp.concatenate([t, extra, jnp.zeros((2 * heads, LEN, HD - 1), BF16)], -1)

    qk = jnp.einsum("td,jde->jte", x_full, w_qk, preferred_element_type=F32)
    v = jnp.einsum("td,jde->jte", x_full, w_vo[:, :, :head_cols], preferred_element_type=F32)
    ones = jnp.ones((LEN,), BF16)
    bias = jnp.where(jnp.arange(LEN, dtype=jnp.int32) < own_length, 0.0, NEGATIVE).astype(BF16)
    q_pad = by_head(rotate(qk[:, :, :head_cols]) * (HD ** -0.5), ones)
    k_pad = by_head(rotate(qk[:, :, head_cols:]), bias)
    v_pad = by_head(v, ones)
    attended, attended_t, lse = attend_forward(q_pad, k_pad, v_pad)

    def split_sum(whole):
        own = lax.dynamic_index_in_dim(whole, d, 0, keepdims=False)
        other = lax.dynamic_index_in_dim(whole, 1 - d, 0, keepdims=False)
        return own, core(other.astype(BF16)).astype(F32)

    w_o = w_vo[:, :, head_cols:]
    partial = jnp.einsum("jte,jde->td", attended, w_o, preferred_element_type=F32)
    own, other = split_sum(partial.reshape(2, tokens, width))
    residual = x_own.astype(F32) + (own + other)
    scale_one = lax.rsqrt(jnp.mean(residual * residual, -1, keepdims=True) + EPSILON)
    normed = residual * scale_one * gains_rel[0]
    normed_b = normed.astype(BF16)
    normed_full = jnp.concatenate([normed_b, core(normed_b)], 0)

    gate_up = jnp.einsum("td,sde->ste", normed_full, w_gu, preferred_element_type=F32)
    gate_act = gate_up[:, :, :half]
    up_act = gate_up[:, :, half:]
    sigmoid_g = jax.nn.sigmoid(gate_act)
    silu_g = gate_act * sigmoid_g
    hidden = (silu_g * up_act).astype(BF16)
    ffn_other = jnp.einsum("ste,sde->td", hidden[:, tokens:], w_dn, preferred_element_type=F32)
    ffn_got = core(ffn_other.astype(BF16)).astype(F32)
    ffn_own = jnp.einsum("ste,sde->td", hidden[:, :tokens], w_dn, preferred_element_type=F32)
    summed = normed + (ffn_own + ffn_got)
    scale_two = lax.rsqrt(jnp.mean(summed * summed, -1, keepdims=True) + EPSILON)
    output = summed * scale_two * gains_rel[1]
    output = swap_tokens(absolute(output.astype(BF16))).astype(F32)

    position = d * tokens + jnp.arange(tokens, dtype=jnp.int32)
    row_live = (position < own_length).astype(F32)[:, None]
    cot_live = relative(swap_tokens(out_grad)).astype(F32) * row_live
    grad_gain_two = jnp.sum(cot_live * summed * scale_two, 0)
    hat_two = cot_live * gains_rel[1]
    inner_two = jnp.sum(hat_two * summed, -1, keepdims=True)
    d_summed = scale_two * (hat_two - summed * scale_two * scale_two * inner_two / width)
    d_ffn = d_summed.astype(BF16)
    d_ffn_full = jnp.concatenate([d_ffn, core(d_ffn)], 0)
    grad_dn = jnp.einsum("td,ste->sde", d_ffn_full, hidden, preferred_element_type=F32).astype(BF16)
    shard_d = scatter_rows([t for t in scatter_cols(grad_dn, 1).astype(BF16)])
    d_hidden = jnp.einsum("td,sde->ste", d_ffn_full, w_dn, preferred_element_type=F32)
    d_gate = d_hidden * up_act * (sigmoid_g * (1.0 + gate_act * (1.0 - sigmoid_g)))
    d_up = d_hidden * silu_g
    d_gu = jnp.concatenate([d_gate, d_up], -1).astype(BF16)
    dn_other = jnp.einsum("ste,sde->td", d_gu[:, tokens:], w_gu, preferred_element_type=F32)
    dn_got = core(dn_other.astype(BF16)).astype(F32)
    dn_own = jnp.einsum("ste,sde->td", d_gu[:, :tokens], w_gu, preferred_element_type=F32)
    grad_gu = [
        jnp.einsum("td,te->de", normed_full, d_gu[s], preferred_element_type=F32).astype(BF16)
        for s in range(4)
    ]
    shard_g = scatter_cols(scatter_rows(grad_gu).astype(BF16), 0)
    d_normed = d_summed + (dn_own + dn_got)
    grad_gain_one = jnp.sum(d_normed * residual * scale_one, 0)
    hat_one = d_normed * gains_rel[0]
    inner_one = jnp.sum(hat_one * residual, -1, keepdims=True)
    d_residual = scale_one * (hat_one - residual * scale_one * scale_one * inner_one / width)
    d_branch = d_residual.astype(BF16)
    d_branch_other = core(d_branch)
    d_branch_full = jnp.where(
        core0,
        jnp.concatenate([d_branch, d_branch_other], 0),
        jnp.concatenate([d_branch_other, d_branch], 0),
    )
    d_attended = jnp.einsum("td,jde->jte", d_branch_full, w_o, preferred_element_type=F32).astype(BF16)
    cos_pad, sin_pad = padded_tables()
    d_qk, d_v = attend_backward(q_pad, k_pad, v_pad, d_attended, attended_t, lse, cos_pad, sin_pad)
    grad_o = jnp.einsum("td,jte->jde", d_branch_full, attended, preferred_element_type=F32)
    grad_v = jnp.einsum("td,jte->jde", x_full, d_v, preferred_element_type=F32)
    grad_qk = jnp.einsum("td,jte->jde", x_full, d_qk, preferred_element_type=F32).astype(BF16)
    grad_vo = jnp.concatenate([grad_v, grad_o], -1).astype(BF16)
    mine = jnp.where(core0, grad_qk, grad_vo)
    got = core(jnp.where(core0, grad_vo, grad_qk))
    slots = [
        jnp.where(core0, mine[0], got[0]),
        jnp.where(core0, mine[1], mine[0]),
        jnp.where(core0, got[0], got[1]),
        jnp.where(core0, got[1], mine[1]),
    ]
    shard_a = scatter_cols(scatter_rows(slots).astype(BF16), 0)
    dx = jnp.einsum("jte,jde->td", d_qk, w_qk, preferred_element_type=F32) + jnp.einsum(
        "jte,jde->td", d_v, w_vo[:, :, :head_cols], preferred_element_type=F32
    )
    own, other = split_sum(dx.reshape(2, tokens, width))
    input_grad = absolute((d_residual + (own + other)).astype(BF16))
    input_grad = swap_tokens(input_grad).astype(F32)

    def both(t):
        t = t.astype(BF16)
        other = core(t)
        return jnp.where(core0, t, other).astype(F32), jnp.where(core0, other, t).astype(F32), t.astype(F32)

    g_qk, g_vo, own_a = both(shard_a)
    g_lo, g_hi, own_g = both(shard_g)
    d_lo, d_hi, own_d = both(shard_d)
    g_qkv = jnp.stack([g_qk[:, :head_cols], g_qk[:, head_cols:], g_vo[:, :head_cols]])
    g_out = g_vo[:, head_cols:].T
    g_gate_up = jnp.stack(
        [
            jnp.concatenate([g_lo[:, :half], g_hi[:, :half]], 1),
            jnp.concatenate([g_lo[:, half:], g_hi[:, half:]], 1),
        ]
    )
    g_down = jnp.concatenate([d_lo.T, d_hi.T], 0)
    gain_total = sum_all(absolute(jnp.stack([grad_gain_one, grad_gain_two])))
    local_squares = jnp.sum(own_a * own_a) + jnp.sum(own_g * own_g) + jnp.sum(own_d * own_d)
    first_device = core0 & (r == 0) & (c == 0)
    local_squares = local_squares + jnp.where(first_device, jnp.sum(gain_total * gain_total), 0.0)
    squares = sum_all(jnp.full((8, 128), local_squares, F32))[0, 0]
    grad_norm = jnp.sqrt(squares)
    factor = jnp.minimum(1.0, CLIP / (grad_norm + 1e-06))
    grads_all = (g_qkv, g_out, g_gate_up, g_down, gain_total)
    params = (w_qkv, w_out, w_gate_up, w_down, gains)
    moments = (mom_qkv, mom_out, mom_gate_up, mom_down, mom_gains)
    averages = (ema_qkv, ema_out, ema_gate_up, ema_down, ema_gains)
    results = [
        update(g_arr, m_arr, w_arr, e_arr, factor)
        for g_arr, m_arr, w_arr, e_arr in zip(grads_all, moments, params, averages)
    ]
    return (
        output,
        input_grad,
        grad_norm,
        *[t[0] for t in results],
        *[t[1] for t in results],
        *[t[2] for t in results],
    )


def solution(mesh):
    tok = P(("dp", "col", "row"), None)
    weights = (P(None, "col", "row"), P("row", "col"), P(None, "col", "row"), P("row", "col"), P())
    in_specs = (tok, tok, P(("dp", "col"), None)) + weights * 3
    out_specs = (tok, tok, P()) + weights * 3
    fn = functools.partial(body, mesh.shape["row"], mesh.shape["col"])
    return jax.shard_map(fn, mesh=mesh, in_specs=in_specs, out_specs=out_specs, check_vma=False)
```

time: 820 us -> 474 us (0.58)
  matrix products: 212 us -> 53.8 us
  blocking collectives: 145 us -> 0 us
  waiting for transfers between devices: 280 us -> 168 us
  starting transfers between devices: 1.51 us -> 98.9 us
  Pallas kernels: 0 us -> 30.4 us
  local copies, waits for them, and re-layouts: 75.3 us -> 53.4 us
  between operations: 22.4 us -> 6.95 us
  loops' own time: 15.4 us -> 0 us
    ppermute x0 -> x64, waiting for transfers between devices: none -> 168 us  [the longest x18 101 us: along(): return lax.ppermute(t, 'col', [(i, (i + k) % cols) for i in range(cols)])]
    dot_general x40 -> x20, matrix products: 212 us -> 53.8 us  [the longest x1 6.13 us: body(): jnp.einsum('td,sde->ste', d_ffn_full, w_dn, preferred_element_type=F32)]
    reduce_scatter x5 -> x0, waiting for transfers between devices: 151 us -> none  [the longest x2 85.3 us: sum_rows(): lax.psum_scatter(partial_value.astype(jnp.bfloat16), 'row', scatter_dimen...]
    all_gather x5 -> x0, waiting for transfers between devices: 101 us -> none  [the longest x2 76.7 us: gather_grads(): return lax.all_gather(operand, 'row', axis=0, tiled=True)]
    ppermute x0 -> x64, starting transfers between devices: none -> 98.9 us  [the longest x18 29.3 us: along(): return lax.ppermute(t, 'col', [(i, (i + k) % cols) for i in range(cols)])]
    psum x2 -> x0, blocking collectives: 80.4 us -> none  [the longest x1 41.4 us: body(): grad_norm = jnp.sqrt(lax.psum(local_squares, ('row', 'col')))]
    all_gather x3 -> x0, blocking collectives: 64.4 us -> none  [the longest x1 28.5 us: gather_weights(): lax.all_gather(w_qkv.astype(jnp.bfloat16), 'col', axis=1, tiled=True)]
    pallas_call x0 -> x2, Pallas kernels: none -> 30.4 us  [the longest x1 17.4 us: attend_backward(): pl.pallas_call(attend_backward_kernel, grid=(groups,), in_specs=[blk] * 3...]
  transfers between devices with their start and end apart: 14 -> 64, of which waited for: 10 -> 26; matrix products, arithmetic and copies ran while one was open for 29% -> 30% of each run, Pallas kernels for 0% -> 6%
where the time goes in v1:
time: 474 us; the launch traced here: 468 us
  waiting for transfers between devices  168 us (35%)
  starting transfers between devices  98.9 us (21%)
  other arithmetic  56.3 us (12%)
  matrix products  53.8 us (11%)
  local copies, waits for them, and re-layouts  53.4 us (11%)
  Pallas kernels  30.4 us (6%)
  between operations  6.95 us (1%)
    ppermute x18, waiting for transfers between devices, along(): return lax.ppermute(t, 'col', [(i, (i + k) % cols) for i in range(cols)])  101 us
    unnamed x201, local copies, waits for them, and re-layouts  37.6 us
    ppermute x12, waiting for transfers between devices, second(): return lax.ppermute(t, ('dp', 'row'), second_pairs)  29.9 us
    ppermute x18, starting transfers between devices, along(): return lax.ppermute(t, 'col', [(i, (i + k) % cols) for i in range(cols)])  29.3 us
    ppermute x10, starting transfers between devices, sum_all(): t = t + lax.ppermute(t, axis, [(i, i ^ bit) for i in range(size)])  23.8 us
    ppermute x10, waiting for transfers between devices, sum_all(): t = t + lax.ppermute(t, axis, [(i, i ^ bit) for i in range(size)])  19.8 us
    pallas_call x1, Pallas kernels, attend_backward(): pl.pallas_call(attend_backward_kernel, grid=(groups,), in_specs=[blk] * 3...  17.4 us
    ppermute x6, waiting for transfers between devices, first(): return lax.ppermute(t, ('dp', 'row'), first_pairs)  17.3 us
  transfers between devices with their start and end apart: 64, of which 26 were waited for; matrix products, arithmetic and copies ran while one was open for 30% of the time, Pallas kernels for 6%

profile of v1, /device:TPU:0, one launch (start us, length us, event | category | flops | bytes accessed | tf_op | source)
XLA Modules:
  0.0 468.0 jit_solution(9700644014955887650)
XLA Ops:
  2.2 5.1 %collective-permute-start.1 = (bf16[192,384]{0,1:T(8,128)(2,1)S(1)}, bf16[192,384]{0,1:T(8,128)(2,1)S(1)}, u32[]{:S(2)}, u32[]{:S(2)}) collective-permute-start(bf16[192,384]{0,1:T(8,128)(2,1)S(1)} %maximum_select_fusion.2), channel_id=1, source_target_pairs={{0,3},{1,0},{2,1},{3,2},{4,7},{5,4},{6,5},{7,6},{8,11},{9,8},{10,9... | collective-permute-start | bytes 442376 | tf_op jit(solution)/shard_map/ppermute | solution.py:223
  8.3 4.3 collective-permute-done.1
  12.7 11.3 %collective-permute-done.2 = bf16[192,384]{0,1:T(8,128)(2,1)S(1)} collective-permute-done((bf16[192,384]{0,1:T(8,128)(2,1)S(1)}, bf16[192,384]{0,1:T(8,128)(2,1)S(1)}, u32[]{:S(2)}, u32[]{:S(2)}) %collective-permute-start.2) | collective-permute-done | bytes 147488 | tf_op jit(solution)/shard_map/ppermute | solution.py:223
  27.3 13.1 %collective-permute-done.4 = bf16[768,384]{0,1:T(8,128)(2,1)S(1)} collective-permute-done((bf16[768,384]{0,1:T(8,128)(2,1)S(1)}, bf16[768,384]{0,1:T(8,128)(2,1)S(1)}, u32[]{:S(2)}, u32[]{:S(2)}) %collective-permute-start.4) | collective-permute-done | bytes 589856 | tf_op jit(solution)/shard_map/ppermute | solution.py:214
  42.6 7.7 %collective-permute-done.5 = bf16[768,384]{0,1:T(8,128)(2,1)S(1)} collective-permute-done((bf16[768,384]{0,1:T(8,128)(2,1)S(1)}, bf16[768,384]{0,1:T(8,128)(2,1)S(1)}, u32[]{:S(2)}, u32[]{:S(2)}) %collective-permute-start.5) | collective-permute-done | bytes 589856 | tf_op jit(solution)/shard_map/ppermute | solution.py:217
  52.3 3.9 collective-permute-start.8
  59.8 2.9 collective-permute-start.12
  63.5 2.0 collective-permute-start.13
  68.3 17.9 %collective-permute-done.12 = bf16[192,512]{0,1:T(8,128)(2,1)S(1)} collective-permute-done((bf16[192,512]{0,1:T(8,128)(2,1)}, bf16[192,512]{0,1:T(8,128)(2,1)S(1)}, u32[]{:S(2)}, u32[]{:S(2)}) %collective-permute-start.12) | collective-permute-done | bytes 196640 | tf_op jit(solution)/shard_map/ppermute | solution.py:223
  86.2 2.3 pad_maximum_fusion.11
  88.5 2.2 collective-permute-start.14
  90.7 3.4 convolution_bitcast_fusion.1
  96.9 2.5 copy.119
  99.3 3.2 copy.120
  102.5 2.7 fusion.99
  105.2 3.2 copy.121
  108.4 3.2 copy.122
  111.6 2.2 broadcast_select_fusion.2
  113.7 3.1 fusion.26
  117.9 2.4 copy.78
  120.3 4.9 %subtract_convert_fusion = (bf16[2,1024,3,32]{3,1,2,0:T(8,128)(2,1)S(1)}, bf16[2,1024,3,32]{3,1,2,0:T(8,128)(2,1)S(1)}, f32[2,1024,3,32]{3,1,2,0:T(8,128)S(1)}, f32[2,1024,3,32]{3,1,2,0:T(8,128)S(1)}) fusion(f32[2,1024,3,32]{3,1,2,0:T(8,128)} %copy.122, f32[2,1024,3,32]{3,1,2,0:T(8,128)} %copy.121, f32[1024,32]{1,0:T(8,128)} %constant.121.clone, ...), kind=kLoop, calls=%fused_computation.24 | loop fusion | flops 2752512 | bytes 5767168 | tf_op jit(solution)/shard_map/convert.19
  128.4 2.9 maximum_maximum_fusion.2
  131.3 13.0 %shard_map.349 = (bf16[2,1024,192]{2,1,0:T(8,128)(2,1)S(1)}, bf16[2,192,1024]{2,1,0:T(8,128)(2,1)S(1)}, f32[2,8,1024]{2,1,0:T(8,128)S(1)}) custom-call(bf16[6,1024,128]{2,1,0:T(8,128)(2,1)S(1)} %get-tuple-element.150.q_ref, bf16[6,1024,128]{2,1,0:T(8,128)(2,1)S(1)} %get-tuple-element.151.k_ref, bf16[6,1024,128]{2,1,0:T(8,128)(2,1)} %get-tuple-element.149.v_ref), custom_call_target="tpu_custom_call" | custom-call | flops 4294967296 | bytes 6291456 | tf_op jit(solution)/shard_map/pallas_call | solution.py:81
  149.7 2.6 multiply_reduce_fusion.5
  155.4 4.2 collective-permute-done.18
  160.8 9.4 %collective-permute-done.19 = bf16[192,256]{1,0:T(8,128)(2,1)S(1)} collective-permute-done((bf16[192,256]{1,0:T(8,128)(2,1)S(1)}, bf16[192,256]{1,0:T(8,128)(2,1)S(1)}, u32[]{:S(2)}, u32[]{:S(2)}) %collective-permute-start.19) | collective-permute-done | bytes 98336 | tf_op jit(solution)/shard_map/ppermute | solution.py:217
  175.9 4.6 convolution_bitcast_fusion
  183.9 21.6 %collective-permute-done.22 = bf16[4,192,256]{2,1,0:T(8,128)(2,1)S(1)} collective-permute-done((bf16[4,192,256]{2,1,0:T(8,128)(2,1)S(1)}, bf16[4,192,256]{2,1,0:T(8,128)(2,1)S(1)}, u32[]{:S(2)}, u32[]{:S(2)}) %collective-permute-start.22) | collective-permute-done | bytes 393248 | tf_op jit(solution)/shard_map/ppermute | solution.py:223
  205.6 3.8 bitcast_convert_fusion.1
  212.2 3.3 multiply_reduce_fusion.4
  218.4 8.0 %collective-permute-start.27 = (bf16[512,768]{1,0:T(8,128)(2,1)}, bf16[512,768]{1,0:T(8,128)(2,1)}, u32[]{:S(2)}, u32[]{:S(2)}) collective-permute-start(bf16[512,768]{1,0:T(8,128)(2,1)} %get-tuple-element.104), channel_id=1, source_target_pairs={{0,16},{16,0},{1,17},{17,1},{2,18},{18,2},{3,19},{19,3},{4,20},{20... | collective-permute-start | bytes 2359304 | tf_op jit(solution)/shard_map/ppermute | solution.py:220
  226.4 2.0 copy.97
  232.5 2.1 copy.94
  234.6 2.2 copy.98
  238.4 7.5 %collective-permute-start.25 = (bf16[512,768]{1,0:T(8,128)(2,1)}, bf16[512,768]{1,0:T(8,128)(2,1)}, u32[]{:S(2)}, u32[]{:S(2)}) collective-permute-start(bf16[512,768]{1,0:T(8,128)(2,1)} %fusion.55), channel_id=1, source_target_pairs={{0,0},{4,16},{8,8},{12,24},{16,4},{20,20},{24,12},{28,28},{1,1},{5... | collective-permute-start | bytes 2359304 | tf_op jit(solution)/shard_map/ppermute | solution.py:211
  246.0 6.1 %fusion.2 = (bf16[4,1024,256]{1,2,0:T(8,128)(2,1)S(1)}, bf16[4,1024,256]{1,2,0:T(8,128)(2,1)S(1)}) fusion(f32[4,1024,512]{1,2,0:T(8,128)} %copy-done.5, bf16[512,768]{1,0:T(8,128)(2,1)} %collective-permute-done.27, bf16[512,768]{1,0:T(8,128)(2,1)} %get-tuple-element.104, bf16[4,192,256]{2,1,0:T(8,128)(2,1)S(1)} %copy-done.84, ...), kind=kOutput, calls=%fused_computation.14 | convolution fusion | flops 1638400000 | bytes 15728640 | tf_op jit(solution)/shard_map/td,sde->ste/dot_general | solution.py:363
  252.2 3.8 bitcast_convert_fusion
  256.1 3.2 fusion.20
  262.8 3.3 collective-permute-start.47
  270.1 6.3 %collective-permute-done.45 = bf16[4,192,256]{1,2,0:T(8,128)(2,1)S(1)} collective-permute-done((bf16[4,192,256]{1,2,0:T(8,128)(2,1)S(1)}, bf16[4,192,256]{1,2,0:T(8,128)(2,1)S(1)}, u32[]{:S(2)}, u32[]{:S(2)}) %collective-permute-start.45) | collective-permute-done | bytes 393248 | tf_op jit(solution)/shard_map/ppermute | solution.py:223
  278.0 20.6 %collective-permute-done.46 = bf16[4,192,256]{1,2,0:T(8,128)(2,1)S(1)} collective-permute-done((bf16[4,192,256]{1,2,0:T(8,128)(2,1)S(1)}, bf16[4,192,256]{1,2,0:T(8,128)(2,1)S(1)}, u32[]{:S(2)}, u32[]{:S(2)}) %collective-permute-start.46) | collective-permute-done | bytes 393248 | tf_op jit(solution)/shard_map/ppermute | solution.py:223
  301.6 3.9 multiply_reduce_fusion.1
  306.6 5.5 %collective-permute-done.48 = bf16[192,256]{0,1:T(8,128)(2,1)S(1)} collective-permute-done((bf16[192,256]{0,1:T(8,128)(2,1)S(1)}, bf16[192,256]{0,1:T(8,128)(2,1)S(1)}, u32[]{:S(2)}, u32[]{:S(2)}) %collective-permute-start.48) | collective-permute-done | bytes 98336 | tf_op jit(solution)/shard_map/ppermute | solution.py:217
  315.0 2.5 collective-permute-done.52
  318.2 2.0 collective-permute-start.40
  322.0 2.2 copy.88
  324.2 17.4 %shard_map.350 = (bf16[2,1024,384]{2,1,0:T(8,128)(2,1)}, bf16[2,1024,192]{2,1,0:T(8,128)(2,1)}) custom-call(bf16[6,1024,128]{2,1,0:T(8,128)(2,1)} %copy-done, bf16[6,1024,128]{2,1,0:T(8,128)(2,1)} %copy-done.1, bf16[6,1024,128]{2,1,0:T(8,128)(2,1)} %get-tuple-element.149.v_ref, bf16[2,1024,192]{2,1,0:T(8,128)(2,1)} %bitcast.202, ...), custom_call_target="tpu_custom_call" | custom-call | flops 10737418240 | bytes 8388608 | tf_op jit(solution)/shard_map/pallas_call | solution.py:145
  342.9 2.8 fusion.27
  345.8 4.6 broadcast_select_fusion.1
  354.1 10.1 %collective-permute-start.54 = (f32[2,768]{1,0:T(2,128)S(1)}, f32[2,768]{1,0:T(2,128)S(1)}, u32[]{:S(2)}, u32[]{:S(2)}) collective-permute-start(f32[2,768]{1,0:T(2,128)S(1)} %add.282), channel_id=1, source_target_pairs={{0,1},{1,0},{2,3},{3,2},{4,5},{5,4},{6,7},{7,6},{8,9},{9,8},{10,11... | collective-permute-start | bytes 18440 | tf_op jit(solution)/shard_map/ppermute | solution.py:229
  365.2 2.4 convert_element_type.311
  367.6 3.4 collective-permute-start.55
  379.0 2.9 collective-permute-start.43
  381.9 2.8 collective-permute-start.44
  390.3 5.0 %collective-permute-done.43 = bf16[192,512]{1,0:T(8,128)(2,1)S(1)} collective-permute-done((bf16[192,512]{1,0:T(8,128)(2,1)S(1)}, bf16[192,512]{1,0:T(8,128)(2,1)S(1)}, u32[]{:S(2)}, u32[]{:S(2)}) %collective-permute-start.43) | collective-permute-done | bytes 196640 | tf_op jit(solution)/shard_map/ppermute | solution.py:223
  396.0 5.9 %collective-permute-done.35 = bf16[768,384]{0,1:T(8,128)(2,1)S(1)} collective-permute-done((bf16[768,384]{0,1:T(8,128)(2,1)S(1)}, bf16[768,384]{0,1:T(8,128)(2,1)S(1)}, u32[]{:S(2)}, u32[]{:S(2)}) %collective-permute-start.35) | collective-permute-done | bytes 589856 | tf_op jit(solution)/shard_map/ppermute | solution.py:217
  404.1 3.3 collective-permute-start.38
  408.0 5.3 %collective-permute-done.36 = bf16[192,384]{0,1:T(8,128)(2,1)S(1)} collective-permute-done((bf16[192,384]{0,1:T(8,128)(2,1)S(1)}, bf16[192,384]{0,1:T(8,128)(2,1)S(1)}, u32[]{:S(2)}, u32[]{:S(2)}) %collective-permute-start.36) | collective-permute-done | bytes 147488 | tf_op jit(solution)/shard_map/ppermute | solution.py:223
  413.3 7.0 %collective-permute-done.37 = bf16[192,384]{0,1:T(8,128)(2,1)S(1)} collective-permute-done((bf16[192,384]{0,1:T(8,128)(2,1)S(1)}, bf16[192,384]{0,1:T(8,128)(2,1)S(1)}, u32[]{:S(2)}, u32[]{:S(2)}) %collective-permute-start.37) | collective-permute-done | bytes 147488 | tf_op jit(solution)/shard_map/ppermute | solution.py:223
  425.4 3.4 collective-permute-start.57
  428.9 9.7 %collective-permute-done.57 = f32[8,128]{1,0:T(8,128)S(1)} collective-permute-done((f32[8,128]{1,0:T(8,128)S(1)}, f32[8,128]{1,0:T(8,128)S(1)}, u32[]{:S(2)}, u32[]{:S(2)}) %collective-permute-start.57) | collective-permute-done | bytes 4128 | tf_op jit(solution)/shard_map/ppermute | solution.py:229
  439.3 2.9 collective-permute-done.58
  442.2 3.8 collective-permute-start.59
  457.4 3.1 multiply_add_fusion.1
  (379 shorter events, 114.9 us)
Async XLA Ops:
  2.2 10.5 %collective-permute-start.1 = (bf16[192,384]{0,1:T(8,128)(2,1)S(1)}, bf16[192,384]{0,1:T(8,128)(2,1)S(1)}, u32[]{:S(2)}, u32[]{:S(2)}) collective-permute-start(bf16[192,384]{0,1:T(8,128)(2,1)S(1)} %maximum_select_fusion.2), channel_id=1, source_target_pairs={{0,3},{1,0},{2,1},{3,2},{4,7},{5,4},{6,5},{7,6},{8,11},{9,8},{10,9... | collective-permute-start | bytes 442376 | tf_op jit(solution)/shard_map/ppermute | solution.py:223
  7.3 16.7 %collective-permute-start.2 = (bf16[192,384]{0,1:T(8,128)(2,1)S(1)}, bf16[192,384]{0,1:T(8,128)(2,1)S(1)}, u32[]{:S(2)}, u32[]{:S(2)}) collective-permute-start(bf16[192,384]{0,1:T(8,128)(2,1)S(1)} %maximum_select_fusion.2), channel_id=1, source_target_pairs={{0,2},{1,3},{2,0},{3,1},{4,6},{5,7},{6,4},{7,5},{8,10},{9,11},{10,... | collective-permute-start | bytes 442376 | tf_op jit(solution)/shard_map/ppermute | solution.py:223
  7.3 16.7 %collective-permute-start.3 = (bf16[192,384]{0,1:T(8,128)(2,1)S(1)}, bf16[192,384]{0,1:T(8,128)(2,1)S(1)}, u32[]{:S(2)}, u32[]{:S(2)}) collective-permute-start(bf16[192,384]{0,1:T(8,128)(2,1)S(1)} %maximum_select_fusion.2), channel_id=1, source_target_pairs={{0,1},{1,2},{2,3},{3,0},{4,5},{5,6},{6,7},{7,4},{8,9},{9,10},{10,1... | collective-permute-start | bytes 442376 | tf_op jit(solution)/shard_map/ppermute | solution.py:223
  24.3 16.2 %collective-permute-start.4 = (bf16[768,384]{0,1:T(8,128)(2,1)S(1)}, bf16[768,384]{0,1:T(8,128)(2,1)S(1)}, u32[]{:S(2)}, u32[]{:S(2)}) collective-permute-start(bf16[768,384]{0,1:T(8,128)(2,1)S(1)} %pad_maximum_fusion.12), channel_id=1, source_target_pairs={{0,4},{4,0},{8,12},{12,8},{16,24},{20,28},{24,16},{28,20},{1,5},{5... | collective-permute-start | bytes 1769480 | tf_op jit(solution)/shard_map/ppermute | solution.py:214
  25.8 16.8 %collective-permute-start.6 = (bf16[768,384]{0,1:T(8,128)(2,1)S(1)}, bf16[768,384]{0,1:T(8,128)(2,1)S(1)}, u32[]{:S(2)}, u32[]{:S(2)}) collective-permute-start(bf16[768,384]{0,1:T(8,128)(2,1)S(1)} %pad_maximum_fusion.12), channel_id=1, source_target_pairs={{0,8},{4,12},{8,0},{12,4},{16,20},{20,16},{24,28},{28,24},{1,9},{5... | collective-permute-start | bytes 1769480 | tf_op jit(solution)/shard_map/ppermute | solution.py:217
  40.5 9.9 %collective-permute-start.5 = (bf16[768,384]{0,1:T(8,128)(2,1)S(1)}, bf16[768,384]{0,1:T(8,128)(2,1)S(1)}, u32[]{:S(2)}, u32[]{:S(2)}) collective-permute-start(bf16[768,384]{0,1:T(8,128)(2,1)S(1)} %collective-permute-done.4), channel_id=1, source_target_pairs={{0,8},{4,12},{8,0},{12,4},{16,20},{20,16},{24,28},{28,24},{1,9},{5... | collective-permute-start | bytes 1769480 | tf_op jit(solution)/shard_map/ppermute | solution.py:217
  40.6 10.1 %collective-permute-start = (bf16[512,768]{1,0:T(8,128)(2,1)}, bf16[512,768]{1,0:T(8,128)(2,1)S(1)}, u32[]{:S(2)}, u32[]{:S(2)}) collective-permute-start(bf16[512,768]{1,0:T(8,128)(2,1)} %param.22), channel_id=1, source_target_pairs={{0,0},{4,16},{8,8},{12,24},{16,4},{20,20},{24,12},{28,28},{1,1},{5... | collective-permute-start | bytes 2359304 | tf_op jit(solution)/shard_map/ppermute | solution.py:211
  50.5 40.1 %collective-permute-start.7 = (bf16[2,768,384]{1,2,0:T(8,128)(2,1)S(1)}, bf16[2,768,384]{1,2,0:T(8,128)(2,1)}, u32[]{:S(2)}, u32[]{:S(2)}) collective-permute-start(bf16[2,768,384]{1,2,0:T(8,128)(2,1)S(1)} %fusion.30), channel_id=1, source_target_pairs={{0,16},{16,0},{1,17},{17,1},{2,18},{18,2},{3,19},{19,3},{4,20},{20... | collective-permute-start | bytes 3538952 | tf_op jit(solution)/shard_map/ppermute | solution.py:220
  52.3 38.4 %collective-permute-start.8 = (bf16[512,768]{1,0:T(8,128)(2,1)}, bf16[512,768]{1,0:T(8,128)(2,1)}, u32[]{:S(2)}, u32[]{:S(2)}) collective-permute-start(bf16[512,768]{1,0:T(8,128)(2,1)} %fusion.56), channel_id=1, source_target_pairs={{0,16},{16,0},{1,17},{17,1},{2,18},{18,2},{3,19},{19,3},{4,20},{20... | collective-permute-start | bytes 2359304 | tf_op jit(solution)/shard_map/ppermute | solution.py:220
  59.8 8.5 %collective-permute-start.11 = (bf16[192,512]{0,1:T(8,128)(2,1)}, bf16[192,512]{0,1:T(8,128)(2,1)}, u32[]{:S(2)}, u32[]{:S(2)}) collective-permute-start(bf16[192,512]{0,1:T(8,128)(2,1)} %pad_maximum_fusion.14), channel_id=1, source_target_pairs={{0,3},{1,0},{2,1},{3,2},{4,7},{5,4},{6,5},{7,6},{8,11},{9,8},{10,9... | collective-permute-start | bytes 589832 | tf_op jit(solution)/shard_map/ppermute | solution.py:223
  59.8 26.4 %collective-permute-start.12 = (bf16[192,512]{0,1:T(8,128)(2,1)}, bf16[192,512]{0,1:T(8,128)(2,1)S(1)}, u32[]{:S(2)}, u32[]{:S(2)}) collective-permute-start(bf16[192,512]{0,1:T(8,128)(2,1)} %pad_maximum_fusion.14), channel_id=1, source_target_pairs={{0,2},{1,3},{2,0},{3,1},{4,6},{5,7},{6,4},{7,5},{8,10},{9,11},{10,... | collective-permute-start | bytes 589832 | tf_op jit(solution)/shard_map/ppermute | solution.py:223
  62.6 0.8 collective-permute-start.9
  63.5 22.7 %collective-permute-start.13 = (bf16[192,512]{0,1:T(8,128)(2,1)}, bf16[192,512]{0,1:T(8,128)(2,1)S(1)}, u32[]{:S(2)}, u32[]{:S(2)}) collective-permute-start(bf16[192,512]{0,1:T(8,128)(2,1)} %pad_maximum_fusion.14), channel_id=1, source_target_pairs={{0,1},{1,2},{2,3},{3,0},{4,5},{5,6},{6,7},{7,4},{8,9},{9,10},{10,1... | collective-permute-start | bytes 589832 | tf_op jit(solution)/shard_map/ppermute | solution.py:223
  88.5 60.2 %collective-permute-start.14 = (bf16[768,512]{0,1:T(8,128)(2,1)}, bf16[768,512]{0,1:T(8,128)(2,1)}, u32[]{:S(2)}, u32[]{:S(2)}) collective-permute-start(bf16[768,512]{0,1:T(8,128)(2,1)} %pad_maximum_fusion.11), channel_id=1, source_target_pairs={{0,4},{4,0},{8,12},{12,8},{16,24},{20,28},{24,16},{28,20},{1,5},{5... | collective-permute-start | bytes 2359304 | tf_op jit(solution)/shard_map/ppermute | solution.py:214
  147.2 2.5 collective-permute-start.10
  147.4 25.4 %collective-permute-start.15 = (bf16[768,512]{0,1:T(8,128)(2,1)}, bf16[768,512]{0,1:T(8,128)(2,1)S(1)}, u32[]{:S(2)}, u32[]{:S(2)}) collective-permute-start(bf16[768,512]{0,1:T(8,128)(2,1)} %pad_maximum_fusion.11), channel_id=1, source_target_pairs={{0,8},{4,12},{8,0},{12,4},{16,20},{20,16},{24,28},{28,24},{1,9},{5... | collective-permute-start | bytes 2359304 | tf_op jit(solution)/shard_map/ppermute | solution.py:217
  148.7 26.1 %collective-permute-start.16 = (bf16[768,512]{0,1:T(8,128)(2,1)}, bf16[768,512]{0,1:T(8,128)(2,1)S(1)}, u32[]{:S(2)}, u32[]{:S(2)}) collective-permute-start(bf16[768,512]{0,1:T(8,128)(2,1)} %collective-permute-done.14), channel_id=1, source_target_pairs={{0,8},{4,12},{8,0},{12,4},{16,20},{20,16},{24,28},{28,24},{1,9},{5... | collective-permute-start | bytes 2359304 | tf_op jit(solution)/shard_map/ppermute | solution.py:217
  152.6 22.2 %collective-permute-start.17 = (bf16[512,768]{1,0:T(8,128)(2,1)S(1)}, bf16[512,768]{1,0:T(8,128)(2,1)S(1)}, u32[]{:S(2)}, u32[]{:S(2)}) collective-permute-start(bf16[512,768]{1,0:T(8,128)(2,1)S(1)} %multiply_convert_fusion.2), channel_id=1, source_target_pairs={{0,16},{16,0},{1,17},{17,1},{2,18},{18,2},{3,19},{19,3},{4,20},{20... | collective-permute-start | bytes 2359304 | tf_op jit(solution)/shard_map/ppermute | solution.py:220
  153.8 5.8 %collective-permute-start.18 = (bf16[192,256]{1,0:T(8,128)(2,1)S(1)}, bf16[192,256]{1,0:T(8,128)(2,1)S(1)}, u32[]{:S(2)}, u32[]{:S(2)}) collective-permute-start(bf16[192,256]{1,0:T(8,128)(2,1)S(1)} %get-tuple-element.141), channel_id=1, source_target_pairs={{0,4},{4,0},{8,12},{12,8},{16,24},{20,28},{24,16},{28,20},{1,5},{5... | collective-permute-start | bytes 294920 | tf_op jit(solution)/shard_map/ppermute | solution.py:214
  154.6 15.6 %collective-permute-start.19 = (bf16[192,256]{1,0:T(8,128)(2,1)S(1)}, bf16[192,256]{1,0:T(8,128)(2,1)S(1)}, u32[]{:S(2)}, u32[]{:S(2)}) collective-permute-start(bf16[192,256]{1,0:T(8,128)(2,1)S(1)} %get-tuple-element.141), channel_id=1, source_target_pairs={{0,8},{4,12},{8,0},{12,4},{16,20},{20,16},{24,28},{28,24},{1,9},{5... | collective-permute-start | bytes 294920 | tf_op jit(solution)/shard_map/ppermute | solution.py:217
  159.6 11.6 %collective-permute-start.20 = (bf16[192,256]{1,0:T(8,128)(2,1)S(1)}, bf16[192,256]{1,0:T(8,128)(2,1)S(1)}, u32[]{:S(2)}, u32[]{:S(2)}) collective-permute-start(bf16[192,256]{1,0:T(8,128)(2,1)S(1)} %collective-permute-done.18), channel_id=1, source_target_pairs={{0,8},{4,12},{8,0},{12,4},{16,20},{20,16},{24,28},{28,24},{1,9},{5... | collective-permute-start | bytes 294920 | tf_op jit(solution)/shard_map/ppermute | solution.py:217
  171.3 12.6 %collective-permute-start.21 = (bf16[4,192,256]{2,1,0:T(8,128)(2,1)S(1)}, bf16[4,192,256]{2,1,0:T(8,128)(2,1)S(1)}, u32[]{:S(2)}, u32[]{:S(2)}) collective-permute-start(bf16[4,192,256]{2,1,0:T(8,128)(2,1)S(1)} %pad_maximum_fusion.13), channel_id=1, source_target_pairs={{0,3},{1,0},{2,1},{3,2},{4,7},{5,4},{6,5},{7,6},{8,11},{9,8},{10,9... | collective-permute-start | bytes 1179656 | tf_op jit(solution)/shard_map/ppermute | solution.py:223
  171.4 34.2 %collective-permute-start.22 = (bf16[4,192,256]{2,1,0:T(8,128)(2,1)S(1)}, bf16[4,192,256]{2,1,0:T(8,128)(2,1)S(1)}, u32[]{:S(2)}, u32[]{:S(2)}) collective-permute-start(bf16[4,192,256]{2,1,0:T(8,128)(2,1)S(1)} %pad_maximum_fusion.13), channel_id=1, source_target_pairs={{0,2},{1,3},{2,0},{3,1},{4,6},{5,7},{6,4},{7,5},{8,10},{9,11},{10,... | collective-permute-start | bytes 1179656 | tf_op jit(solution)/shard_map/ppermute | solution.py:223
  172.8 32.8 %collective-permute-start.23 = (bf16[4,192,256]{2,1,0:T(8,128)(2,1)S(1)}, bf16[4,192,256]{2,1,0:T(8,128)(2,1)S(1)}, u32[]{:S(2)}, u32[]{:S(2)}) collective-permute-start(bf16[4,192,256]{2,1,0:T(8,128)(2,1)S(1)} %pad_maximum_fusion.13), channel_id=1, source_target_pairs={{0,1},{1,2},{2,3},{3,0},{4,5},{5,6},{6,7},{7,4},{8,9},{9,10},{10,1... | collective-permute-start | bytes 1179656 | tf_op jit(solution)/shard_map/ppermute | solution.py:223
  209.5 2.7 collective-permute-start.24
  209.6 6.0 %collective-permute-start.26 = (bf16[512,768]{1,0:T(8,128)(2,1)}, bf16[512,768]{1,0:T(8,128)(2,1)S(1)}, u32[]{:S(2)}, u32[]{:S(2)}) collective-permute-start(bf16[512,768]{1,0:T(8,128)(2,1)} %param.23), channel_id=1, source_target_pairs={{0,0},{4,16},{8,8},{12,24},{16,4},{20,20},{24,12},{28,28},{1,1},{5... | collective-permute-start | bytes 2359304 | tf_op jit(solution)/shard_map/ppermute | solution.py:211
  218.4 27.6 %collective-permute-start.27 = (bf16[512,768]{1,0:T(8,128)(2,1)}, bf16[512,768]{1,0:T(8,128)(2,1)}, u32[]{:S(2)}, u32[]{:S(2)}) collective-permute-start(bf16[512,768]{1,0:T(8,128)(2,1)} %get-tuple-element.104), channel_id=1, source_target_pairs={{0,16},{16,0},{1,17},{17,1},{2,18},{18,2},{3,19},{19,3},{4,20},{20... | collective-permute-start | bytes 2359304 | tf_op jit(solution)/shard_map/ppermute | solution.py:220
  238.4 115.6 %collective-permute-start.25 = (bf16[512,768]{1,0:T(8,128)(2,1)}, bf16[512,768]{1,0:T(8,128)(2,1)}, u32[]{:S(2)}, u32[]{:S(2)}) collective-permute-start(bf16[512,768]{1,0:T(8,128)(2,1)} %fusion.55), channel_id=1, source_target_pairs={{0,0},{4,16},{8,8},{12,24},{16,4},{20,20},{24,12},{28,28},{1,1},{5... | collective-permute-start | bytes 2359304 | tf_op jit(solution)/shard_map/ppermute | solution.py:211
  256.0 45.5 %collective-permute-start.28 = (bf16[512,768]{1,0:T(8,128)(2,1)S(1)}, bf16[512,768]{1,0:T(8,128)(2,1)S(1)}, u32[]{:S(2)}, u32[]{:S(2)}) collective-permute-start(bf16[512,768]{1,0:T(8,128)(2,1)S(1)} %bitcast_convert_fusion), channel_id=1, source_target_pairs={{0,16},{16,0},{1,17},{17,1},{2,18},{18,2},{3,19},{19,3},{4,20},{20... | collective-permute-start | bytes 2359304 | tf_op jit(solution)/shard_map/ppermute | solution.py:220
  259.8 16.7 %collective-permute-start.45 = (bf16[4,192,256]{1,2,0:T(8,128)(2,1)S(1)}, bf16[4,192,256]{1,2,0:T(8,128)(2,1)S(1)}, u32[]{:S(2)}, u32[]{:S(2)}) collective-permute-start(bf16[4,192,256]{1,2,0:T(8,128)(2,1)S(1)} %get-tuple-element.106), channel_id=1, source_target_pairs={{0,1},{1,2},{2,3},{3,0},{4,5},{5,6},{6,7},{7,4},{8,9},{9,10},{10,1... | collective-permute-start | bytes 1179656 | tf_op jit(solution)/shard_map/ppermute | solution.py:223
  260.8 37.7 %collective-permute-start.46 = (bf16[4,192,256]{1,2,0:T(8,128)(2,1)S(1)}, bf16[4,192,256]{1,2,0:T(8,128)(2,1)S(1)}, u32[]{:S(2)}, u32[]{:S(2)}) collective-permute-start(bf16[4,192,256]{1,2,0:T(8,128)(2,1)S(1)} %get-tuple-element.108), channel_id=1, source_target_pairs={{0,2},{1,3},{2,0},{3,1},{4,6},{5,7},{6,4},{7,5},{8,10},{9,11},{10,... | collective-permute-start | bytes 1179656 | tf_op jit(solution)/shard_map/ppermute | solution.py:223
  262.8 37.2 %collective-permute-start.47 = (bf16[4,192,256]{1,2,0:T(8,128)(2,1)S(1)}, bf16[4,192,256]{1,2,0:T(8,128)(2,1)S(1)}, u32[]{:S(2)}, u32[]{:S(2)}) collective-permute-start(bf16[4,192,256]{1,2,0:T(8,128)(2,1)S(1)} %get-tuple-element.107), channel_id=1, source_target_pairs={{0,3},{1,0},{2,1},{3,2},{4,7},{5,4},{6,5},{7,6},{8,11},{9,8},{10,9... | collective-permute-start | bytes 1179656 | tf_op jit(solution)/shard_map/ppermute | solution.py:223
  276.5 37.3 %collective-permute-start.39 = (bf16[768,512]{1,0:T(8,128)(2,1)S(1)}, bf16[768,512]{1,0:T(8,128)(2,1)S(1)}, u32[]{:S(2)}, u32[]{:S(2)}) collective-permute-start(bf16[768,512]{1,0:T(8,128)(2,1)S(1)} %convolution_convert_fusion.5), channel_id=1, source_target_pairs={{0,8},{4,12},{8,0},{12,4},{16,20},{20,16},{24,28},{28,24},{1,9},{5... | collective-permute-start | bytes 2359304 | tf_op jit(solution)/shard_map/ppermute | solution.py:217
  298.5 76.0 %collective-permute-start.41 = (bf16[768,512]{1,0:T(8,128)(2,1)}, bf16[768,512]{1,0:T(8,128)(2,1)}, u32[]{:S(2)}, u32[]{:S(2)}) collective-permute-start(bf16[768,512]{1,0:T(8,128)(2,1)} %convolution_convert_fusion.4), channel_id=1, source_target_pairs={{0,8},{4,12},{8,0},{12,4},{16,20},{20,16},{24,28},{28,24},{1,9},{5... | collective-permute-start | bytes 2359304 | tf_op jit(solution)/shard_map/ppermute | solution.py:217
  300.9 11.2 %collective-permute-start.48 = (bf16[192,256]{0,1:T(8,128)(2,1)S(1)}, bf16[192,256]{0,1:T(8,128)(2,1)S(1)}, u32[]{:S(2)}, u32[]{:S(2)}) collective-permute-start(bf16[192,256]{0,1:T(8,128)(2,1)S(1)} %get-tuple-element.128), channel_id=1, source_target_pairs={{0,8},{4,12},{8,0},{12,4},{16,20},{20,16},{24,28},{28,24},{1,9},{5... | collective-permute-start | bytes 294920 | tf_op jit(solution)/shard_map/ppermute | solution.py:217
  305.6 6.6 %collective-permute-start.51 = (f32[2,768]{1,0:T(2,128)S(1)}, f32[2,768]{1,0:T(2,128)S(1)}, u32[]{:S(2)}, u32[]{:S(2)}) collective-permute-start(f32[2,768]{1,0:T(2,128)S(1)} %fusion.71), channel_id=1, source_target_pairs={{0,16},{16,0},{1,17},{17,1},{2,18},{18,2},{3,19},{19,3},{4,20},{20... | collective-permute-start | bytes 18440 | tf_op jit(solution)/shard_map/ppermute | solution.py:229
  312.1 6.1 %collective-permute-start.29 = (bf16[512,768]{1,0:T(8,128)(2,1)S(1)}, bf16[512,768]{1,0:T(8,128)(2,1)S(1)}, u32[]{:S(2)}, u32[]{:S(2)}) collective-permute-start(bf16[512,768]{1,0:T(8,128)(2,1)S(1)} %fusion.90), channel_id=1, source_target_pairs={{0,16},{16,0},{1,17},{17,1},{2,18},{18,2},{3,19},{19,3},{4,20},{20... | collective-permute-start | bytes 2359304 | tf_op jit(solution)/shard_map/ppermute | solution.py:220
  312.2 38.2 %collective-permute-start.50 = (bf16[192,256]{0,1:T(8,128)(2,1)}, bf16[192,256]{0,1:T(8,128)(2,1)S(1)}, u32[]{:S(2)}, u32[]{:S(2)}) collective-permute-start(bf16[192,256]{0,1:T(8,128)(2,1)} %get-tuple-element.129), channel_id=1, source_target_pairs={{0,8},{4,12},{8,0},{12,4},{16,20},{20,16},{24,28},{28,24},{1,9},{5... | collective-permute-start | bytes 294920 | tf_op jit(solution)/shard_map/ppermute | solution.py:217
  313.8 3.7 collective-permute-start.52
  317.5 33.5 %collective-permute-start.49 = (bf16[192,256]{0,1:T(8,128)(2,1)S(1)}, bf16[192,256]{0,1:T(8,128)(2,1)}, u32[]{:S(2)}, u32[]{:S(2)}) collective-permute-start(bf16[192,256]{0,1:T(8,128)(2,1)S(1)} %fusion.64), channel_id=1, source_target_pairs={{0,4},{4,0},{8,12},{12,8},{16,24},{20,28},{24,16},{28,20},{1,5},{5... | collective-permute-start | bytes 294920 | tf_op jit(solution)/shard_map/ppermute | solution.py:214
  318.2 56.3 %collective-permute-start.40 = (bf16[768,512]{1,0:T(8,128)(2,1)}, bf16[768,512]{1,0:T(8,128)(2,1)}, u32[]{:S(2)}, u32[]{:S(2)}) collective-permute-start(bf16[768,512]{1,0:T(8,128)(2,1)} %add_convert_fusion.2), channel_id=1, source_target_pairs={{0,4},{4,0},{8,12},{12,8},{16,24},{20,28},{24,16},{28,20},{1,5},{5... | collective-permute-start | bytes 2359304 | tf_op jit(solution)/shard_map/ppermute | solution.py:214
  350.4 3.6 collective-permute-start.53
  351.1 25.2 %collective-permute-start.32 = (bf16[2,768,384]{1,2,0:T(8,128)(2,1)}, bf16[2,768,384]{1,2,0:T(8,128)(2,1)}, u32[]{:S(2)}, u32[]{:S(2)}) collective-permute-start(bf16[2,768,384]{1,2,0:T(8,128)(2,1)} %get-tuple-element.103), channel_id=1, source_target_pairs={{0,16},{16,0},{1,17},{17,1},{2,18},{18,2},{3,19},{19,3},{4,20},{20... | collective-permute-start | bytes 3538952 | tf_op jit(solution)/shard_map/ppermute | solution.py:220
  354.0 17.0 %collective-permute-start.63 = (bf16[192,256]{0,1:T(8,128)(2,1)S(1)}, bf16[192,256]{0,1:T(8,128)(2,1)S(1)}, u32[]{:S(2)}, u32[]{:S(2)}) collective-permute-start(bf16[192,256]{0,1:T(8,128)(2,1)S(1)} %get-tuple-element.86), channel_id=1, source_target_pairs={{0,16},{16,0},{1,17},{17,1},{2,18},{18,2},{3,19},{19,3},{4,20},{20... | collective-permute-start | bytes 294920 | tf_op jit(solution)/shard_map/ppermute | solution.py:220
  354.1 13.6 %collective-permute-start.54 = (f32[2,768]{1,0:T(2,128)S(1)}, f32[2,768]{1,0:T(2,128)S(1)}, u32[]{:S(2)}, u32[]{:S(2)}) collective-permute-start(f32[2,768]{1,0:T(2,128)S(1)} %add.282), channel_id=1, source_target_pairs={{0,1},{1,0},{2,3},{3,2},{4,5},{5,4},{6,7},{7,6},{8,9},{9,8},{10,11... | collective-permute-start | bytes 18440 | tf_op jit(solution)/shard_map/ppermute | solution.py:229
  367.6 5.1 %collective-permute-start.55 = (f32[2,768]{1,0:T(2,128)S(1)}, f32[2,768]{1,0:T(2,128)S(1)}, u32[]{:S(2)}, u32[]{:S(2)}) collective-permute-start(f32[2,768]{1,0:T(2,128)S(1)} %add.283), channel_id=1, source_target_pairs={{0,2},{1,3},{2,0},{3,1},{4,6},{5,7},{6,4},{7,5},{8,10},{9,11},{10,... | collective-permute-start | bytes 18440 | tf_op jit(solution)/shard_map/ppermute | solution.py:229
  377.8 9.9 %collective-permute-start.33 = (bf16[768,384]{0,1:T(8,128)(2,1)S(1)}, bf16[768,384]{0,1:T(8,128)(2,1)S(1)}, u32[]{:S(2)}, u32[]{:S(2)}) collective-permute-start(bf16[768,384]{0,1:T(8,128)(2,1)S(1)} %get-tuple-element.114), channel_id=1, source_target_pairs={{0,8},{4,12},{8,0},{12,4},{16,20},{20,16},{24,28},{28,24},{1,9},{5... | collective-permute-start | bytes 1769480 | tf_op jit(solution)/shard_map/ppermute | solution.py:217
  378.8 11.4 %collective-permute-start.42 = (bf16[192,512]{1,0:T(8,128)(2,1)S(1)}, bf16[192,512]{1,0:T(8,128)(2,1)S(1)}, u32[]{:S(2)}, u32[]{:S(2)}) collective-permute-start(bf16[192,512]{1,0:T(8,128)(2,1)S(1)} %get-tuple-element.119), channel_id=1, source_target_pairs={{0,1},{1,2},{2,3},{3,0},{4,5},{5,6},{6,7},{7,4},{8,9},{9,10},{10,1... | collective-permute-start | bytes 589832 | tf_op jit(solution)/shard_map/ppermute | solution.py:223
  379.0 16.2 %collective-permute-start.43 = (bf16[192,512]{1,0:T(8,128)(2,1)S(1)}, bf16[192,512]{1,0:T(8,128)(2,1)S(1)}, u32[]{:S(2)}, u32[]{:S(2)}) collective-permute-start(bf16[192,512]{1,0:T(8,128)(2,1)S(1)} %get-tuple-element.121), channel_id=1, source_target_pairs={{0,2},{1,3},{2,0},{3,1},{4,6},{5,7},{6,4},{7,5},{8,10},{9,11},{10,... | collective-permute-start | bytes 589832 | tf_op jit(solution)/shard_map/ppermute | solution.py:223
  381.9 13.3 %collective-permute-start.44 = (bf16[192,512]{1,0:T(8,128)(2,1)S(1)}, bf16[192,512]{1,0:T(8,128)(2,1)S(1)}, u32[]{:S(2)}, u32[]{:S(2)}) collective-permute-start(bf16[192,512]{1,0:T(8,128)(2,1)S(1)} %get-tuple-element.120), channel_id=1, source_target_pairs={{0,3},{1,0},{2,1},{3,2},{4,7},{5,4},{6,5},{7,6},{8,11},{9,8},{10,9... | collective-permute-start | bytes 589832 | tf_op jit(solution)/shard_map/ppermute | solution.py:223
  386.2 15.7 %collective-permute-start.35 = (bf16[768,384]{0,1:T(8,128)(2,1)S(1)}, bf16[768,384]{0,1:T(8,128)(2,1)S(1)}, u32[]{:S(2)}, u32[]{:S(2)}) collective-permute-start(bf16[768,384]{0,1:T(8,128)(2,1)S(1)} %get-tuple-element.115), channel_id=1, source_target_pairs={{0,8},{4,12},{8,0},{12,4},{16,20},{20,16},{24,28},{28,24},{1,9},{5... | collective-permute-start | bytes 1769480 | tf_op jit(solution)/shard_map/ppermute | solution.py:217
  388.0 13.9 %collective-permute-start.34 = (bf16[768,384]{0,1:T(8,128)(2,1)S(1)}, bf16[768,384]{0,1:T(8,128)(2,1)S(1)}, u32[]{:S(2)}, u32[]{:S(2)}) collective-permute-start(bf16[768,384]{0,1:T(8,128)(2,1)S(1)} %fusion.31), channel_id=1, source_target_pairs={{0,4},{4,0},{8,12},{12,8},{16,24},{20,28},{24,16},{28,20},{1,5},{5... | collective-permute-start | bytes 1769480 | tf_op jit(solution)/shard_map/ppermute | solution.py:214
  390.2 17.2 %collective-permute-start.30 = (bf16[512,768]{1,0:T(8,128)(2,1)S(1)}, bf16[512,768]{1,0:T(8,128)(2,1)S(1)}, u32[]{:S(2)}, u32[]{:S(2)}) collective-permute-start(bf16[512,768]{1,0:T(8,128)(2,1)S(1)} %fusion.52), channel_id=1, source_target_pairs={{0,16},{16,0},{1,17},{17,1},{2,18},{18,2},{3,19},{19,3},{4,20},{20... | collective-permute-start | bytes 2359304 | tf_op jit(solution)/shard_map/ppermute | solution.py:220
  396.0 32.9 %collective-permute-start.62 = (bf16[192,512]{1,0:T(8,128)(2,1)S(1)}, bf16[192,512]{1,0:T(8,128)(2,1)S(1)}, u32[]{:S(2)}, u32[]{:S(2)}) collective-permute-start(bf16[192,512]{1,0:T(8,128)(2,1)S(1)} %get-tuple-element.88), channel_id=1, source_target_pairs={{0,16},{16,0},{1,17},{17,1},{2,18},{18,2},{3,19},{19,3},{4,20},{20... | collective-permute-start | bytes 589832 | tf_op jit(solution)/shard_map/ppermute | solution.py:220
  403.5 9.8 %collective-permute-start.36 = (bf16[192,384]{0,1:T(8,128)(2,1)S(1)}, bf16[192,384]{0,1:T(8,128)(2,1)S(1)}, u32[]{:S(2)}, u32[]{:S(2)}) collective-permute-start(bf16[192,384]{0,1:T(8,128)(2,1)S(1)} %get-tuple-element.125), channel_id=1, source_target_pairs={{0,1},{1,2},{2,3},{3,0},{4,5},{5,6},{6,7},{7,4},{8,9},{9,10},{10,1... | collective-permute-start | bytes 442376 | tf_op jit(solution)/shard_map/ppermute | solution.py:223
  403.6 16.8 %collective-permute-start.37 = (bf16[192,384]{0,1:T(8,128)(2,1)S(1)}, bf16[192,384]{0,1:T(8,128)(2,1)S(1)}, u32[]{:S(2)}, u32[]{:S(2)}) collective-permute-start(bf16[192,384]{0,1:T(8,128)(2,1)S(1)} %get-tuple-element.127), channel_id=1, source_target_pairs={{0,2},{1,3},{2,0},{3,1},{4,6},{5,7},{6,4},{7,5},{8,10},{9,11},{10,... | collective-permute-start | bytes 442376 | tf_op jit(solution)/shard_map/ppermute | solution.py:223
  404.1 16.2 %collective-permute-start.38 = (bf16[192,384]{0,1:T(8,128)(2,1)S(1)}, bf16[192,384]{0,1:T(8,128)(2,1)S(1)}, u32[]{:S(2)}, u32[]{:S(2)}) collective-permute-start(bf16[192,384]{0,1:T(8,128)(2,1)S(1)} %get-tuple-element.126), channel_id=1, source_target_pairs={{0,3},{1,0},{2,1},{3,2},{4,7},{5,4},{6,5},{7,6},{8,11},{9,8},{10,9... | collective-permute-start | bytes 442376 | tf_op jit(solution)/shard_map/ppermute | solution.py:223
  423.7 1.7 collective-permute-start.56
  424.5 25.4 %collective-permute-start.31 = (bf16[512,768]{1,0:T(8,128)(2,1)S(1)}, bf16[512,768]{1,0:T(8,128)(2,1)S(1)}, u32[]{:S(2)}, u32[]{:S(2)}) collective-permute-start(bf16[512,768]{1,0:T(8,128)(2,1)S(1)} %fusion.53), channel_id=1, source_target_pairs={{0,0},{4,16},{8,8},{12,24},{16,4},{20,20},{24,12},{28,28},{1,1},{5... | collective-permute-start | bytes 2359304 | tf_op jit(solution)/shard_map/ppermute | solution.py:211
  425.4 13.1 %collective-permute-start.57 = (f32[8,128]{1,0:T(8,128)S(1)}, f32[8,128]{1,0:T(8,128)S(1)}, u32[]{:S(2)}, u32[]{:S(2)}) collective-permute-start(f32[8,128]{1,0:T(8,128)S(1)} %broadcast_add_fusion), channel_id=1, source_target_pairs={{0,4},{4,0},{8,12},{12,8},{1,5},{5,1},{9,13},{13,9},{2,6},{6,2},{1... | collective-permute-start | bytes 12296 | tf_op jit(solution)/shard_map/ppermute | solution.py:229
  438.6 3.6 collective-permute-start.58
  442.2 5.4 %collective-permute-start.59 = (f32[8,128]{1,0:T(8,128)S(1)}, f32[8,128]{1,0:T(8,128)S(1)}, u32[]{:S(2)}, u32[]{:S(2)}) collective-permute-start(f32[8,128]{1,0:T(8,128)S(1)} %add.288), channel_id=1, source_target_pairs={{0,1},{1,0},{2,3},{3,2},{4,5},{5,4},{6,7},{7,6},{8,9},{9,8},{10,11... | collective-permute-start | bytes 12296 | tf_op jit(solution)/shard_map/ppermute | solution.py:229
  447.6 4.5 collective-permute-start.60
  451.2 10.0 %collective-permute-start.61 = (bf16[192,384]{0,1:T(8,128)(2,1)}, bf16[192,384]{0,1:T(8,128)(2,1)}, u32[]{:S(2)}, u32[]{:S(2)}) collective-permute-start(bf16[192,384]{0,1:T(8,128)(2,1)} %get-tuple-element.90), channel_id=1, source_target_pairs={{0,16},{16,0},{1,17},{17,1},{2,18},{18,2},{3,19},{19,3},{4,20},{20... | collective-permute-start | bytes 442376 | tf_op jit(solution)/shard_map/ppermute | solution.py:220
  (92 other events, 1125.2 us)

commit v2 on v1

v2 whole, which is shorter than its diff:
```python
import functools

import jax
import jax.numpy as jnp
import numpy as np
from jax import lax
from jax.experimental import pallas as pl
from jax.experimental.pallas import tpu as pltpu
from jax.sharding import PartitionSpec as P

HD = 64
LEN = 1024

EPSILON = 1e-06
THETA = 10000.0
MOMENTUM = 0.9
RATE = 300.0
DECAY = 0.6
CLIP = 1.0
NEGATIVE = -1e30

F32 = jnp.float32
BF16 = jnp.bfloat16
NT = (((1,), (1,)), ((), ()))
NN = (((1,), (0,)), ((), ()))
TN = (((0,), (0,)), ((), ()))
BQ = 256


def rope_tables():
    half = HD // 2
    freqs = np.float32(THETA) ** (-(np.arange(half, dtype=np.float32) * np.float32(2.0)) / np.float32(HD))
    angles = np.arange(LEN, dtype=np.float32)[:, None] * freqs[None, :].astype(np.float32)
    return np.cos(angles), np.sin(angles)


def pair_tables():
    cosine, sine = rope_tables()
    return (
        jnp.asarray(np.concatenate([cosine] * 4, 1)),
        jnp.asarray(np.concatenate([-sine, sine] * 2, 1)),
    )


def mxu(lhs, rhs, dims=NN):
    return lax.dot_general(lhs, rhs, dims, preferred_element_type=F32)


def fence(*values):
    return lax.optimization_barrier(values)


def params(mib):
    return pltpu.CompilerParams(vmem_limit_bytes=mib << 20)


def cost(flops, bytes_moved, exps=0):
    return pl.CostEstimate(flops=int(flops), bytes_accessed=int(bytes_moved), transcendentals=int(exps))


def out(*shape, dtype=BF16):
    return jax.ShapeDtypeStruct(shape, dtype)


VMEM = pl.BlockSpec(memory_space=pltpu.VMEM)
SMEM = pl.BlockSpec(memory_space=pltpu.SMEM)


def pieces_ad_kernel(s_ref, qkv_ref, out_ref, down_ref, a_ref, d_ref):
    core = s_ref[0]
    n = qkv_ref.shape[2]

    @pl.when(core == 0)
    def _():
        a_ref[:, :n] = qkv_ref[0].astype(BF16)
        a_ref[:, n:] = qkv_ref[1].astype(BF16)

    @pl.when(core == 1)
    def _():
        a_ref[:, :n] = qkv_ref[2].astype(BF16)
        a_ref[:, n:] = out_ref[...].T.astype(BF16)

    half = d_ref.shape[1]
    d_ref[...] = down_ref[pl.ds(pl.multiple_of(core * half, half), half), :].T.astype(BF16)


def pieces_g_kernel(s_ref, gu_ref, g_ref):
    half = g_ref.shape[1] // 2
    at = pl.ds(pl.multiple_of(s_ref[0] * half, half), half)
    g_ref[:, :half] = gu_ref[0, :, at].astype(BF16)
    g_ref[:, half:] = gu_ref[1, :, at].astype(BF16)


def causal(scores_t, block):
    keys = scores_t.shape[0]
    row = lax.broadcasted_iota(jnp.int32, (block, block), 0)
    column = lax.broadcasted_iota(jnp.int32, (block, block), 1)
    tail = jnp.where(row <= column, scores_t[keys - block :], NEGATIVE)
    return tail if keys == block else jnp.concatenate([scores_t[: keys - block], tail], 0)


def swap_halves(t):
    lane = lax.broadcasted_iota(jnp.int32, (1, t.shape[1]), 1)
    return jnp.where(lane % HD < HD // 2, pltpu.roll(t, t.shape[1] - HD // 2, 1), pltpu.roll(t, HD // 2, 1))


def pick_weights(core, j, a0_ref, a1_ref, a3_ref, got_ref, qk_ref, vo_ref):
    @pl.when(core == 0)
    def _():
        vo_ref[...] = got_ref[0]

        @pl.when(j == 0)
        def _():
            qk_ref[...] = a0_ref[...]

        @pl.when(j == 1)
        def _():
            qk_ref[...] = a1_ref[...]

    @pl.when(core == 1)
    def _():
        qk_ref[...] = got_ref[0]

        @pl.when(j == 0)
        def _():
            vo_ref[...] = a1_ref[...]

        @pl.when(j == 1)
        def _():
            vo_ref[...] = a3_ref[...]


def attend_forward_kernel(
    s_ref, x0_ref, x1_ref, a0_ref, a1_ref, a3_ref, got_ref, cos_ref, sin_ref,
    q_ref, k_ref, v_ref, o_ref, ot_ref, lse_ref, xt_ref, far_ref, near_ref,
    qk_w, vo_w, total_ref,
):
    core, live = s_ref[0], s_ref[1]
    j = pl.program_id(0)
    length = q_ref.shape[1]
    tokens = x0_ref.shape[0]
    n = 3 * HD
    pick_weights(core, j, a0_ref, a1_ref, a3_ref, got_ref, qk_w, vo_w)
    lane = lax.broadcasted_iota(jnp.int32, (tokens, HD), 1)
    one = jnp.where(lane == 0, 1.0, 0.0).astype(BF16)
    for x_ref, which in ((x0_ref, core), (x1_ref, 1 - core)):
        start = pl.multiple_of(which * tokens, tokens)
        at = pl.ds(start, tokens)
        qk = mxu(x_ref[...], qk_w[...])
        cos = jnp.concatenate([cos_ref[at, :]] * 3, 1)
        sin = jnp.concatenate([sin_ref[at, :]] * 3, 1)
        qk = qk * cos + swap_halves(qk) * sin
        q = (qk[:, :n] * (HD ** -0.5)).astype(BF16)
        k = qk[:, n:].astype(BF16)
        v = mxu(x_ref[...], vo_w[:, :n]).astype(BF16)
        key = start + lax.broadcasted_iota(jnp.int32, (tokens, HD), 0)
        bias = jnp.where((lane == 0) & (key >= live), NEGATIVE, 0.0).astype(BF16)
        for head in range(3):
            lanes = slice(head * HD, (head + 1) * HD)
            q_ref[head, at, :] = jnp.concatenate([q[:, lanes], one], 1)
            k_ref[head, at, :] = jnp.concatenate([k[:, lanes], bias], 1)
            v_ref[head, at, :] = jnp.concatenate([v[:, lanes], one], 1)

        @pl.when(j == 0)
        def _():
            xt_ref[:, at] = x_ref[...].T

    for block in range(length // BQ):
        keys = (block + 1) * BQ
        span = slice(block * BQ, keys)
        parts = []
        for head in range(3):
            scores = causal(mxu(k_ref[head, :keys, :], q_ref[head, span, :], NT), BQ)
            top = jnp.max(scores, 0, keepdims=True)
            probs = jnp.exp(scores - top).astype(BF16)
            o = mxu(v_ref[head, :keys, :], probs, TN)
            total = o[HD : HD + 1]
            parts.append(o[:HD] / total)
            lse_ref[0, head : head + 1, span] = top + jnp.log(total)
        o = jnp.concatenate(parts, 0)
        ot_ref[0, :, span] = o.astype(BF16)
        o_ref[0, span, :] = o.T.astype(BF16)
    part = mxu(o_ref[0], vo_w[:, n:], NT)

    @pl.when(j == 0)
    def _():
        total_ref[...] = part

    @pl.when(j == 1)
    def _():
        total_ref[...] += part
        near_ref[...] = total_ref[pl.ds(pl.multiple_of(core * tokens, tokens), tokens), :]
        far_ref[...] = total_ref[pl.ds(pl.multiple_of((1 - core) * tokens, tokens), tokens), :].astype(BF16)


def attend_forward(scalars, x_own, x_other, slots, got, cos, sin):
    tokens, width = x_own.shape
    wide = slots[0].shape[1]
    n = wide // 2
    whole = lambda *shape: pl.BlockSpec(shape, lambda j: (0,) * len(shape))
    by_j = lambda *shape: pl.BlockSpec(shape, lambda j: (j,) + (0,) * (len(shape) - 1))
    return pl.pallas_call(
        attend_forward_kernel,
        grid=(2,),
        in_specs=[SMEM]
        + [whole(tokens, width)] * 2
        + [whole(width, wide)] * 3
        + [by_j(1, width, wide), whole(LEN, 128), whole(LEN, 128)],
        out_specs=[by_j(3, LEN, 128)] * 3
        + [by_j(1, LEN, n), by_j(1, n, LEN), by_j(1, 8, LEN), whole(width, LEN)]
        + [whole(tokens, width)] * 2,
        out_shape=[out(6, LEN, 128)] * 3
        + [out(2, LEN, n), out(2, n, LEN), out(2, 8, LEN, dtype=F32), out(width, LEN)]
        + [out(tokens, width), out(tokens, width, dtype=F32)],
        scratch_shapes=[
            pltpu.VMEM((width, wide), BF16),
            pltpu.VMEM((width, wide), BF16),
            pltpu.VMEM((LEN, width), F32),
        ],
        compiler_params=params(44),
        cost_estimate=cost(8e9, 12e6, 4e6),
        name="attend_forward",
    )(scalars, x_own, x_other, slots[0], slots[1], slots[3], got, cos, sin)


def attend_backward_kernel(
    s_ref, d0_ref, d1_ref, a0_ref, a1_ref, a3_ref, got_ref, cos_ref, sin_ref,
    q_ref, k_ref, v_ref, ot_ref, lse_ref,
    dqk_ref, dv_ref, dt_ref,
    qk_w, vo_w, do_ref, dk_acc, dv_acc,
):
    core = s_ref[0]
    j = pl.program_id(0)
    length = q_ref.shape[1]
    tokens = d0_ref.shape[0]
    n = 3 * HD
    pick_weights(core, j, a0_ref, a1_ref, a3_ref, got_ref, qk_w, vo_w)
    for d_ref, which in ((d0_ref, core), (d1_ref, 1 - core)):
        at = pl.ds(pl.multiple_of(which * tokens, tokens), tokens)
        do_ref[at, :] = mxu(d_ref[...], vo_w[:, n:]).astype(BF16)

        @pl.when(j == 0)
        def _():
            dt_ref[:, at] = d_ref[...].T

    products = do_ref[...].astype(F32).T * ot_ref[0].astype(F32)

    def unrotate(t):
        return t * cos_ref[...] - swap_halves(t) * sin_ref[...]

    for head in range(3):
        lanes = slice(head * HD, (head + 1) * HD)
        delta = jnp.sum(products[lanes], 0, keepdims=True)
        dq_parts = []
        for block in range(length // BQ):
            keys = (block + 1) * BQ
            span = slice(block * BQ, keys)
            before = keys - BQ
            q = q_ref[head, span, :]
            scores = causal(mxu(k_ref[head, :keys, :], q, NT), BQ)
            probs = jnp.exp(scores - lse_ref[0, head : head + 1, span])
            d_out = do_ref[span, lanes]
            d_probs = mxu(v_ref[head, :keys, :HD], d_out, NT)
            d_scores = (probs * (d_probs - delta[:, span])).astype(BF16)
            dv_part = mxu(probs.astype(BF16), d_out)
            dk_part = mxu(d_scores, q)
            if block:
                dv_acc[:before, :] += dv_part[:before]
                dk_acc[:before, :] += dk_part[:before]
            dv_acc[before:keys, :] = dv_part[before:]
            dk_acc[before:keys, :] = dk_part[before:]
            dq_parts.append(mxu(d_scores, k_ref[head, :keys, :], TN))
        dq = jnp.concatenate(dq_parts, 0) * (HD ** -0.5)
        dqk_ref[0, :, head * HD : (head + 1) * HD] = unrotate(dq)[:, :HD].astype(BF16)
        dqk_ref[0, :, n + head * HD : n + (head + 1) * HD] = unrotate(dk_acc[...])[:, :HD].astype(BF16)
        dv_ref[0, :, lanes] = dv_acc[...].astype(BF16)


def attend_backward(scalars, d_own, d_other, slots, got, cos, sin, q, k, v, out_t, lse):
    tokens, width = d_own.shape
    wide = slots[0].shape[1]
    n = wide // 2
    whole = lambda *shape: pl.BlockSpec(shape, lambda j: (0,) * len(shape))
    by_j = lambda *shape: pl.BlockSpec(shape, lambda j: (j,) + (0,) * (len(shape) - 1))
    return pl.pallas_call(
        attend_backward_kernel,
        grid=(2,),
        in_specs=[SMEM]
        + [whole(tokens, width)] * 2
        + [whole(width, wide)] * 3
        + [by_j(1, width, wide), whole(LEN, 128), whole(LEN, 128)]
        + [by_j(3, LEN, 128)] * 3
        + [by_j(1, n, LEN), by_j(1, 8, LEN)],
        out_specs=[by_j(1, LEN, wide), by_j(1, LEN, n), whole(width, LEN)],
        out_shape=[out(2, LEN, wide), out(2, LEN, n), out(width, LEN)],
        scratch_shapes=[
            pltpu.VMEM((width, wide), BF16),
            pltpu.VMEM((width, wide), BF16),
            pltpu.VMEM((LEN, n), BF16),
            pltpu.VMEM((LEN, 128), F32),
            pltpu.VMEM((LEN, HD), F32),
        ],
        compiler_params=params(44),
        cost_estimate=cost(12e9, 14e6, 4e6),
        name="attend_backward",
    )(scalars, d_own, d_other, slots[0], slots[1], slots[3], got, cos, sin, q, k, v, out_t, lse)


def grads_a_kernel(s_ref, xt_ref, dt_ref, dqk_ref, dv_ref, o_ref, mine_ref, send_ref):
    n = dv_ref.shape[2]
    qk = mxu(xt_ref[...], dqk_ref[0]).astype(BF16)
    v = mxu(xt_ref[...], dv_ref[0]).astype(BF16)
    o = mxu(dt_ref[...], o_ref[0]).astype(BF16)

    @pl.when(s_ref[0] == 0)
    def _():
        mine_ref[0] = qk
        send_ref[0, :, :n] = v
        send_ref[0, :, n:] = o

    @pl.when(s_ref[0] == 1)
    def _():
        send_ref[0] = qk
        mine_ref[0, :, :n] = v
        mine_ref[0, :, n:] = o


def grads_a(scalars, x_t, d_t, d_qk, d_v, attended):
    width, length = x_t.shape
    wide, n = d_qk.shape[2], d_v.shape[2]
    whole = pl.BlockSpec((width, length), lambda j: (0, 0))
    by_j = lambda *shape: pl.BlockSpec(shape, lambda j: (j,) + (0,) * (len(shape) - 1))
    return pl.pallas_call(
        grads_a_kernel,
        grid=(2,),
        in_specs=[SMEM, whole, whole, by_j(1, length, wide), by_j(1, length, n), by_j(1, length, n)],
        out_specs=[by_j(1, width, wide)] * 2,
        out_shape=[out(2, width, wide)] * 2,
        compiler_params=params(32),
        cost_estimate=cost(2.4e9, 8e6),
        name="grads_a",
    )(scalars, x_t, d_t, d_qk, d_v, attended)


def input_grad_kernel(s_ref, dqk_ref, dv_ref, a0_ref, a1_ref, a3_ref, got_ref, far_ref, near_ref, qk_w, vo_w, total_ref):
    core = s_ref[0]
    j = pl.program_id(0)
    n = dv_ref.shape[2]
    tokens = far_ref.shape[0]
    pick_weights(core, j, a0_ref, a1_ref, a3_ref, got_ref, qk_w, vo_w)
    part = mxu(dqk_ref[0], qk_w[...], NT) + mxu(dv_ref[0], vo_w[:, :n], NT)

    @pl.when(j == 0)
    def _():
        total_ref[...] = part

    @pl.when(j == 1)
    def _():
        total_ref[...] += part
        near_ref[...] = total_ref[pl.ds(pl.multiple_of(core * tokens, tokens), tokens), :]
        far_ref[...] = total_ref[pl.ds(pl.multiple_of((1 - core) * tokens, tokens), tokens), :].astype(BF16)


def input_grad_parts(scalars, d_qk, d_v, slots, got, tokens):
    width, wide = slots[0].shape
    n = wide // 2
    whole = lambda *shape: pl.BlockSpec(shape, lambda j: (0,) * len(shape))
    by_j = lambda *shape: pl.BlockSpec(shape, lambda j: (j,) + (0,) * (len(shape) - 1))
    return pl.pallas_call(
        input_grad_kernel,
        grid=(2,),
        in_specs=[SMEM, by_j(1, LEN, wide), by_j(1, LEN, n)] + [whole(width, wide)] * 3 + [by_j(1, width, wide)],
        out_specs=[whole(tokens, width)] * 2,
        out_shape=[out(tokens, width), out(tokens, width, dtype=F32)],
        scratch_shapes=[
            pltpu.VMEM((width, wide), BF16),
            pltpu.VMEM((width, wide), BF16),
            pltpu.VMEM((LEN, width), F32),
        ],
        compiler_params=params(32),
        cost_estimate=cost(1.8e9, 8e6),
        name="input_grad",
    )(scalars, d_qk, d_v, slots[0], slots[1], slots[3], got)


def first_norm_kernel(x_ref, near_ref, far_ref, gain_ref, resid_ref, normed_ref):
    residual = x_ref[...].astype(F32) + (near_ref[...] + far_ref[...].astype(F32))
    scale = lax.rsqrt(jnp.mean(residual * residual, -1, keepdims=True) + EPSILON)
    resid_ref[...] = residual
    normed_ref[...] = (residual * scale * gain_ref[0:1, :]).astype(BF16)


def last_norm_kernel(s_ref, resid_ref, near_ref, far_ref, gain_ref, cot_ref, out_ref, dsum_ref, dffn_ref, dgain_ref):
    core, live = s_ref[0], s_ref[1]
    tokens, width = resid_ref.shape
    residual = resid_ref[...]
    scale = lax.rsqrt(jnp.mean(residual * residual, -1, keepdims=True) + EPSILON)
    summed = residual * scale * gain_ref[0:1, :] + (near_ref[...] + far_ref[...].astype(F32))
    scale = lax.rsqrt(jnp.mean(summed * summed, -1, keepdims=True) + EPSILON)
    unit = summed * scale
    out_ref[...] = (unit * gain_ref[1:2, :]).astype(BF16)
    position = core * tokens + lax.broadcasted_iota(jnp.int32, (tokens, 1), 0)
    cot = jnp.where(position < live, cot_ref[...].astype(F32), 0.0)
    dgain_ref[...] = jnp.sum(cot * unit, 0, keepdims=True)
    hat = cot * gain_ref[1:2, :]
    inner = jnp.mean(hat * unit, -1, keepdims=True)
    d_summed = scale * (hat - unit * inner)
    dsum_ref[...] = d_summed
    dffn_ref[...] = d_summed.astype(BF16)


def back_norm_kernel(resid_ref, near_ref, far_ref, dsum_ref, gain_ref, dres_ref, dbranch_ref, dgain_ref):
    residual = resid_ref[...]
    scale = lax.rsqrt(jnp.mean(residual * residual, -1, keepdims=True) + EPSILON)
    unit = residual * scale
    d_normed = dsum_ref[...] + (near_ref[...] + far_ref[...].astype(F32))
    dgain_ref[...] = jnp.sum(d_normed * unit, 0, keepdims=True)
    hat = d_normed * gain_ref[0:1, :]
    inner = jnp.mean(hat * unit, -1, keepdims=True)
    d_residual = scale * (hat - unit * inner)
    dres_ref[...] = d_residual
    dbranch_ref[...] = d_residual.astype(BF16)


def ffn_forward_kernel(y0_ref, y1_ref, g0_ref, g1_ref, g2_ref, g3_ref, dn_ref, hid_ref, silu_ref, slope_ref, far_ref, near_ref):
    tokens = y0_ref.shape[0]
    half = dn_ref.shape[2]
    for part, y_ref in ((1, y1_ref), (0, y0_ref)):
        at = slice(part * tokens, (part + 1) * tokens)
        total = None
        for slot, g_ref in enumerate((g0_ref, g1_ref, g2_ref, g3_ref)):
            both = mxu(y_ref[...], g_ref[...])
            gate, up = both[:, :half], both[:, half:]
            sig = jax.nn.sigmoid(gate)
            silu = gate * sig
            hidden = (silu * up).astype(BF16)
            hid_ref[slot, at, :] = hidden
            silu_ref[slot, at, :] = silu.astype(BF16)
            slope_ref[slot, at, :] = (up * (sig * (1.0 + gate * (1.0 - sig)))).astype(BF16)
            term = mxu(hidden, dn_ref[slot], NT)
            total = term if total is None else total + term
        if part:
            far_ref[...] = total.astype(BF16)
        else:
            near_ref[...] = total


def ffn_backward_kernel(d0_ref, d1_ref, silu_ref, slope_ref, dn_ref, g0_ref, g1_ref, g2_ref, g3_ref, dgu_ref, far_ref, near_ref):
    tokens = d0_ref.shape[0]
    half = dn_ref.shape[2]
    for part, d_ref in ((1, d1_ref), (0, d0_ref)):
        at = slice(part * tokens, (part + 1) * tokens)
        total = None
        for slot, g_ref in enumerate((g0_ref, g1_ref, g2_ref, g3_ref)):
            d_hidden = mxu(d_ref[...], dn_ref[slot])
            dgu_ref[slot, at, :half] = (d_hidden * slope_ref[slot, at, :].astype(F32)).astype(BF16)
            dgu_ref[slot, at, half:] = (d_hidden * silu_ref[slot, at, :].astype(F32)).astype(BF16)
            term = mxu(dgu_ref[slot, at, :], g_ref[...], NT)
            total = term if total is None else total + term
        if part:
            far_ref[...] = total.astype(BF16)
        else:
            near_ref[...] = total


def update(grad_full, moment, weight, average, factor):
    clipped = grad_full * factor
    new_moment = MOMENTUM * moment + clipped
    new_weight = weight - RATE * (clipped + MOMENTUM * new_moment)
    new_average = DECAY * average + (1.0 - DECAY) * new_weight
    return (new_moment, new_weight, new_average)


def update_kernel(s_ref, f_ref, a0_ref, a1_ref, g0_ref, g1_ref, d0_ref, d1_ref, *refs):
    old, new = refs[:12], refs[12:]
    factor = f_ref[0]
    n = old[0].shape[2]
    half = d0_ref.shape[1]

    def put(kind, at, grad):
        results = update(grad, old[4 + kind][at], old[kind][at], old[8 + kind][at], factor)
        for which, value in enumerate(results):
            new[4 * which + kind][at] = value

    def all_of(a_qk, a_vo, g_lo, g_hi, d_lo, d_hi):
        put(0, (0, slice(None), slice(None)), a_qk[:, :n].astype(F32))
        put(0, (1, slice(None), slice(None)), a_qk[:, n:].astype(F32))
        put(0, (2, slice(None), slice(None)), a_vo[:, :n].astype(F32))
        put(1, (slice(None), slice(None)), a_vo[:, n:].astype(F32).T)
        for which, (g_ref, d_ref) in enumerate(((g_lo, d_lo), (g_hi, d_hi))):
            lanes = slice(which * half, (which + 1) * half)
            put(2, (0, slice(None), lanes), g_ref[:, :half].astype(F32))
            put(2, (1, slice(None), lanes), g_ref[:, half:].astype(F32))
            put(3, (lanes, slice(None)), d_ref[...].astype(F32).T)

    @pl.when(s_ref[0] == 0)
    def _():
        all_of(a0_ref, a1_ref, g0_ref, g1_ref, d0_ref, d1_ref)

    @pl.when(s_ref[0] == 1)
    def _():
        all_of(a1_ref, a0_ref, g1_ref, g0_ref, d1_ref, d0_ref)


def body(
    rows,
    cols,
    block_input,
    out_grad,
    lengths,
    w_qkv,
    w_out,
    w_gate_up,
    w_down,
    gains,
    mom_qkv,
    mom_out,
    mom_gate_up,
    mom_down,
    mom_gains,
    ema_qkv,
    ema_out,
    ema_gate_up,
    ema_down,
    ema_gains,
):
    d = lax.axis_index("dp")
    r = lax.axis_index("row")
    c = lax.axis_index("col")
    core0 = d == 0
    tokens, width = block_input.shape
    ring = cols <= 4
    part = width // cols
    head_cols = w_qkv.shape[2]
    half = w_gate_up.shape[2] // 2

    pairs = [(i, j) for i in range(2) for j in range(rows)]
    swap_pairs = [(i * rows + j, (j % 2) * rows + (j // 2) * 2 + i) for i, j in pairs]
    first_pairs = [(i * rows + j, i * rows + (j ^ (1 if i == 0 else 2))) for i, j in pairs]
    second_pairs = [(i * rows + j, i * rows + (j ^ (2 if i == 0 else 1))) for i, j in pairs]

    def swap_tokens(t):
        return lax.ppermute(t, ("dp", "row"), swap_pairs)

    def first(t):
        return lax.ppermute(t, ("dp", "row"), first_pairs)

    def second(t):
        return lax.ppermute(t, ("dp", "row"), second_pairs)

    def core(t):
        return lax.ppermute(t, "dp", [(0, 1), (1, 0)])

    def along(t, k):
        return lax.ppermute(t, "col", [(i, (i + k) % cols) for i in range(cols)])

    def sum_over(t, axis, size):
        values = [t] + [lax.ppermute(t, axis, [(i, i ^ b) for i in range(size)]) for b in range(1, size)]
        while len(values) > 1:
            values = [values[i] + values[i + 1] for i in range(0, len(values), 2)]
        return values[0]

    def sum_chips(t):
        t = sum_over(t, "row", rows)
        if cols <= 4:
            return sum_over(t, "col", cols)
        return lax.psum(t, "col")

    def shift(k):
        return lax.rem(c + k + cols, cols) * part

    def spread_cols(t, axis):
        return [along(t, k) for k in range(1, cols)]

    def join_cols(t, got, axis):
        shape = list(t.shape)
        shape[axis] = width
        whole = jnp.zeros(shape, t.dtype)
        for k, block in enumerate([t] + got):
            whole = lax.dynamic_update_slice_in_dim(whole, block, shift(-k), axis)
        return whole

    def block_of(t, k, axis):
        return lax.dynamic_slice_in_dim(t, shift(k), part, axis)

    def scatter_cols(t):
        if not ring:
            return lax.psum_scatter(t, "col", scatter_dimension=0, tiled=True).astype(F32)
        got = [along(block_of(t, k, 0), k) for k in range(1, cols)]
        total = block_of(t, 0, 0).astype(F32)
        for block in got:
            total = total + block.astype(F32)
        return total

    core_id = jnp.full((1,), d, jnp.int32)
    piece_a, piece_d = pl.pallas_call(
        pieces_ad_kernel,
        in_specs=[SMEM, VMEM, VMEM, VMEM],
        out_specs=[VMEM] * 2,
        out_shape=[out(part, 2 * head_cols), out(part, half)],
        compiler_params=params(16),
        name="pieces_ad",
    )(core_id, w_qkv, w_out, w_down)

    x_own = swap_tokens(block_input)
    own_length = swap_tokens(lengths)[0, :]
    seq_ids = jnp.arange(own_length.shape[0], dtype=jnp.int32)
    own_length = jnp.sum(jnp.where(seq_ids == r // 2, own_length, 0))
    scalars = jnp.stack([d.astype(jnp.int32), own_length])
    (piece_g,) = pl.pallas_call(
        pieces_g_kernel,
        in_specs=[SMEM, VMEM],
        out_specs=[VMEM],
        out_shape=[out(part, 2 * half)],
        compiler_params=params(16),
        name="pieces_g",
    )(core_id, w_gate_up)

    got_a = spread_cols(piece_a, 0) if ring else lax.all_gather(piece_a, "col", axis=0, tiled=True)
    d1, d2 = first(piece_d), second(piece_d)
    got_a, d1, d2, piece_g, x_own = fence(got_a, d1, d2, piece_g, x_own)
    full_a = join_cols(piece_a, got_a, 0) if ring else got_a
    a1, a2 = first(full_a), second(full_a)
    got_g = spread_cols(piece_g, 0) if ring else lax.all_gather(piece_g, "col", axis=0, tiled=True)
    d3 = second(d1)
    x_other = core(x_own)
    full_a, a1, a2, got_g, d3, x_other = fence(full_a, a1, a2, got_g, d3, x_other)
    a3 = second(a1)
    slots_d = jnp.stack([piece_d, d1, d2, d3])
    if ring:
        ring_d = [along(slots_d, 1)]
    full_g = join_cols(piece_g, got_g, 0) if ring else got_g
    a3, ring_d, full_g = fence(a3, ring_d if ring else [], full_g)
    slots_a = [full_a, a1, a2, a3]
    send = jnp.where(core0, jnp.stack([a2, a3]), jnp.stack([full_a, a2]))
    got = core(send)
    g1, g2 = first(full_g), second(full_g)
    if ring and cols > 2:
        ring_d = ring_d + [along(ring_d[-1], 1)]

    cos, sin = pair_tables()
    q, k, v, attended, attended_t, lse, x_t, far, near = attend_forward(
        scalars, x_own, x_other, slots_a, got, cos, sin
    )
    far, g1, g2, ring_d = fence(far, g1, g2, ring_d)
    g3 = second(g1)
    if ring and cols > 3:
        ring_d = ring_d + [along(ring_d[-1], 1)]
    slots_g = [full_g, g1, g2, g3]
    if ring:
        w_dn = join_cols(slots_d, ring_d, 1)
    else:
        w_dn = lax.all_gather(slots_d, "col", axis=1, tiled=True)

    residual, normed = pl.pallas_call(
        first_norm_kernel,
        in_specs=[VMEM] * 4,
        out_specs=[VMEM] * 2,
        out_shape=[out(tokens, width, dtype=F32), out(tokens, width)],
        compiler_params=params(24),
        cost_estimate=cost(4e6, 6e6),
        name="first_norm",
    )(x_own, near, core(far), gains)
    normed_other = core(normed)

    hidden, silu, slope, far, near = pl.pallas_call(
        ffn_forward_kernel,
        in_specs=[VMEM] * 7,
        out_specs=[VMEM] * 5,
        out_shape=[out(4, 2 * tokens, half)] * 3 + [out(tokens, width), out(tokens, width, dtype=F32)],
        compiler_params=params(48),
        cost_estimate=cost(5e9, 15e6, 1e6),
        name="ffn_forward",
    )(normed, normed_other, *slots_g, w_dn)
    cot = swap_tokens(out_grad)
    output, d_summed, d_ffn, grad_gain_two = pl.pallas_call(
        last_norm_kernel,
        in_specs=[SMEM] + [VMEM] * 5,
        out_specs=[VMEM] * 4,
        out_shape=[out(tokens, width), out(tokens, width, dtype=F32), out(tokens, width), out(1, width, dtype=F32)],
        compiler_params=params(32),
        cost_estimate=cost(10e6, 8e6),
        name="last_norm",
    )(scalars, residual, near, core(far), gains, cot)
    d_ffn_other = core(d_ffn)
    d_ffn_full = jnp.concatenate([d_ffn, d_ffn_other], 0)
    normed_full = jnp.concatenate([normed, normed_other], 0)

    grad_dn = jnp.einsum("td,ste->sde", d_ffn_full, hidden, preferred_element_type=F32).astype(BF16)
    if ring:
        moving = along(block_of(grad_dn, cols - 1, 1), 1)
    d_gu, far, near = pl.pallas_call(
        ffn_backward_kernel,
        in_specs=[VMEM] * 9,
        out_specs=[VMEM] * 3,
        out_shape=[out(4, 2 * tokens, 2 * half), out(tokens, width), out(tokens, width, dtype=F32)],
        compiler_params=params(48),
        cost_estimate=cost(5e9, 15e6),
        name="ffn_backward",
    )(d_ffn, d_ffn_other, silu, slope, w_dn, *slots_g)
    if ring:
        far, moving, d_gu = fence(far, moving, d_gu)

    def grad_gu(s):
        return jnp.einsum("td,te->de", normed_full, d_gu[s], preferred_element_type=F32).astype(BF16)

    got_far = core(far)
    gu3 = grad_gu(3)
    gu1 = grad_gu(1)
    got_far, gu3, gu1 = fence(got_far, gu3, gu1)
    moved = second(gu3)
    if ring:
        for hop in range(cols - 2, 0, -1):
            block = (block_of(grad_dn, hop, 1).astype(F32) + moving.astype(F32)).astype(BF16)
            moving = along(block, 1)
        own_dn = (block_of(grad_dn, 0, 1).astype(F32) + moving.astype(F32)).astype(BF16)
    else:
        own_dn = lax.psum_scatter(grad_dn, "col", scatter_dimension=1, tiled=True)
    d_residual, d_branch, grad_gain_one = pl.pallas_call(
        back_norm_kernel,
        in_specs=[VMEM] * 5,
        out_specs=[VMEM] * 3,
        out_shape=[out(tokens, width, dtype=F32), out(tokens, width), out(1, width, dtype=F32)],
        compiler_params=params(32),
        cost_estimate=cost(10e6, 8e6),
        name="back_norm",
    )(residual, near, got_far, d_summed, gains)
    d_branch_other = core(d_branch)
    gu2, gu0 = grad_gu(2), grad_gu(0)
    moved, d_branch_other, gu2, gu0 = fence(moved, d_branch_other, gu2, gu0)
    gu1 = (gu1.astype(F32) + moved.astype(F32)).astype(BF16)
    moved_one, moved_two = first(gu1), second(gu2)
    d_qk, d_v, d_t = attend_backward(
        scalars, d_branch, d_branch_other, slots_a, got, cos, sin, q, k, v, attended_t, lse
    )
    moved_one, moved_two, d_qk, d_v, d_t = fence(moved_one, moved_two, d_qk, d_v, d_t)
    gu0 = (gu0.astype(F32) + moved_one.astype(F32) + moved_two.astype(F32)).astype(BF16)
    shard_g = scatter_cols(gu0).astype(BF16)
    mine, send = grads_a(scalars, x_t, d_t, d_qk, d_v, attended)
    theirs = core(send)
    s3 = jnp.where(core0, theirs[1], mine[1])
    s1 = jnp.where(core0, mine[1], mine[0])
    s2 = jnp.where(core0, theirs[0], theirs[1])
    s0 = jnp.where(core0, mine[0], theirs[0])
    moved = second(s3)
    far, near = input_grad_parts(scalars, d_qk, d_v, slots_a, got, tokens)
    moved, far, near = fence(moved, far, near)
    s1 = (s1.astype(F32) + moved.astype(F32)).astype(BF16)
    moved_one, moved_two = first(s1), second(s2)
    input_grad = (d_residual + (near + core(far).astype(F32))).astype(BF16)
    moved_dn = second(own_dn[3])
    moved_one, moved_two, input_grad, moved_dn = fence(moved_one, moved_two, input_grad, moved_dn)
    s0 = (s0.astype(F32) + moved_one.astype(F32) + moved_two.astype(F32)).astype(BF16)
    shard_a = scatter_cols(s0).astype(BF16)
    dn1 = (own_dn[1].astype(F32) + moved_dn.astype(F32)).astype(BF16)
    shard_d = (own_dn[0].astype(F32) + first(dn1).astype(F32) + second(own_dn[2]).astype(F32)).astype(BF16)
    input_grad = swap_tokens(input_grad).astype(F32)
    output = swap_tokens(output).astype(F32)

    far_a, far_g, far_d = core(shard_a), core(shard_g), core(shard_d)
    gain_total = jnp.concatenate([grad_gain_one, grad_gain_two], 0)
    gain_total = sum_chips(sum_over(gain_total, "dp", 2))
    local_squares = sum(jnp.sum(jnp.square(t.astype(F32))) for t in (shard_a, shard_g, shard_d))
    remote_squares = sum(jnp.sum(jnp.square(t.astype(F32))) for t in (far_a, far_g, far_d))
    local_squares = local_squares + remote_squares
    squares = sum_chips(jnp.full((8, 128), local_squares, F32))[0, 0] + jnp.sum(gain_total * gain_total)
    grad_norm = jnp.sqrt(squares)
    factor = jnp.minimum(1.0, CLIP / (grad_norm + 1e-06))
    weights = (w_qkv, w_out, w_gate_up, w_down)
    moments = (mom_qkv, mom_out, mom_gate_up, mom_down)
    averages = (ema_qkv, ema_out, ema_gate_up, ema_down)
    results = pl.pallas_call(
        update_kernel,
        in_specs=[SMEM, SMEM] + [VMEM] * 18,
        out_specs=[VMEM] * 12,
        out_shape=[out(*t.shape, dtype=F32) for t in weights * 3],
        compiler_params=params(40),
        cost_estimate=cost(5e6, 12e6),
        name="update",
    )(core_id, factor[None], shard_a, far_a, shard_g, far_g, shard_d, far_d, *weights, *moments, *averages)
    gain_new = update(gain_total, mom_gains, gains, ema_gains, factor)
    return (
        output,
        input_grad,
        grad_norm,
        *results[0:4],
        gain_new[0],
        *results[4:8],
        gain_new[1],
        *results[8:12],
        gain_new[2],
    )


def solution(mesh):
    tok = P(("dp", "col", "row"), None)
    weights = (P(None, "col", "row"), P("row", "col"), P(None, "col", "row"), P("row", "col"), P())
    in_specs = (tok, tok, P(("dp", "col"), None)) + weights * 3
    out_specs = (tok, tok, P()) + weights * 3
    fn = functools.partial(body, mesh.shape["row"], mesh.shape["col"])
    return jax.shard_map(fn, mesh=mesh, in_specs=in_specs, out_specs=out_specs, check_vma=False)
```

time: 474 us -> 350 us (0.74)
  waiting for transfers between devices: 168 us -> 90.6 us
  Pallas kernels: 30.4 us -> 80.6 us
  matrix products: 53.8 us -> 10.3 us
  other arithmetic: 56.3 us -> 25.1 us
  local copies, waits for them, and re-layouts: 53.4 us -> 41.2 us
  starting transfers between devices: 98.9 us -> 88.4 us
    pallas_call x2 -> x12, Pallas kernels: 30.4 us -> 80.6 us  [the longest x1 21.6 us: attend_forward(): pl.pallas_call(attend_forward_kernel, grid=(2,), in_specs=[SMEM] + [whole...]
    ppermute x18, waiting for transfers between devices: 101 us -> 52.9 us  [along(): return lax.ppermute(t, 'col', [(i, (i + k) % cols) for i in range(cols)])]
    dot_general x19 -> x4, matrix products: 50.6 us -> 6.33 us  [grad_gu(): jnp.einsum('td,te->de', normed_full, d_gu[s], preferred_element_type=F32)]
    ppermute x10 -> x13, waiting for transfers between devices: 19.8 us -> 4.25 us  [sum_over(): lax.ppermute(t, axis, [(i, i ^ b) for i in range(size)])]
    ppermute x6, waiting for transfers between devices: 17.3 us -> 2.17 us  [first(): return lax.ppermute(t, ('dp', 'row'), first_pairs)]
    concatenate x10 -> x1, other arithmetic: 11.2 us -> 0.01 us  [body(): gain_total = jnp.concatenate([grad_gain_one, grad_gain_two], 0)]
    ppermute x13, starting transfers between devices: 12.5 us -> 1.89 us  [core(): return lax.ppermute(t, 'dp', [(0, 1), (1, 0)])]
    another operation x6 -> x1, other arithmetic: 7.3 us -> 0.72 us  [body(): scalars = jnp.stack([d.astype(jnp.int32), own_length])]
  transfers between devices with their start and end apart: 64 -> 67, of which waited for: 26 -> 22; matrix products, arithmetic and copies ran while one was open for 30% -> 12% of each run, Pallas kernels for 6% -> 22%
where the time goes in v2:
time: 350 us; the launch traced here: 345 us
  waiting for transfers between devices  90.6 us (26%)
  starting transfers between devices  88.4 us (25%)
  Pallas kernels  80.6 us (23%)
  local copies, waits for them, and re-layouts  41.2 us (12%)
  other arithmetic  25.1 us (7%)
  matrix products  10.3 us (3%)
  between operations  8.57 us (2%)
    ppermute x18, waiting for transfers between devices, along(): return lax.ppermute(t, 'col', [(i, (i + k) % cols) for i in range(cols)])  52.9 us
    unnamed x187, local copies, waits for them, and re-layouts  37.2 us
    ppermute x18, starting transfers between devices, along(): return lax.ppermute(t, 'col', [(i, (i + k) % cols) for i in range(cols)])  26.6 us
    ppermute x12, waiting for transfers between devices, second(): return lax.ppermute(t, ('dp', 'row'), second_pairs)  25.5 us
    pallas_call x1, Pallas kernels, attend_forward(): pl.pallas_call(attend_forward_kernel, grid=(2,), in_specs=[SMEM] + [whole...  21.6 us
    ppermute x5, starting transfers between devices, swap_tokens(): return lax.ppermute(t, ('dp', 'row'), swap_pairs)  18.7 us
    pallas_call x1, Pallas kernels, attend_backward(): pl.pallas_call(attend_backward_kernel, grid=(2,), in_specs=[SMEM] + [whol...  18.4 us
    ppermute x13, starting transfers between devices, sum_over(): lax.ppermute(t, axis, [(i, i ^ b) for i in range(size)])  17.7 us
  transfers between devices with their start and end apart: 67, of which 22 were waited for; matrix products, arithmetic and copies ran while one was open for 12% of the time, Pallas kernels for 22%

profile of v2, /device:TPU:0, one launch (start us, length us, event | category | flops | bytes accessed | tf_op | source)
XLA Modules:
  0.0 344.7 jit_solution(2535911619366168140)
XLA Ops:
  0.7 1.9 collective-permute-start.6
  6.0 3.1 collective-permute-start.4
  9.1 1.6 collective-permute-start.1
  10.7 2.6 collective-permute-start.2
  13.3 1.3 collective-permute-start.3
  14.7 2.2 collective-permute-done.4
  17.5 1.5 collective-permute-start.5
  19.1 3.0 collective-permute-done.5
  22.1 1.8 collective-permute-done.2
  26.5 2.6 collective-permute-start.10
  30.2 11.7 %collective-permute-done.12 = bf16[192,256]{1,0:T(8,128)(2,1)S(1)} collective-permute-done((bf16[192,256]{1,0:T(8,128)(2,1)S(1)}, bf16[192,256]{1,0:T(8,128)(2,1)S(1)}, u32[]{:S(2)}, u32[]{:S(2)}) %collective-permute-start.12) | collective-permute-done | bytes 98336 | tf_op jit(solution)/shard_map/ppermute | solution.py:549
  41.9 4.5 %collective-permute-start.11 = (bf16[192,512]{1,0:T(8,128)(2,1)S(1)}, bf16[192,512]{1,0:T(8,128)(2,1)}, u32[]{:S(2)}, u32[]{:S(2)}) collective-permute-start(bf16[192,512]{1,0:T(8,128)(2,1)S(1)} %pieces_g.1), channel_id=1, source_target_pairs={{0,3},{1,0},{2,1},{3,2},{4,7},{5,4},{6,5},{7,6},{8,11},{9,8},{10,9... | collective-permute-start | bytes 589832 | tf_op jit(solution)/shard_map/ppermute | solution.py:555
  46.5 5.2 %collective-permute-done.11 = bf16[192,512]{1,0:T(8,128)(2,1)} collective-permute-done((bf16[192,512]{1,0:T(8,128)(2,1)S(1)}, bf16[192,512]{1,0:T(8,128)(2,1)}, u32[]{:S(2)}, u32[]{:S(2)}) %collective-permute-start.11) | collective-permute-done | bytes 196640 | tf_op jit(solution)/shard_map/ppermute | solution.py:555
  51.6 4.7 %collective-permute-done.9 = bf16[192,512]{1,0:T(8,128)(2,1)} collective-permute-done((bf16[192,512]{1,0:T(8,128)(2,1)S(1)}, bf16[192,512]{1,0:T(8,128)(2,1)}, u32[]{:S(2)}, u32[]{:S(2)}) %collective-permute-start.9) | collective-permute-done | bytes 196640 | tf_op jit(solution)/shard_map/ppermute | solution.py:555
  57.8 1.7 collective-permute-start.15
  61.6 8.6 %collective-permute-done.15 = bf16[4,192,256]{2,1,0:T(8,128)(2,1)S(1)} collective-permute-done((bf16[4,192,256]{2,1,0:T(8,128)(2,1)S(1)}, bf16[4,192,256]{2,1,0:T(8,128)(2,1)S(1)}, u32[]{:S(2)}, u32[]{:S(2)}) %collective-permute-start.15) | collective-permute-done | bytes 393248 | tf_op jit(solution)/shard_map/ppermute | solution.py:555
  70.9 2.5 maximum_select_fusion
  74.7 5.2 %collective-permute-start.17 = (bf16[768,512]{1,0:T(8,128)(2,1)S(1)}, bf16[768,512]{1,0:T(8,128)(2,1)S(1)}, u32[]{:S(2)}, u32[]{:S(2)}) collective-permute-start(bf16[768,512]{1,0:T(8,128)(2,1)S(1)} %constant_dynamic-update-slice_fusion.6.g0_ref), channel_id=1, source_target_pairs={{0,4},{4,0},{8,12},{12,8},{16,24},{20,28},{24,16},{28,20},{1,5},{5... | collective-permute-start | bytes 2359304 | tf_op jit(solution)/shard_map/ppermute | solution.py:546
  85.0 21.6 %attend_forward.1 = (bf16[6,1024,128]{2,1,0:T(8,128)(2,1)S(1)}, bf16[6,1024,128]{2,1,0:T(8,128)(2,1)}, bf16[6,1024,128]{2,1,0:T(8,128)(2,1)}, bf16[2,1024,192]{2...) custom-call(s32[2]{0:T(128)S(1)} %pad_add_fusion.s_ref, ...), custom_call_target="tpu_custom_call" | custom-call | flops 8000000000 | bytes 12000000 | tf_op jit(solution)/shard_map/attend_forward/pallas_call | solution.py:202
  111.7 1.4 copy-done.10
  116.2 11.1 %collective-permute-done.23 = bf16[4,192,256]{2,1,0:T(8,128)(2,1)S(1)} collective-permute-done((bf16[4,192,256]{2,1,0:T(8,128)(2,1)S(1)}, bf16[4,192,256]{2,1,0:T(8,128)(2,1)S(1)}, u32[]{:S(2)}, u32[]{:S(2)}) %collective-permute-start.23) | collective-permute-done | bytes 393248 | tf_op jit(solution)/shard_map/ppermute | solution.py:555
  128.5 10.6 %ffn_forward.1 = (bf16[4,1024,256]{2,1,0:T(8,128)(2,1)}, bf16[4,1024,256]{2,1,0:T(8,128)(2,1)}, bf16[4,1024,256]{2,1,0:T(8,128)(2,1)}, bf16[512,768]{1,0:T(8,128)(2,1)S(1)}, f32[512,768]{1,0:T(8,128)}) custom-call(bf16[512,768]{1,0:T(8,128)(2,1)S(1)} %get-tuple-element.134.y0_ref, bf16[512,768]{1,0:T(8,128)(2,1)S(1)} %collective-permute-done.21.y1_ref, ...), custom_call_target="tpu_custom_call" | custom-call | flops 5000000000 | bytes 15000000 | tf_op jit(solution)/shard_map/ffn_forward/pallas_call | solution.py:666
  139.2 2.3 collective-permute-done.24.far_ref
  141.5 1.4 copy-done.11
  142.9 2.7 last_norm.1
  146.9 2.5 collective-permute-done.27.d1_ref
  149.4 4.0 %convolution_convert_fusion = bf16[4,256,768]{1,2,0:T(8,128)(2,1)S(1)} fusion(bf16[4,1024,256]{2,1,0:T(8,128)(2,1)} %get-tuple-element.147, bf16[512,768]{1,0:T(8,128)(2,1)} %collective-permute-done.27.d1_ref, bf16[512,768]{1,0:T(8,128)(2,1)} %get-tuple-element.143.d0_ref), kind=kOutput, calls=%fused_computation | convolution fusion | flops 1614544896 | bytes 5242880 | tf_op jit(solution)/shard_map/td,ste->sde/dot_general | solution.py:689
  153.7 10.9 %ffn_backward.1 = (bf16[4,1024,512]{2,1,0:T(8,128)(2,1)}, bf16[512,768]{1,0:T(8,128)(2,1)S(1)}, f32[512,768]{1,0:T(8,128)}) custom-call(bf16[512,768]{1,0:T(8,128)(2,1)} %get-tuple-element.143.d0_ref, bf16[512,768]{1,0:T(8,128)(2,1)} %collective-permute-done.27.d1_ref, bf16[4,1024,256]{2,1,0:T(8,128)(2,1)} %get-tuple-element.144.silu_ref, ...), custom_call_target="tpu_custom_call" | custom-call | flops 5000000000 | bytes 15000000 | tf_op jit(solution)/shard_map/ffn_backward/pallas_call | solution.py:692
  164.6 2.0 collective-permute-done.28
  166.8 2.4 convolution_convert_fusion.3
  174.8 2.0 convolution_convert_fusion.1
  177.8 6.7 %collective-permute-done.30 = bf16[768,512]{1,0:T(8,128)(2,1)S(1)} collective-permute-done((bf16[768,512]{1,0:T(8,128)(2,1)S(1)}, bf16[768,512]{1,0:T(8,128)(2,1)S(1)}, u32[]{:S(2)}, u32[]{:S(2)}) %collective-permute-start.30) | collective-permute-done | bytes 786464 | tf_op jit(solution)/shard_map/ppermute | solution.py:549
  186.4 18.4 %attend_backward.1 = (bf16[2,1024,384]{2,1,0:T(8,128)(2,1)S(1)}, bf16[2,1024,192]{2,1,0:T(8,128)(2,1)S(1)}, bf16[768,1024]{1,0:T(8,128)(2,1)}) custom-call(s32[2]{0:T(128)S(1)} %pad_add_fusion.s_ref, bf16[512,768]{1,0:T(8,128)(2,1)S(1)} %get-tuple-element.156.d0_ref, bf16[512,768]{1,0:T(8,128)(2,1)S(1)} %collective-permute-done.31.d1_ref, ...), custom_call_target="tpu_custom_call" | custom-call | flops 12000000000 | bytes 14000000 | tf_op jit(solution)/shard_map/attend_backward/pallas_call | solution.py:285
  205.7 1.9 copy-done.56
  207.6 5.4 %grads_a.1 = (bf16[2,768,384]{2,1,0:T(8,128)(2,1)S(1)}, bf16[2,768,384]{2,1,0:T(8,128)(2,1)}) custom-call(s32[2]{0:T(128)S(1)} %pad_add_fusion.s_ref, bf16[768,1024]{1,0:T(8,128)(2,1)S(1)} %copy-done.55, bf16[768,1024]{1,0:T(8,128)(2,1)S(1)} %copy-done.56, bf16[2,1024,384]{2,1,0:T(8,128)(2,1)S(1)} %get-tuple-element.169.dqk_ref, ...), custom_call_target="tpu_custom_call" | custom-call | flops 2400000000 | bytes 8000000 | tf_op jit(solution)/shard_map/grads_a/pallas_call | solution.py:333
  213.0 7.5 %collective-permute-start.26 = (bf16[512,768]{1,0:T(8,128)(2,1)}, bf16[512,768]{1,0:T(8,128)(2,1)}, u32[]{:S(2)}, u32[]{:S(2)}) collective-permute-start(bf16[512,768]{1,0:T(8,128)(2,1)} %get-tuple-element.141), channel_id=1, source_target_pairs={{0,0},{4,16},{8,8},{12,24},{16,4},{20,20},{24,12},{28,28},{1,1},{5... | collective-permute-start | bytes 2359304 | tf_op jit(solution)/shard_map/ppermute | solution.py:543
  220.5 2.0 fusion.14
  223.7 2.0 copy.43.refs_11_
  225.7 2.4 convert_element_type.187
  228.1 1.5 collective-permute-start.60
  229.6 3.0 collective-permute-done.40
  233.8 1.5 select_bitcast_fusion
  236.3 5.2 %input_grad.1 = (bf16[512,768]{1,0:T(8,128)(2,1)S(1)}, f32[512,768]{1,0:T(8,128)S(1)}) custom-call(s32[2]{0:T(128)S(1)} %pad_add_fusion.s_ref, bf16[2,1024,384]{2,1,0:T(8,128)(2,1)S(1)} %copy-done.52, bf16[2,1024,192]{2,1,0:T(8,128)(2,1)S(1)} %copy-done.54, bf16[768,384]{1,0:T(8,128)(2,1)S(1)} %constant_dynamic-update-slice_fusion.10.a0_ref, ...), custom_call_target="tpu_custom_call" | custom-call | flops 1800000000 | bytes 8000000 | tf_op jit(solution)/shard_map/input_grad/pallas_call | solution.py:369
  241.8 3.5 %collective-permute-done.35 = bf16[768,384]{1,0:T(8,128)(2,1)S(1)} collective-permute-done((bf16[768,384]{1,0:T(8,128)(2,1)S(1)}, bf16[768,384]{1,0:T(8,128)(2,1)S(1)}, u32[]{:S(2)}, u32[]{:S(2)}) %collective-permute-start.35) | collective-permute-done | bytes 589856 | tf_op jit(solution)/shard_map/ppermute | solution.py:549
  246.4 2.8 collective-permute-start.48
  250.3 4.7 %collective-permute-done.46 = bf16[192,512]{1,0:T(8,128)(2,1)S(1)} collective-permute-done((bf16[192,512]{1,0:T(8,128)(2,1)S(1)}, bf16[192,512]{1,0:T(8,128)(2,1)S(1)}, u32[]{:S(2)}, u32[]{:S(2)}) %collective-permute-start.46) | collective-permute-done | bytes 196640 | tf_op jit(solution)/shard_map/ppermute | solution.py:555
  255.1 7.5 %collective-permute-done.47 = bf16[192,512]{1,0:T(8,128)(2,1)S(1)} collective-permute-done((bf16[192,512]{1,0:T(8,128)(2,1)S(1)}, bf16[192,512]{1,0:T(8,128)(2,1)S(1)}, u32[]{:S(2)}, u32[]{:S(2)}) %collective-permute-start.47) | collective-permute-done | bytes 196640 | tf_op jit(solution)/shard_map/ppermute | solution.py:555
  268.0 1.5 collective-permute-start.49
  269.5 1.4 fusion.3
  270.9 3.7 %collective-permute-start.43 = (bf16[192,384]{1,0:T(8,128)(2,1)S(1)}, bf16[192,384]{1,0:T(8,128)(2,1)S(1)}, u32[]{:S(2)}, u32[]{:S(2)}) collective-permute-start(bf16[192,384]{1,0:T(8,128)(2,1)S(1)} %get-tuple-element.236), channel_id=1, source_target_pairs={{0,1},{1,2},{2,3},{3,0},{4,5},{5,6},{6,7},{7,4},{8,9},{9,10},{10,1... | collective-permute-start | bytes 442376 | tf_op jit(solution)/shard_map/ppermute | solution.py:555
  274.7 2.7 collective-permute-start.45
  280.9 3.4 collective-permute-done.44
  284.8 1.4 multiply_reduce_fusion.3
  288.9 1.5 multiply_reduce_fusion.4
  294.2 2.4 collective-permute-start.56
  296.6 3.6 %collective-permute-start.64 = (f32[2,768]{1,0:T(2,128)S(1)}, f32[2,768]{1,0:T(2,128)S(1)}, u32[]{:S(2)}, u32[]{:S(2)}) collective-permute-start(f32[2,768]{1,0:T(2,128)S(1)} %add_add_fusion.1), channel_id=1, source_target_pairs={{0,1},{1,0},{2,3},{3,2},{4,5},{5,4},{6,7},{7,6},{8,9},{9,8},{10,11... | collective-permute-start | bytes 18440 | tf_op jit(solution)/shard_map/ppermute | solution.py:558
  300.2 1.9 collective-permute-start.65
  302.7 7.4 %collective-permute-start.42 = (bf16[512,768]{1,0:T(8,128)(2,1)}, bf16[512,768]{1,0:T(8,128)(2,1)}, u32[]{:S(2)}, u32[]{:S(2)}) collective-permute-start(bf16[512,768]{1,0:T(8,128)(2,1)} %add_convert_fusion.1), channel_id=1, source_target_pairs={{0,0},{4,16},{8,8},{12,24},{16,4},{20,20},{24,12},{28,28},{1,1},{5... | collective-permute-start | bytes 2359304 | tf_op jit(solution)/shard_map/ppermute | solution.py:543
  311.3 2.8 collective-permute-start.58
  315.8 3.7 %collective-permute-done.59 = f32[8,128]{1,0:T(8,128)S(1)} collective-permute-done((f32[8,128]{1,0:T(8,128)S(1)}, f32[8,128]{1,0:T(8,128)S(1)}, u32[]{:S(2)}, u32[]{:S(2)}) %collective-permute-start.59) | collective-permute-done | bytes 4128 | tf_op jit(solution)/shard_map/ppermute | solution.py:558
  328.6 4.4 %update.1 = (f32[3,192,192]{2,1,0:T(8,128)}, f32[192,192]{1,0:T(8,128)}, f32[2,192,512]{2,1,0:T(8,128)}, f32[512,192]{1,0:T(8,128)S(1)}, f32[3,192,192]{2,1,0:T(...) custom-call(s32[1]{0:T(128)} %bitcast.s_ref, ...), custom_call_target="tpu_custom_call" | custom-call | flops 5000000 | bytes 12000000 | tf_op jit(solution)/shard_map/update/pallas_call | solution.py:772
  335.4 2.0 copy.44
  337.4 2.0 copy.45
  341.0 2.4 convert_element_type.214
  (324 shorter events, 71.8 us)
Async XLA Ops:
  0.7 23.3 %collective-permute-start.6 = (bf16[512,768]{1,0:T(8,128)(2,1)}, bf16[512,768]{1,0:T(8,128)(2,1)S(1)}, u32[]{:S(2)}, u32[]{:S(2)}) collective-permute-start(bf16[512,768]{1,0:T(8,128)(2,1)} %param.20), channel_id=1, source_target_pairs={{0,0},{4,16},{8,8},{12,24},{16,4},{20,20},{24,12},{28,28},{1,1},{5... | collective-permute-start | bytes 2359304 | tf_op jit(solution)/shard_map/ppermute | solution.py:543
  6.0 10.9 %collective-permute-start.4 = (bf16[192,256]{1,0:T(8,128)(2,1)S(1)}, bf16[192,256]{1,0:T(8,128)(2,1)S(1)}, u32[]{:S(2)}, u32[]{:S(2)}) collective-permute-start(bf16[192,256]{1,0:T(8,128)(2,1)S(1)} %get-tuple-element.111), channel_id=1, source_target_pairs={{0,4},{4,0},{8,12},{12,8},{16,24},{20,28},{24,16},{28,20},{1,5},{5... | collective-permute-start | bytes 294920 | tf_op jit(solution)/shard_map/ppermute | solution.py:546
  9.1 13.0 %collective-permute-start.1 = (bf16[192,384]{1,0:T(8,128)(2,1)S(1)}, bf16[192,384]{1,0:T(8,128)(2,1)S(1)}, u32[]{:S(2)}, u32[]{:S(2)}) collective-permute-start(bf16[192,384]{1,0:T(8,128)(2,1)S(1)} %get-tuple-element.110), channel_id=1, source_target_pairs={{0,1},{1,2},{2,3},{3,0},{4,5},{5,6},{6,7},{7,4},{8,9},{9,10},{10,1... | collective-permute-start | bytes 442376 | tf_op jit(solution)/shard_map/ppermute | solution.py:555
  10.7 13.2 %collective-permute-start.2 = (bf16[192,384]{1,0:T(8,128)(2,1)S(1)}, bf16[192,384]{1,0:T(8,128)(2,1)S(1)}, u32[]{:S(2)}, u32[]{:S(2)}) collective-permute-start(bf16[192,384]{1,0:T(8,128)(2,1)S(1)} %get-tuple-element.110), channel_id=1, source_target_pairs={{0,2},{1,3},{2,0},{3,1},{4,6},{5,7},{6,4},{7,5},{8,10},{9,11},{10,... | collective-permute-start | bytes 442376 | tf_op jit(solution)/shard_map/ppermute | solution.py:555
  13.3 10.7 %collective-permute-start.3 = (bf16[192,384]{1,0:T(8,128)(2,1)S(1)}, bf16[192,384]{1,0:T(8,128)(2,1)}, u32[]{:S(2)}, u32[]{:S(2)}) collective-permute-start(bf16[192,384]{1,0:T(8,128)(2,1)S(1)} %get-tuple-element.110), channel_id=1, source_target_pairs={{0,3},{1,0},{2,1},{3,2},{4,7},{5,4},{6,5},{7,6},{8,11},{9,8},{10,9... | collective-permute-start | bytes 442376 | tf_op jit(solution)/shard_map/ppermute | solution.py:555
  17.5 4.6 %collective-permute-start.5 = (bf16[192,256]{1,0:T(8,128)(2,1)S(1)}, bf16[192,256]{1,0:T(8,128)(2,1)S(1)}, u32[]{:S(2)}, u32[]{:S(2)}) collective-permute-start(bf16[192,256]{1,0:T(8,128)(2,1)S(1)} %get-tuple-element.111), channel_id=1, source_target_pairs={{0,8},{4,12},{8,0},{12,4},{16,20},{20,16},{24,28},{28,24},{1,9},{5... | collective-permute-start | bytes 294920 | tf_op jit(solution)/shard_map/ppermute | solution.py:549
  24.0 32.4 %collective-permute-start.13 = (bf16[512,768]{1,0:T(8,128)(2,1)S(1)}, bf16[512,768]{1,0:T(8,128)(2,1)}, u32[]{:S(2)}, u32[]{:S(2)}) collective-permute-start(bf16[512,768]{1,0:T(8,128)(2,1)S(1)} %collective-permute-done.6.x0_ref.x_ref), channel_id=1, source_target_pairs={{0,16},{16,0},{1,17},{17,1},{2,18},{18,2},{3,19},{19,3},{4,20},{20... | collective-permute-start | bytes 2359304 | tf_op jit(solution)/shard_map/ppermute | solution.py:552
  25.2 31.2 %collective-permute-start.7 = (bf16[768,384]{1,0:T(8,128)(2,1)S(1)}, bf16[768,384]{1,0:T(8,128)(2,1)}, u32[]{:S(2)}, u32[]{:S(2)}) collective-permute-start(bf16[768,384]{1,0:T(8,128)(2,1)S(1)} %constant_dynamic-update-slice_fusion.10.a0_ref), channel_id=1, source_target_pairs={{0,4},{4,0},{8,12},{12,8},{16,24},{20,28},{24,16},{28,20},{1,5},{5... | collective-permute-start | bytes 1769480 | tf_op jit(solution)/shard_map/ppermute | solution.py:546
  25.5 30.9 %collective-permute-start.8 = (bf16[768,384]{1,0:T(8,128)(2,1)S(1)}, bf16[768,384]{1,0:T(8,128)(2,1)}, u32[]{:S(2)}, u32[]{:S(2)}) collective-permute-start(bf16[768,384]{1,0:T(8,128)(2,1)S(1)} %constant_dynamic-update-slice_fusion.10.a0_ref), channel_id=1, source_target_pairs={{0,8},{4,12},{8,0},{12,4},{16,20},{20,16},{24,28},{28,24},{1,9},{5... | collective-permute-start | bytes 1769480 | tf_op jit(solution)/shard_map/ppermute | solution.py:549
  26.5 19.9 %collective-permute-start.10 = (bf16[192,512]{1,0:T(8,128)(2,1)S(1)}, bf16[192,512]{1,0:T(8,128)(2,1)S(1)}, u32[]{:S(2)}, u32[]{:S(2)}) collective-permute-start(bf16[192,512]{1,0:T(8,128)(2,1)S(1)} %pieces_g.1), channel_id=1, source_target_pairs={{0,2},{1,3},{2,0},{3,1},{4,6},{5,7},{6,4},{7,5},{8,10},{9,11},{10,... | collective-permute-start | bytes 589832 | tf_op jit(solution)/shard_map/ppermute | solution.py:555
  29.1 12.8 %collective-permute-start.12 = (bf16[192,256]{1,0:T(8,128)(2,1)S(1)}, bf16[192,256]{1,0:T(8,128)(2,1)S(1)}, u32[]{:S(2)}, u32[]{:S(2)}) collective-permute-start(bf16[192,256]{1,0:T(8,128)(2,1)S(1)} %copy-done.79), channel_id=1, source_target_pairs={{0,8},{4,12},{8,0},{12,4},{16,20},{20,16},{24,28},{28,24},{1,9},{5... | collective-permute-start | bytes 294920 | tf_op jit(solution)/shard_map/ppermute | solution.py:549
  41.9 9.7 %collective-permute-start.11 = (bf16[192,512]{1,0:T(8,128)(2,1)S(1)}, bf16[192,512]{1,0:T(8,128)(2,1)}, u32[]{:S(2)}, u32[]{:S(2)}) collective-permute-start(bf16[192,512]{1,0:T(8,128)(2,1)S(1)} %pieces_g.1), channel_id=1, source_target_pairs={{0,3},{1,0},{2,1},{3,2},{4,7},{5,4},{6,5},{7,6},{8,11},{9,8},{10,9... | collective-permute-start | bytes 589832 | tf_op jit(solution)/shard_map/ppermute | solution.py:555
  46.4 10.0 %collective-permute-start.9 = (bf16[192,512]{1,0:T(8,128)(2,1)S(1)}, bf16[192,512]{1,0:T(8,128)(2,1)}, u32[]{:S(2)}, u32[]{:S(2)}) collective-permute-start(bf16[192,512]{1,0:T(8,128)(2,1)S(1)} %pieces_g.1), channel_id=1, source_target_pairs={{0,1},{1,2},{2,3},{3,0},{4,5},{5,6},{6,7},{7,4},{8,9},{9,10},{10,1... | collective-permute-start | bytes 589832 | tf_op jit(solution)/shard_map/ppermute | solution.py:555
  56.4 13.7 %collective-permute-start.14 = (bf16[768,384]{1,0:T(8,128)(2,1)}, bf16[768,384]{1,0:T(8,128)(2,1)S(1)}, u32[]{:S(2)}, u32[]{:S(2)}) collective-permute-start(bf16[768,384]{1,0:T(8,128)(2,1)} %collective-permute-done.7.a1_ref), channel_id=1, source_target_pairs={{0,8},{4,12},{8,0},{12,4},{16,20},{20,16},{24,28},{28,24},{1,9},{5... | collective-permute-start | bytes 1769480 | tf_op jit(solution)/shard_map/ppermute | solution.py:549
  57.8 12.4 %collective-permute-start.15 = (bf16[4,192,256]{2,1,0:T(8,128)(2,1)S(1)}, bf16[4,192,256]{2,1,0:T(8,128)(2,1)S(1)}, u32[]{:S(2)}, u32[]{:S(2)}) collective-permute-start(bf16[4,192,256]{2,1,0:T(8,128)(2,1)S(1)} %get-tuple-element.242), channel_id=1, source_target_pairs={{0,1},{1,2},{2,3},{3,0},{4,5},{5,6},{6,7},{7,4},{8,9},{9,10},{10,1... | collective-permute-start | bytes 1179656 | tf_op jit(solution)/shard_map/ppermute | solution.py:555
  73.4 8.4 %collective-permute-start.16 = (bf16[2,768,384]{2,1,0:T(8,128)(2,1)}, bf16[2,768,384]{2,1,0:T(8,128)(2,1)}, u32[]{:S(2)}, u32[]{:S(2)}) collective-permute-start(bf16[2,768,384]{2,1,0:T(8,128)(2,1)} %maximum_select_fusion), channel_id=1, source_target_pairs={{0,16},{16,0},{1,17},{17,1},{2,18},{18,2},{3,19},{19,3},{4,20},{20... | collective-permute-start | bytes 3538952 | tf_op jit(solution)/shard_map/ppermute | solution.py:552
  74.7 34.6 %collective-permute-start.17 = (bf16[768,512]{1,0:T(8,128)(2,1)S(1)}, bf16[768,512]{1,0:T(8,128)(2,1)S(1)}, u32[]{:S(2)}, u32[]{:S(2)}) collective-permute-start(bf16[768,512]{1,0:T(8,128)(2,1)S(1)} %constant_dynamic-update-slice_fusion.6.g0_ref), channel_id=1, source_target_pairs={{0,4},{4,0},{8,12},{12,8},{16,24},{20,28},{24,16},{28,20},{1,5},{5... | collective-permute-start | bytes 2359304 | tf_op jit(solution)/shard_map/ppermute | solution.py:546
  79.9 29.4 %collective-permute-start.18 = (bf16[768,512]{1,0:T(8,128)(2,1)S(1)}, bf16[768,512]{1,0:T(8,128)(2,1)S(1)}, u32[]{:S(2)}, u32[]{:S(2)}) collective-permute-start(bf16[768,512]{1,0:T(8,128)(2,1)S(1)} %constant_dynamic-update-slice_fusion.6.g0_ref), channel_id=1, source_target_pairs={{0,8},{4,12},{8,0},{12,4},{16,20},{20,16},{24,28},{28,24},{1,9},{5... | collective-permute-start | bytes 2359304 | tf_op jit(solution)/shard_map/ppermute | solution.py:549
  81.5 27.9 %collective-permute-start.19 = (bf16[4,192,256]{2,1,0:T(8,128)(2,1)}, bf16[4,192,256]{2,1,0:T(8,128)(2,1)S(1)}, u32[]{:S(2)}, u32[]{:S(2)}) collective-permute-start(bf16[4,192,256]{2,1,0:T(8,128)(2,1)} %copy-done.74), channel_id=1, source_target_pairs={{0,1},{1,2},{2,3},{3,0},{4,5},{5,6},{6,7},{7,4},{8,9},{9,10},{10,1... | collective-permute-start | bytes 1179656 | tf_op jit(solution)/shard_map/ppermute | solution.py:555
  109.4 2.4 collective-permute-start.20
  109.4 17.9 %collective-permute-start.22 = (bf16[768,512]{1,0:T(8,128)(2,1)S(1)}, bf16[768,512]{1,0:T(8,128)(2,1)S(1)}, u32[]{:S(2)}, u32[]{:S(2)}) collective-permute-start(bf16[768,512]{1,0:T(8,128)(2,1)S(1)} %collective-permute-done.17.g1_ref), channel_id=1, source_target_pairs={{0,8},{4,12},{8,0},{12,4},{16,20},{20,16},{24,28},{28,24},{1,9},{5... | collective-permute-start | bytes 2359304 | tf_op jit(solution)/shard_map/ppermute | solution.py:549
  113.6 13.7 %collective-permute-start.21 = (bf16[512,768]{1,0:T(8,128)(2,1)S(1)}, bf16[512,768]{1,0:T(8,128)(2,1)S(1)}, u32[]{:S(2)}, u32[]{:S(2)}) collective-permute-start(bf16[512,768]{1,0:T(8,128)(2,1)S(1)} %get-tuple-element.134.y0_ref), channel_id=1, source_target_pairs={{0,16},{16,0},{1,17},{17,1},{2,18},{18,2},{3,19},{19,3},{4,20},{20... | collective-permute-start | bytes 2359304 | tf_op jit(solution)/shard_map/ppermute | solution.py:552
  113.8 13.5 %collective-permute-start.23 = (bf16[4,192,256]{2,1,0:T(8,128)(2,1)S(1)}, bf16[4,192,256]{2,1,0:T(8,128)(2,1)S(1)}, u32[]{:S(2)}, u32[]{:S(2)}) collective-permute-start(bf16[4,192,256]{2,1,0:T(8,128)(2,1)S(1)} %collective-permute-done.19), channel_id=1, source_target_pairs={{0,1},{1,2},{2,3},{3,0},{4,5},{5,6},{6,7},{7,4},{8,9},{9,10},{10,1... | collective-permute-start | bytes 1179656 | tf_op jit(solution)/shard_map/ppermute | solution.py:555
  114.8 24.4 %collective-permute-start.25 = (bf16[512,768]{1,0:T(8,128)(2,1)S(1)}, bf16[512,768]{1,0:T(8,128)(2,1)S(1)}, u32[]{:S(2)}, u32[]{:S(2)}) collective-permute-start(bf16[512,768]{1,0:T(8,128)(2,1)S(1)} %copy-done.87), channel_id=1, source_target_pairs={{0,0},{4,16},{8,8},{12,24},{16,4},{20,20},{24,12},{28,28},{1,1},{5... | collective-permute-start | bytes 2359304 | tf_op jit(solution)/shard_map/ppermute | solution.py:543
  146.8 2.6 collective-permute-start.27
  153.4 13.2 %collective-permute-start.28 = (bf16[4,192,256]{2,1,0:T(8,128)(2,1)S(1)}, bf16[4,192,256]{2,1,0:T(8,128)(2,1)S(1)}, u32[]{:S(2)}, u32[]{:S(2)}) collective-permute-start(bf16[4,192,256]{2,1,0:T(8,128)(2,1)S(1)} %dynamic-slice_bitcast_fusion), channel_id=1, source_target_pairs={{0,1},{1,2},{2,3},{3,0},{4,5},{5,6},{6,7},{7,4},{8,9},{9,10},{10,1... | collective-permute-start | bytes 1179656 | tf_op jit(solution)/shard_map/ppermute | solution.py:555
  166.6 3.7 %collective-permute-start.29 = (bf16[512,768]{1,0:T(8,128)(2,1)S(1)}, bf16[512,768]{1,0:T(8,128)(2,1)S(1)}, u32[]{:S(2)}, u32[]{:S(2)}) collective-permute-start(bf16[512,768]{1,0:T(8,128)(2,1)S(1)} %get-tuple-element.149), channel_id=1, source_target_pairs={{0,16},{16,0},{1,17},{17,1},{2,18},{18,2},{3,19},{19,3},{4,20},{20... | collective-permute-start | bytes 2359304 | tf_op jit(solution)/shard_map/ppermute | solution.py:552
  172.0 5.9 %collective-permute-start.31 = (bf16[512,768]{1,0:T(8,128)(2,1)S(1)}, bf16[512,768]{1,0:T(8,128)(2,1)S(1)}, u32[]{:S(2)}, u32[]{:S(2)}) collective-permute-start(bf16[512,768]{1,0:T(8,128)(2,1)S(1)} %get-tuple-element.156.d0_ref), channel_id=1, source_target_pairs={{0,16},{16,0},{1,17},{17,1},{2,18},{18,2},{3,19},{19,3},{4,20},{20... | collective-permute-start | bytes 2359304 | tf_op jit(solution)/shard_map/ppermute | solution.py:552
  172.5 12.0 %collective-permute-start.30 = (bf16[768,512]{1,0:T(8,128)(2,1)S(1)}, bf16[768,512]{1,0:T(8,128)(2,1)S(1)}, u32[]{:S(2)}, u32[]{:S(2)}) collective-permute-start(bf16[768,512]{1,0:T(8,128)(2,1)S(1)} %convolution_convert_fusion.4), channel_id=1, source_target_pairs={{0,8},{4,12},{8,0},{12,4},{16,20},{20,16},{24,28},{28,24},{1,9},{5... | collective-permute-start | bytes 2359304 | tf_op jit(solution)/shard_map/ppermute | solution.py:549
  174.6 45.9 %collective-permute-start.39 = (bf16[4,192,256]{2,1,0:T(8,128)(2,1)}, bf16[4,192,256]{2,1,0:T(8,128)(2,1)}, u32[]{:S(2)}, u32[]{:S(2)}) collective-permute-start(bf16[4,192,256]{2,1,0:T(8,128)(2,1)} %fusion.13), channel_id=1, source_target_pairs={{0,1},{1,2},{2,3},{3,0},{4,5},{5,6},{6,7},{7,4},{8,9},{9,10},{10,1... | collective-permute-start | bytes 1179656 | tf_op jit(solution)/shard_map/ppermute | solution.py:555
  184.7 20.0 %collective-permute-start.32 = (bf16[768,512]{1,0:T(8,128)(2,1)S(1)}, bf16[768,512]{1,0:T(8,128)(2,1)S(1)}, u32[]{:S(2)}, u32[]{:S(2)}) collective-permute-start(bf16[768,512]{1,0:T(8,128)(2,1)S(1)} %add_convert_fusion.2), channel_id=1, source_target_pairs={{0,4},{4,0},{8,12},{12,8},{16,24},{20,28},{24,16},{28,20},{1,5},{5... | collective-permute-start | bytes 2359304 | tf_op jit(solution)/shard_map/ppermute | solution.py:546
  185.1 19.7 %collective-permute-start.33 = (bf16[768,512]{1,0:T(8,128)(2,1)S(1)}, bf16[768,512]{1,0:T(8,128)(2,1)S(1)}, u32[]{:S(2)}, u32[]{:S(2)}) collective-permute-start(bf16[768,512]{1,0:T(8,128)(2,1)S(1)} %convolution_convert_fusion.2), channel_id=1, source_target_pairs={{0,8},{4,12},{8,0},{12,4},{16,20},{20,16},{24,28},{28,24},{1,9},{5... | collective-permute-start | bytes 2359304 | tf_op jit(solution)/shard_map/ppermute | solution.py:549
  213.0 20.8 %collective-permute-start.34 = (bf16[2,768,384]{2,1,0:T(8,128)(2,1)}, bf16[2,768,384]{2,1,0:T(8,128)(2,1)}, u32[]{:S(2)}, u32[]{:S(2)}) collective-permute-start(bf16[2,768,384]{2,1,0:T(8,128)(2,1)} %get-tuple-element.173), channel_id=1, source_target_pairs={{0,16},{16,0},{1,17},{17,1},{2,18},{18,2},{3,19},{19,3},{4,20},{20... | collective-permute-start | bytes 3538952 | tf_op jit(solution)/shard_map/ppermute | solution.py:552
  213.0 12.7 %collective-permute-start.26 = (bf16[512,768]{1,0:T(8,128)(2,1)}, bf16[512,768]{1,0:T(8,128)(2,1)}, u32[]{:S(2)}, u32[]{:S(2)}) collective-permute-start(bf16[512,768]{1,0:T(8,128)(2,1)} %get-tuple-element.141), channel_id=1, source_target_pairs={{0,0},{4,16},{8,8},{12,24},{16,4},{20,20},{24,12},{28,28},{1,1},{5... | collective-permute-start | bytes 2359304 | tf_op jit(solution)/shard_map/ppermute | solution.py:543
  222.5 10.1 %collective-permute-start.40 = (bf16[4,192,256]{2,1,0:T(8,128)(2,1)}, bf16[4,192,256]{2,1,0:T(8,128)(2,1)}, u32[]{:S(2)}, u32[]{:S(2)}) collective-permute-start(bf16[4,192,256]{2,1,0:T(8,128)(2,1)} %fusion.14), channel_id=1, source_target_pairs={{0,1},{1,2},{2,3},{3,0},{4,5},{5,6},{6,7},{7,4},{8,9},{9,10},{10,1... | collective-permute-start | bytes 1179656 | tf_op jit(solution)/shard_map/ppermute | solution.py:555
  228.1 21.3 %collective-permute-start.60 = (f32[2,768]{1,0:T(2,128)S(1)}, f32[2,768]{1,0:T(2,128)S(1)}, u32[]{:S(2)}, u32[]{:S(2)}) collective-permute-start(f32[2,768]{1,0:T(2,128)S(1)} %pad_maximum_fusion.1), channel_id=1, source_target_pairs={{0,16},{16,0},{1,17},{17,1},{2,18},{18,2},{3,19},{19,3},{4,20},{20... | collective-permute-start | bytes 18440 | tf_op jit(solution)/shard_map/ppermute | solution.py:558
  235.3 9.9 %collective-permute-start.35 = (bf16[768,384]{1,0:T(8,128)(2,1)S(1)}, bf16[768,384]{1,0:T(8,128)(2,1)S(1)}, u32[]{:S(2)}, u32[]{:S(2)}) collective-permute-start(bf16[768,384]{1,0:T(8,128)(2,1)S(1)} %get-tuple-element.232), channel_id=1, source_target_pairs={{0,8},{4,12},{8,0},{12,4},{16,20},{20,16},{24,28},{28,24},{1,9},{5... | collective-permute-start | bytes 1769480 | tf_op jit(solution)/shard_map/ppermute | solution.py:549
  245.3 20.0 %collective-permute-start.38 = (bf16[512,768]{1,0:T(8,128)(2,1)S(1)}, bf16[512,768]{1,0:T(8,128)(2,1)S(1)}, u32[]{:S(2)}, u32[]{:S(2)}) collective-permute-start(bf16[512,768]{1,0:T(8,128)(2,1)S(1)} %get-tuple-element.179), channel_id=1, source_target_pairs={{0,16},{16,0},{1,17},{17,1},{2,18},{18,2},{3,19},{19,3},{4,20},{20... | collective-permute-start | bytes 2359304 | tf_op jit(solution)/shard_map/ppermute | solution.py:552
  245.3 9.7 %collective-permute-start.46 = (bf16[192,512]{1,0:T(8,128)(2,1)S(1)}, bf16[192,512]{1,0:T(8,128)(2,1)S(1)}, u32[]{:S(2)}, u32[]{:S(2)}) collective-permute-start(bf16[192,512]{1,0:T(8,128)(2,1)S(1)} %get-tuple-element.233), channel_id=1, source_target_pairs={{0,1},{1,2},{2,3},{3,0},{4,5},{5,6},{6,7},{7,4},{8,9},{9,10},{10,1... | collective-permute-start | bytes 589832 | tf_op jit(solution)/shard_map/ppermute | solution.py:555
  245.4 17.1 %collective-permute-start.47 = (bf16[192,512]{1,0:T(8,128)(2,1)S(1)}, bf16[192,512]{1,0:T(8,128)(2,1)S(1)}, u32[]{:S(2)}, u32[]{:S(2)}) collective-permute-start(bf16[192,512]{1,0:T(8,128)(2,1)S(1)} %get-tuple-element.235), channel_id=1, source_target_pairs={{0,2},{1,3},{2,0},{3,1},{4,6},{5,7},{6,4},{7,5},{8,10},{9,11},{10,... | collective-permute-start | bytes 589832 | tf_op jit(solution)/shard_map/ppermute | solution.py:555
  246.4 16.9 %collective-permute-start.48 = (bf16[192,512]{1,0:T(8,128)(2,1)S(1)}, bf16[192,512]{1,0:T(8,128)(2,1)S(1)}, u32[]{:S(2)}, u32[]{:S(2)}) collective-permute-start(bf16[192,512]{1,0:T(8,128)(2,1)S(1)} %get-tuple-element.234), channel_id=1, source_target_pairs={{0,3},{1,0},{2,1},{3,2},{4,7},{5,4},{6,5},{7,6},{8,11},{9,8},{10,9... | collective-permute-start | bytes 589832 | tf_op jit(solution)/shard_map/ppermute | solution.py:555
  249.5 18.5 %collective-permute-start.37 = (bf16[768,384]{1,0:T(8,128)(2,1)S(1)}, bf16[768,384]{1,0:T(8,128)(2,1)S(1)}, u32[]{:S(2)}, u32[]{:S(2)}) collective-permute-start(bf16[768,384]{1,0:T(8,128)(2,1)S(1)} %get-tuple-element.231), channel_id=1, source_target_pairs={{0,8},{4,12},{8,0},{12,4},{16,20},{20,16},{24,28},{28,24},{1,9},{5... | collective-permute-start | bytes 1769480 | tf_op jit(solution)/shard_map/ppermute | solution.py:549
  255.0 12.9 %collective-permute-start.36 = (bf16[768,384]{1,0:T(8,128)(2,1)S(1)}, bf16[768,384]{1,0:T(8,128)(2,1)S(1)}, u32[]{:S(2)}, u32[]{:S(2)}) collective-permute-start(bf16[768,384]{1,0:T(8,128)(2,1)S(1)} %fusion.4), channel_id=1, source_target_pairs={{0,4},{4,0},{8,12},{12,8},{16,24},{20,28},{24,16},{28,20},{1,5},{5... | collective-permute-start | bytes 1769480 | tf_op jit(solution)/shard_map/ppermute | solution.py:546
  262.5 4.6 %collective-permute-start.41 = (bf16[192,256]{1,0:T(8,128)(2,1)S(1)}, bf16[192,256]{1,0:T(8,128)(2,1)S(1)}, u32[]{:S(2)}, u32[]{:S(2)}) collective-permute-start(bf16[192,256]{1,0:T(8,128)(2,1)S(1)} %get-tuple-element.240), channel_id=1, source_target_pairs={{0,8},{4,12},{8,0},{12,4},{16,20},{20,16},{24,28},{28,24},{1,9},{5... | collective-permute-start | bytes 294920 | tf_op jit(solution)/shard_map/ppermute | solution.py:549
  263.3 11.3 %collective-permute-start.50 = (bf16[192,256]{1,0:T(8,128)(2,1)S(1)}, bf16[192,256]{1,0:T(8,128)(2,1)S(1)}, u32[]{:S(2)}, u32[]{:S(2)}) collective-permute-start(bf16[192,256]{1,0:T(8,128)(2,1)S(1)} %get-tuple-element.239), channel_id=1, source_target_pairs={{0,8},{4,12},{8,0},{12,4},{16,20},{20,16},{24,28},{28,24},{1,9},{5... | collective-permute-start | bytes 294920 | tf_op jit(solution)/shard_map/ppermute | solution.py:549
  265.3 28.9 %collective-permute-start.61 = (f32[2,768]{1,0:T(2,128)S(1)}, f32[2,768]{1,0:T(2,128)S(1)}, u32[]{:S(2)}, u32[]{:S(2)}) collective-permute-start(f32[2,768]{1,0:T(2,128)S(1)} %fusion.21), channel_id=1, source_target_pairs={{0,4},{4,0},{8,12},{12,8},{1,5},{5,1},{9,13},{13,9},{2,6},{6,2},{1... | collective-permute-start | bytes 18440 | tf_op jit(solution)/shard_map/ppermute | solution.py:558
  267.2 29.5 %collective-permute-start.62 = (f32[2,768]{1,0:T(2,128)S(1)}, f32[2,768]{1,0:T(2,128)S(1)}, u32[]{:S(2)}, u32[]{:S(2)}) collective-permute-start(f32[2,768]{1,0:T(2,128)S(1)} %fusion.21), channel_id=1, source_target_pairs={{0,8},{4,12},{8,0},{12,4},{1,9},{5,13},{9,1},{13,5},{2,10},{6,14},... | collective-permute-start | bytes 18440 | tf_op jit(solution)/shard_map/ppermute | solution.py:558
  268.0 6.7 %collective-permute-start.49 = (bf16[192,256]{1,0:T(8,128)(2,1)S(1)}, bf16[192,256]{1,0:T(8,128)(2,1)S(1)}, u32[]{:S(2)}, u32[]{:S(2)}) collective-permute-start(bf16[192,256]{1,0:T(8,128)(2,1)S(1)} %fusion.16), channel_id=1, source_target_pairs={{0,4},{4,0},{8,12},{12,8},{16,24},{20,28},{24,16},{28,20},{1,5},{5... | collective-permute-start | bytes 294920 | tf_op jit(solution)/shard_map/ppermute | solution.py:546
  270.9 8.6 %collective-permute-start.43 = (bf16[192,384]{1,0:T(8,128)(2,1)S(1)}, bf16[192,384]{1,0:T(8,128)(2,1)S(1)}, u32[]{:S(2)}, u32[]{:S(2)}) collective-permute-start(bf16[192,384]{1,0:T(8,128)(2,1)S(1)} %get-tuple-element.236), channel_id=1, source_target_pairs={{0,1},{1,2},{2,3},{3,0},{4,5},{5,6},{6,7},{7,4},{8,9},{9,10},{10,1... | collective-permute-start | bytes 442376 | tf_op jit(solution)/shard_map/ppermute | solution.py:555
  274.6 9.6 %collective-permute-start.44 = (bf16[192,384]{1,0:T(8,128)(2,1)S(1)}, bf16[192,384]{1,0:T(8,128)(2,1)S(1)}, u32[]{:S(2)}, u32[]{:S(2)}) collective-permute-start(bf16[192,384]{1,0:T(8,128)(2,1)S(1)} %get-tuple-element.238), channel_id=1, source_target_pairs={{0,2},{1,3},{2,0},{3,1},{4,6},{5,7},{6,4},{7,5},{8,10},{9,11},{10,... | collective-permute-start | bytes 442376 | tf_op jit(solution)/shard_map/ppermute | solution.py:555
  274.7 9.6 %collective-permute-start.45 = (bf16[192,384]{1,0:T(8,128)(2,1)S(1)}, bf16[192,384]{1,0:T(8,128)(2,1)S(1)}, u32[]{:S(2)}, u32[]{:S(2)}) collective-permute-start(bf16[192,384]{1,0:T(8,128)(2,1)S(1)} %get-tuple-element.237), channel_id=1, source_target_pairs={{0,3},{1,0},{2,1},{3,2},{4,7},{5,4},{6,5},{7,6},{8,11},{9,8},{10,9... | collective-permute-start | bytes 442376 | tf_op jit(solution)/shard_map/ppermute | solution.py:555
  279.6 17.0 %collective-permute-start.63 = (f32[2,768]{1,0:T(2,128)S(1)}, f32[2,768]{1,0:T(2,128)S(1)}, u32[]{:S(2)}, u32[]{:S(2)}) collective-permute-start(f32[2,768]{1,0:T(2,128)S(1)} %fusion.21), channel_id=1, source_target_pairs={{0,12},{4,8},{8,4},{12,0},{1,13},{5,9},{9,5},{13,1},{2,14},{6,10},... | collective-permute-start | bytes 18440 | tf_op jit(solution)/shard_map/ppermute | solution.py:558
  284.3 4.6 %collective-permute-start.53 = (bf16[192,256]{1,0:T(8,128)(2,1)}, bf16[192,256]{1,0:T(8,128)(2,1)}, u32[]{:S(2)}, u32[]{:S(2)}) collective-permute-start(bf16[192,256]{1,0:T(8,128)(2,1)} %get-tuple-element.226.d0_ref), channel_id=1, source_target_pairs={{0,16},{16,0},{1,17},{17,1},{2,18},{18,2},{3,19},{19,3},{4,20},{20... | collective-permute-start | bytes 294920 | tf_op jit(solution)/shard_map/ppermute | solution.py:552
  286.1 4.3 %collective-permute-start.51 = (bf16[192,384]{1,0:T(8,128)(2,1)}, bf16[192,384]{1,0:T(8,128)(2,1)S(1)}, u32[]{:S(2)}, u32[]{:S(2)}) collective-permute-start(bf16[192,384]{1,0:T(8,128)(2,1)} %get-tuple-element.230.a0_ref), channel_id=1, source_target_pairs={{0,16},{16,0},{1,17},{17,1},{2,18},{18,2},{3,19},{19,3},{4,20},{20... | collective-permute-start | bytes 442376 | tf_op jit(solution)/shard_map/ppermute | solution.py:552
  293.0 9.1 %collective-permute-start.54 = (f32[8,128]{1,0:T(8,128)S(1)}, f32[8,128]{1,0:T(8,128)S(1)}, u32[]{:S(2)}, u32[]{:S(2)}) collective-permute-start(f32[8,128]{1,0:T(8,128)S(1)} %broadcast_in_dim.24), channel_id=1, source_target_pairs={{0,4},{4,0},{8,12},{12,8},{1,5},{5,1},{9,13},{13,9},{2,6},{6,2},{1... | collective-permute-start | bytes 12296 | tf_op jit(solution)/shard_map/ppermute | solution.py:558
  293.4 9.3 %collective-permute-start.55 = (f32[8,128]{1,0:T(8,128)S(1)}, f32[8,128]{1,0:T(8,128)S(1)}, u32[]{:S(2)}, u32[]{:S(2)}) collective-permute-start(f32[8,128]{1,0:T(8,128)S(1)} %broadcast_in_dim.24), channel_id=1, source_target_pairs={{0,8},{4,12},{8,0},{12,4},{1,9},{5,13},{9,1},{13,5},{2,10},{6,14},... | collective-permute-start | bytes 12296 | tf_op jit(solution)/shard_map/ppermute | solution.py:558
  294.2 15.9 %collective-permute-start.56 = (f32[8,128]{1,0:T(8,128)S(1)}, f32[8,128]{1,0:T(8,128)S(1)}, u32[]{:S(2)}, u32[]{:S(2)}) collective-permute-start(f32[8,128]{1,0:T(8,128)S(1)} %broadcast_in_dim.24), channel_id=1, source_target_pairs={{0,12},{4,8},{8,4},{12,0},{1,13},{5,9},{9,5},{13,1},{2,14},{6,10},... | collective-permute-start | bytes 12296 | tf_op jit(solution)/shard_map/ppermute | solution.py:558
  296.6 14.6 %collective-permute-start.64 = (f32[2,768]{1,0:T(2,128)S(1)}, f32[2,768]{1,0:T(2,128)S(1)}, u32[]{:S(2)}, u32[]{:S(2)}) collective-permute-start(f32[2,768]{1,0:T(2,128)S(1)} %add_add_fusion.1), channel_id=1, source_target_pairs={{0,1},{1,0},{2,3},{3,2},{4,5},{5,4},{6,7},{7,6},{8,9},{9,8},{10,11... | collective-permute-start | bytes 18440 | tf_op jit(solution)/shard_map/ppermute | solution.py:558
  300.2 13.8 %collective-permute-start.65 = (f32[2,768]{1,0:T(2,128)S(1)}, f32[2,768]{1,0:T(2,128)S(1)}, u32[]{:S(2)}, u32[]{:S(2)}) collective-permute-start(f32[2,768]{1,0:T(2,128)S(1)} %add_add_fusion.1), channel_id=1, source_target_pairs={{0,2},{1,3},{2,0},{3,1},{4,6},{5,7},{6,4},{7,5},{8,10},{9,11},{10,... | collective-permute-start | bytes 18440 | tf_op jit(solution)/shard_map/ppermute | solution.py:558
  302.1 12.5 %collective-permute-start.66 = (f32[2,768]{1,0:T(2,128)S(1)}, f32[2,768]{1,0:T(2,128)S(1)}, u32[]{:S(2)}, u32[]{:S(2)}) collective-permute-start(f32[2,768]{1,0:T(2,128)S(1)} %add_add_fusion.1), channel_id=1, source_target_pairs={{0,3},{1,2},{2,1},{3,0},{4,7},{5,6},{6,5},{7,4},{8,11},{9,10},{10,... | collective-permute-start | bytes 18440 | tf_op jit(solution)/shard_map/ppermute | solution.py:558
  302.7 38.3 %collective-permute-start.42 = (bf16[512,768]{1,0:T(8,128)(2,1)}, bf16[512,768]{1,0:T(8,128)(2,1)}, u32[]{:S(2)}, u32[]{:S(2)}) collective-permute-start(bf16[512,768]{1,0:T(8,128)(2,1)} %add_convert_fusion.1), channel_id=1, source_target_pairs={{0,0},{4,16},{8,8},{12,24},{16,4},{20,20},{24,12},{28,28},{1,1},{5... | collective-permute-start | bytes 2359304 | tf_op jit(solution)/shard_map/ppermute | solution.py:543
  310.1 5.1 %collective-permute-start.57 = (f32[8,128]{1,0:T(8,128)S(1)}, f32[8,128]{1,0:T(8,128)S(1)}, u32[]{:S(2)}, u32[]{:S(2)}) collective-permute-start(f32[8,128]{1,0:T(8,128)S(1)} %add_add_fusion.3), channel_id=1, source_target_pairs={{0,1},{1,0},{2,3},{3,2},{4,5},{5,4},{6,7},{7,6},{8,9},{9,8},{10,11... | collective-permute-start | bytes 12296 | tf_op jit(solution)/shard_map/ppermute | solution.py:558
  311.3 4.5 %collective-permute-start.58 = (f32[8,128]{1,0:T(8,128)S(1)}, f32[8,128]{1,0:T(8,128)S(1)}, u32[]{:S(2)}, u32[]{:S(2)}) collective-permute-start(f32[8,128]{1,0:T(8,128)S(1)} %add_add_fusion.3), channel_id=1, source_target_pairs={{0,2},{1,3},{2,0},{3,1},{4,6},{5,7},{6,4},{7,5},{8,10},{9,11},{10,... | collective-permute-start | bytes 12296 | tf_op jit(solution)/shard_map/ppermute | solution.py:558
  314.0 5.4 %collective-permute-start.59 = (f32[8,128]{1,0:T(8,128)S(1)}, f32[8,128]{1,0:T(8,128)S(1)}, u32[]{:S(2)}, u32[]{:S(2)}) collective-permute-start(f32[8,128]{1,0:T(8,128)S(1)} %add_add_fusion.3), channel_id=1, source_target_pairs={{0,3},{1,2},{2,1},{3,0},{4,7},{5,6},{6,5},{7,4},{8,11},{9,10},{10,... | collective-permute-start | bytes 12296 | tf_op jit(solution)/shard_map/ppermute | solution.py:558
  (93 other events, 921.8 us)
